TPU v7x, 32 devices: a whole 2x2x4 slice. The times are simulated.
32 devices in a mesh: stream: 2 (over core), span: 4 (over y, x), height: 4 (over z).
Axes of the slice: x: 2, y: 2, z: 4, core: 2. Of those that a mesh axis runs over, the one named last changes fastest.
Arguments:
- source: bfloat16 [32, 64, 128, 256], P('stream', 'span', 'height'), may hold values from -0.59765625 to 0.59765625
- inflow: bfloat16 [32, 64, 128, 256], P('stream', 'span', 'height'), may hold values from -6 to 6
- recovery: float32 [32, 64, 128], P('stream', 'span', 'height'), may hold values from 0 to 1
- obs_rows: int32 [1024], P(('stream', 'span', 'height')), may hold values from 0 to 8191, as said below
- obs: float32 [1024], P(('stream', 'span', 'height')), may hold values from -6 to 6
- observation_weight: float32 [1024], P(('stream', 'span', 'height')), may hold values from 0.1 to 1
- member_order: int32 [256], replicated, may hold values from 0 to 255, each once
Outputs:
- analysis: bfloat16 [32, 64, 128, 256], P('stream', 'span', 'height')
Inputs may be any that keep to these rules, and one draw needn't show every extreme that they name: `obs_rows`: each entry indexes the rows of the device that holds it. `member_order`: a permutation.
All inputs are finite; a program needn't handle non-finite values.
Results may differ from a plain program's by a relative error of at most 0.0063.
Values may be sent and summed in bfloat16 or wider, within the bound.
No kernel may reach another device: no remote copies, remote signals or barrier semaphores. Data moves between devices by JAX's collectives and lax.ppermute only.
A program may use at most 320 MiB of HBM per device.

v0:
```python
import jax
import jax.numpy as jnp
from jax import lax
from jax.sharding import PartitionSpec as P

vertical_mix = 0.25


def with_halo(block, sides, width):
    for axis, dim in sides:
        count = lax.axis_size(axis)
        forward = [(i, i + 1) for i in range(count - 1)]
        backward = [(target, source) for source, target in forward]
        low = lax.ppermute(
            lax.slice_in_dim(block, block.shape[dim] - width, None, axis=dim), axis, forward
        )
        high = lax.ppermute(lax.slice_in_dim(block, 0, width, axis=dim), axis, backward)
        block = jnp.concatenate([low, block, high], axis=dim)
    return block


def shifted(value, axis, steps):
    count = lax.axis_size(axis)
    initial, last = (max(0, -steps), min(count, count - steps))
    return lax.ppermute(value, axis, [(source, source + steps) for source in range(initial, last)])


def lower_cholesky(matrix):
    return jnp.linalg.cholesky(matrix)


def lower_inverse(lower):
    identity = jnp.eye(lower.shape[0], dtype=jnp.float32)
    return lax.linalg.triangular_solve(lower, identity, left_side=True, lower=True)


def factor_leaf(gram_part, projection, diagonal_add):
    highest = lax.Precision.HIGHEST
    identity = jnp.eye(gram_part.shape[0], dtype=jnp.float32)
    lower_factor = lower_cholesky(gram_part + diagonal_add * identity)
    inverse_lower = lower_inverse(lower_factor)
    coefficients = jnp.dot(inverse_lower, projection, precision=highest)
    return (lower_factor.T, coefficients, inverse_lower)


def shards(source, inflow, recovery, obs_rows, obs, observation_weight, member_order):
    planes, span_cells, height_cells, members = source.shape
    highest = lax.Precision.HIGHEST
    padded = with_halo(source, (("height", 2),), 1)
    centre = source.astype(jnp.float32)
    smoothed = centre + vertical_mix * (
        padded[:, :, 2:].astype(jnp.float32) + padded[:, :, :-2].astype(jnp.float32) - 2.0 * centre
    )

    def march_plane(carried, inputs):
        plane_rate, plane_term = inputs
        advanced = plane_rate[..., None] * carried + plane_term
        return (advanced, advanced)

    zero_plane = jnp.zeros((span_cells, height_cells, members), jnp.float32)
    local_end, local_deficit = lax.scan(march_plane, zero_plane, (recovery, smoothed))
    through = jnp.cumprod(recovery, axis=0)
    total_rate = through[-1]

    def relay_turn(turn_index, incoming):
        return shifted(total_rate[..., None] * incoming + local_end, "stream", 1)

    incoming = lax.fori_loop(0, lax.axis_size("stream") - 1, relay_turn, zero_plane)
    velocity_deficit = local_deficit + through[..., None] * incoming[None]
    prior_ensemble = inflow.astype(jnp.float32) - velocity_deficit
    prior_mean = jnp.mean(prior_ensemble, axis=-1)
    member_anomaly = (prior_ensemble - prior_mean[..., None]).astype(jnp.bfloat16)
    flat_rows = member_anomaly.reshape(-1, members)
    flattened_mean = prior_mean.reshape(-1)
    row_count = flat_rows.shape[0]
    row_select = obs_rows[:, None] == jnp.arange(row_count, dtype=jnp.int32)[None, :]
    picked_rows = jnp.dot(
        row_select.astype(jnp.bfloat16), flat_rows, preferred_element_type=jnp.float32
    )
    picked = picked_rows * observation_weight[:, None]
    one_hot = (member_order[None, :] == jnp.arange(members, dtype=jnp.int32)[:, None]).astype(
        jnp.float32
    )
    observed = jnp.dot(picked, one_hot, precision=highest)
    picked_mean = jnp.dot(row_select.astype(jnp.float32), flattened_mean, precision=highest)
    observation_misfit = observation_weight * (obs - picked_mean)
    gram_local = jnp.dot(observed.T, observed, precision=highest)
    projection = jnp.dot(observed.T, observation_misfit, precision=highest)
    gram_all, projection_all = lax.psum((gram_local, projection), ("stream", "span", "height"))
    upper_factor, coefficients, inverse_lower = factor_leaf(gram_all, projection_all, members - 1.0)
    inverse = inverse_lower.T
    mean_weights = jnp.dot(inverse, coefficients, precision=highest)
    square_root_mapping = jnp.sqrt(members - 1.0) * inverse + mean_weights[:, None]
    weights = jnp.dot(
        jnp.dot(one_hot, square_root_mapping, precision=highest), one_hot.T, precision=highest
    ).astype(jnp.bfloat16)
    update = jnp.dot(flat_rows, weights, preferred_element_type=jnp.float32)
    analysis = (flattened_mean[:, None] + update).astype(jnp.bfloat16)
    return analysis.reshape(planes, span_cells, height_cells, members)


def solution(mesh):
    placed = (
        P("stream", "span", "height", None),
        P("stream", "span", "height", None),
        P("stream", "span", "height"),
        P(("stream", "span", "height")),
        P(("stream", "span", "height")),
        P(("stream", "span", "height")),
        P(),
    )
    return jax.shard_map(
        shards,
        mesh=mesh,
        in_specs=placed,
        out_specs=P("stream", "span", "height", None),
        check_vma=False,
    )
```

profile of v0, /device:TPU:0, one launch (start us, length us, event | category | flops | bytes accessed | tf_op | source)
XLA Modules:
  0.0 300.0 jit_solution(9886303384453420963)
XLA Ops:
  6.5 2.1 fusion.36
  8.6 1.3 collective-permute-start
  9.9 5.6 %collective-permute-start.1 = (bf16[16,16,1,256]{3,2,1,0:T(2,128)(2,1)S(1)}, bf16[16,16,1,256]{3,2,1,0:T(2,128)(2,1)S(1)}, u32[]{:S(2)}, u32[]{:S(2)}) collective-permute-start(bf16[16,16,1,256]{3,2,1,0:T(2,128)(2,1)S(1)} %get-tuple-element.100), channel_id=1, source_target_pairs={{0,1},{1,2},{2,3},{4,5},{5,6},{6,7},{8,9},{9,10},{10,11},{12,13},{... | collective-permute-start | bytes 393224 | tf_op jit(solution)/shard_map/ppermute | solution.py:14
  15.5 0.9 fusion.37
  16.5 3.4 %collective-permute-done = bf16[16,16,1,256]{3,2,1,0:T(2,128)(2,1)S(1)} collective-permute-done((bf16[16,16,1,256]{3,2,1,0:T(2,128)(2,1)S(1)}, bf16[16,16,1,256]{3,2,1,0:T(2,128)(2,1)S(1)}, u32[]{:S(2)}, u32[]{:S(2)}) %collective-permute-start) | collective-permute-done | bytes 131104 | tf_op jit(solution)/shard_map/ppermute | solution.py:17
  19.9 1.2 collective-permute-done.1
  21.0 12.0 %convert_add_fusion = f32[16,16,32,256]{3,2,1,0:T(8,128)} fusion(bf16[16,16,32,256]{3,2,1,0:T(8,128)(2,1)} %param.9, bf16[16,16,1,256]{3,2,1,0:T(2,128)(2,1)S(1)} %collective-permute-done.1, bf16[16,16,1,256]{3,2,1,0:T(2,128)(2,1)S(1)} %collective-permute-done), kind=kLoop, calls=%fused_computation.7 | loop fusion | flops 29360128 | bytes 12845056 | tf_op jit(solution)/shard_map/add | solution.py:51
  33.0 44.0 %while.19 = (s32[]{:T(128)}, f32[16,32,256]{2,1,0:T(8,128)S(1)}, f32[16,16,32,256]{3,2,1,0:T(8,128)}, f32[16,16,32]{2,1,0:T(8,128)}, f32[16,16,32,256]{3,2,1,0:T(8,128)}, /*index=5*/s32[]{:T(128)}, s32[]{:T(128)}) while((s32[]{:T(128)}, f32[16,32,256]{2,1,0:T(8,128)S(1)}, f32[16,16,32,256]{3,2,1,0:T(8,128)}, ...), condition=%wide.region_1.2_spmd.clone, body=%wide.region_0.1_spmd.clone.sunk | while | flops 393219 | bytes 2103899 | solution.py:61
  33.7 2.1 bitcast_dynamic-update-slice_fusion.5
  36.5 2.1 bitcast_dynamic-update-slice_fusion.5
  38.6 0.7 dynamic-slice_bitcast_fusion.2
  39.3 2.0 bitcast_dynamic-update-slice_fusion.5
  41.3 0.7 dynamic-slice_bitcast_fusion.2
  42.0 2.0 bitcast_dynamic-update-slice_fusion.5
  44.8 2.1 bitcast_dynamic-update-slice_fusion.5
  47.5 2.1 bitcast_dynamic-update-slice_fusion.5
  49.6 0.7 dynamic-slice_bitcast_fusion.2
  50.3 2.0 bitcast_dynamic-update-slice_fusion.5
  52.3 0.7 dynamic-slice_bitcast_fusion.2
  53.0 2.0 bitcast_dynamic-update-slice_fusion.5
  55.1 0.7 dynamic-slice_bitcast_fusion.2
  55.8 2.1 bitcast_dynamic-update-slice_fusion.5
  58.5 2.1 bitcast_dynamic-update-slice_fusion.5
  61.3 2.0 bitcast_dynamic-update-slice_fusion.5
  64.0 2.0 bitcast_dynamic-update-slice_fusion.5
  66.8 2.1 bitcast_dynamic-update-slice_fusion.5
  69.5 2.1 bitcast_dynamic-update-slice_fusion.5
  72.3 2.0 bitcast_dynamic-update-slice_fusion.5
  75.0 2.0 bitcast_dynamic-update-slice_fusion.5
  77.2 1.3 collective-permute-start.2
  78.6 1.4 collective-permute-done.2
  80.0 6.0 %fusion.3 = f32[16,16,32]{2,1,0:T(8,128)S(1)} fusion(f32[16,16,32,256]{3,2,1,0:T(8,128)} %get-tuple-element.45, bf16[16,16,32,256]{3,2,1,0:T(8,128)(2,1)} %param.10, f32[16,32,256]{2,1,0:T(8,128)S(1)} %collective-permute-done.2, f32[16,16,32]{2,1,0:T(8,128)S(1)} %fusion.37), kind=kLoop, calls=%fused_computation.14 | loop fusion | flops 10477568 | bytes 13172736 | tf_op jit(solution)/shard_map/reduce_sum | solution.py:71
  86.3 6.2 %subtract_convert_fusion = bf16[16,16,32,256]{3,2,1,0:T(8,128)(2,1)S(1)} fusion(f32[16,16,32,256]{3,2,1,0:T(8,128)} %get-tuple-element.45, bf16[16,16,32,256]{3,2,1,0:T(8,128)(2,1)} %param.10, f32[16,16,32]{2,1,0:T(8,128)S(1)} %broadcast_multiply_fusion, f32[16,32,256]{2,1,0:T(8,128)S(1)} %collective-permute-done.2, f32[16,16,32]{2,1,0:T(8,128)S(1)} %fusion.37), kind=kLoop, calls=%fused_computation.12 | loop fusion | flops 12582912 | bytes 17367040 | tf_op jit(solution)/shard_map/convert_element_type | solution.py:72
  92.5 1.9 copy-done
  94.4 0.8 convolution_multiply_fusion
  95.4 1.1 fusion.38
  97.4 41.8 %psum.15 = f32[256]{0:T(256)S(1)} all-reduce(f32[256]{0:T(256)S(1)} %bitcast.86), channel_id=1, replica_groups=mesh['stream'=2,'span'=4,'height'=4] {'stream','span','height'}, use_global_device_ids=true, to_apply=%region_9.10 | all-reduce | flops 256 | bytes 2048 | tf_op jit(solution)/shard_map/psum | solution.py:89
  139.2 84.9 %all-reduce.3.cloned.1.call-done = f32[256,256]{0,1:T(8,128)} async-done(((f32[256,256]{0,1:T(8,128)}), f32[256,256]{0,1:T(8,128)}) %all-reduce.3.cloned.1.call-update) | async-done | bytes 262160 | tf_op jit(solution)/shard_map/psum | solution.py:89
  224.1 1.0 select_add_fusion
  225.2 1.0 fusion.14
  226.2 11.7 %cholesky.49 = f32[128,128]{1,0:T(8,128)S(1)} custom-call(f32[128,128]{1,0:T(8,128)S(1)} %cholesky.115), custom_call_target="Cholesky" | custom-call | tf_op jit(solution)/shard_map/jit(cholesky)/cholesky | solution.py:29
  238.0 9.8 %custom-call.14 = f32[1,128,128]{1,2,0:T(8,128)S(1)} custom-call(f32[1,128,128]{2,1,0:T(8,128)S(1)} %get-tuple-element.102), custom_call_target="InvertDiagBlocksLowerTriangular" | custom-call | tf_op jit(solution)/shard_map/jit(cholesky)/cholesky | solution.py:29
  248.3 11.7 %cholesky.103 = f32[128,128]{1,0:T(8,128)S(1)} custom-call(f32[128,128]{1,0:T(8,128)S(1)} %convolution_subtract_fusion.1), custom_call_target="Cholesky" | custom-call | tf_op jit(solution)/shard_map/jit(cholesky)/cholesky | solution.py:29
  262.4 4.2 %while.18 = (s32[]{:T(128)}, f32[256,256]{0,1:T(8,128)S(1)}, s32[2,2]{1,0:T(2,128)S(1)}, f32[2,128,128]{2,1,0:T(8,128)S(1)}, s32[]{:T(128)}) while((s32[]{:T(128)}, f32[256,256]{0,1:T(8,128)S(1)}, s32[2,2]{1,0:T(2,128)S(1)}, f32[2,128,128]{2,1,0:T(8,128)S(1)}, s32[]{:T(128)}) %tuple.48), condition=%wide.while_cond, body=%wide.while_body.sunk | while | flops 2 | bytes 393321 | solution.py:34
  263.0 1.4 dynamic-slice.7
  265.1 1.4 dynamic-slice.7
  266.6 19.9 %custom-call.15 = f32[2,128,128]{1,2,0:T(8,128)S(1)} custom-call(f32[2,128,128]{2,1,0:T(8,128)S(1)} %get-tuple-element.54), custom_call_target="InvertDiagBlocksLowerTriangular" | custom-call | tf_op jit(solution)/shard_map/triangular_solve | solution.py:34
  288.8 4.4 %fusion = bf16[8192,256]{1,0:T(8,128)(2,1)} fusion(bf16[8192,256]{1,0:T(8,128)(2,1)} %bitcast.83, bf16[256,256]{1,0:T(8,128)(2,1)S(1)} %convolution_convert_fusion, f32[8192]{0:T(1024)S(1)} %div.18), kind=kOutput, calls=%fused_computation.9 | convolution fusion | flops 1077936128 | bytes 8552448 | tf_op jit(solution)/shard_map/dot_general | solution.py:97
  (65 shorter events, 14.5 us)
Async XLA Ops:
  6.5 217.6 %all-reduce.3.cloned.1.call-start = ((), (), s32[]{:S(2)}) async-start(), calls=%async_computation | async-start | bytes 524288 | tf_op jit(solution)/shard_map/psum | solution.py:89
  8.6 11.2 %collective-permute-start = (bf16[16,16,1,256]{3,2,1,0:T(2,128)(2,1)S(1)}, bf16[16,16,1,256]{3,2,1,0:T(2,128)(2,1)S(1)}, u32[]{:S(2)}, u32[]{:S(2)}) collective-permute-start(bf16[16,16,1,256]{3,2,1,0:T(2,128)(2,1)S(1)} %get-tuple-element.99), channel_id=1, source_target_pairs={{1,0},{2,1},{3,2},{5,4},{6,5},{7,6},{9,8},{10,9},{11,10},{13,12},{... | collective-permute-start | bytes 393224 | tf_op jit(solution)/shard_map/ppermute | solution.py:17
  9.9 11.1 %collective-permute-start.1 = (bf16[16,16,1,256]{3,2,1,0:T(2,128)(2,1)S(1)}, bf16[16,16,1,256]{3,2,1,0:T(2,128)(2,1)S(1)}, u32[]{:S(2)}, u32[]{:S(2)}) collective-permute-start(bf16[16,16,1,256]{3,2,1,0:T(2,128)(2,1)S(1)} %get-tuple-element.100), channel_id=1, source_target_pairs={{0,1},{1,2},{2,3},{4,5},{5,6},{6,7},{8,9},{9,10},{10,11},{12,13},{... | collective-permute-start | bytes 393224 | tf_op jit(solution)/shard_map/ppermute | solution.py:14
  77.2 2.8 collective-permute-start.2
  86.2 8.1 %copy-start.2 = (s32[32]{0:T(128)S(1)}, s32[32]{0:T(128)}, u32[]{:S(2)}) copy-start(s32[32]{0:T(128)} %param.12) | copy-start | bytes 388
  86.2 8.1 %copy-start.3 = (f32[32]{0:T(128)S(1)}, f32[32]{0:T(128)}, u32[]{:S(2)}) copy-start(f32[32]{0:T(128)} %param.14) | copy-start | bytes 388
  86.3 9.0 %copy-start.1 = (s32[256]{0:T(256)S(1)}, s32[256]{0:T(256)}, u32[]{:S(2)}) copy-start(s32[256]{0:T(256)} %param.15) | copy-start | bytes 3076
  86.3 10.3 %copy-start.4 = (f32[32]{0:T(128)S(1)}, f32[32]{0:T(128)}, u32[]{:S(2)}) copy-start(f32[32]{0:T(128)} %param.13) | copy-start | bytes 388
  92.4 1.9 copy-start
Sparse Core Ops, SparseCore 0:
  96.7 127.3 all-reduce.2
where the time goes:
time: 302 us; the launch traced here: 300 us
  other arithmetic  114 us (38%)
  waiting for transfers between devices  90.9 us (30%)
  blocking collectives  41.8 us (14%)
  local copies, waits for them, and re-layouts  20 us (7%)
  between operations  15 us (5%)
  matrix products  10 us (3%)
  starting transfers between devices  8.19 us (3%)
    psum x1, waiting for transfers between devices, shards(): lax.psum((gram_local, projection), ('stream', 'span', 'height'))  84.9 us
    psum x1, blocking collectives, shards(): lax.psum((gram_local, projection), ('stream', 'span', 'height'))  41.8 us
    another operation x6, other arithmetic, lower_cholesky(): return jnp.linalg.cholesky(matrix)  34 us
    dynamic_update_slice x16, other arithmetic, shards(): lax.scan(march_plane, zero_plane, (recovery, smoothed))  32.8 us
    another operation x3, other arithmetic, lower_inverse(): lax.linalg.triangular_solve(lower, identity, left_side=True, lower=True)  19.9 us
    add x1, other arithmetic, shards(): centre + vertical_mix * (padded[:, :, 2:].astype(jnp.float32) + padded[:,...  12 us
    mul x16, local copies, waits for them, and re-layouts, march_plane(): advanced = plane_rate[..., None] * carried + plane_term  11.2 us
    convert_element_type x1, other arithmetic, shards(): (prior_ensemble - prior_mean[..., None]).astype(jnp.bfloat16)  6.16 us
  transfers between devices with their start and end apart: 4, of which 4 were waited for; matrix products, arithmetic and copies ran while one was open for 1% of the time, Pallas kernels for 0%

commit v1 on v0

v1 whole, which is shorter than its diff:
```python
import functools

import jax
import jax.numpy as jnp
from jax import lax
from jax.experimental import pallas as pl
from jax.experimental.pallas import tpu as pltpu
from jax.sharding import PartitionSpec as P

vertical_mix = 0.25
MIB = 1024 * 1024
NT = (((1,), (1,)), ((), ()))
NN = (((1,), (0,)), ((), ()))
EXTRA = 8


def dot(a, b, dims=NN):
    return lax.dot_general(a, b, dims, preferred_element_type=jnp.float32)


def params(mib):
    return pltpu.CompilerParams(vmem_limit_bytes=mib * MIB)


def cost(flops, nbytes):
    return pl.CostEstimate(flops=flops, bytes_accessed=nbytes, transcendentals=0)


def march_kernel(source_ref, inflow_ref, rate_ref, *refs):
    forecast_ref, end_ref = refs[-2:]
    planes, cells, height, members = source_ref.shape
    row = lax.broadcasted_iota(jnp.int32, (height, members), 0)
    inner_low = jnp.where(row == 0, 0.0, vertical_mix)
    inner_high = jnp.where(row == height - 1, 0.0, vertical_mix)
    for a in range(cells):
        rates = rate_ref[a]
        deficit = None
        for p in range(planes):
            x = source_ref[p, a].astype(jnp.float32)
            term = (1.0 - 2.0 * vertical_mix) * x
            term = term + inner_low * pltpu.roll(x, 1, 0)
            term = term + inner_high * pltpu.roll(x, height - 1, 0)
            deficit = term if p == 0 else rates[:, p : p + 1] * deficit + term
            forecast_ref[p, a] = inflow_ref[p, a].astype(jnp.float32) - deficit
        end_ref[a] = deficit


def march(source, inflow, rates, part, parts, held=None):
    planes, span, height, members = source.shape
    step = 2 if span % (2 * parts) == 0 else 1
    count = span // parts // step
    first = part * count
    block = pl.BlockSpec((planes, step, height, members), lambda i: (0, i + first, 0, 0))
    edge = pl.BlockSpec((step, height, members), lambda i: (i + first, 0, 0))
    in_specs = [block, block, pl.BlockSpec((step, height, planes), lambda i: (i + first, 0, 0))]
    args = [source, inflow, rates]
    alias = {}
    if held is not None:
        in_specs += [pl.BlockSpec(memory_space=pl.ANY)] * 2
        args += list(held)
        alias = {3: 0, 4: 1}
    size = source.size // parts
    return pl.pallas_call(
        march_kernel,
        grid=(count,),
        in_specs=in_specs,
        out_specs=[block, edge],
        out_shape=[
            jax.ShapeDtypeStruct(source.shape, jnp.float32),
            jax.ShapeDtypeStruct((span, height, members), jnp.float32),
        ],
        input_output_aliases=alias,
        compiler_params=params(24),
        cost_estimate=cost(10 * size, 8 * size),
    )(*args)


def edge_kernel(parity_ref, first_ref, second_ref, low_rate_ref, high_rate_ref, edge_ref, last_ref):
    planes = first_ref.shape[0]
    even = parity_ref[0] == 0
    low, high = None, None
    for p in range(planes):
        one = vertical_mix * first_ref[p].astype(jnp.float32)
        two = vertical_mix * second_ref[p].astype(jnp.float32)
        low_term = jnp.where(even, two, one)
        high_term = jnp.where(even, one, two)
        low = low_term if p == 0 else low_rate_ref[:, p : p + 1] * low + low_term
        high = high_term if p == 0 else high_rate_ref[:, p : p + 1] * high + high_term
        edge_ref[0, p] = low
        edge_ref[1, p] = high
    last_ref[0] = low
    last_ref[1] = high


def edge_march(parity, first, second, low_rate, high_rate):
    planes, span, members = first.shape
    vmem = pl.BlockSpec(memory_space=pltpu.VMEM)
    return pl.pallas_call(
        edge_kernel,
        in_specs=[pl.BlockSpec(memory_space=pltpu.SMEM)] + [vmem] * 4,
        out_specs=[vmem, vmem],
        out_shape=[
            jax.ShapeDtypeStruct((2, planes, span, members), jnp.float32),
            jax.ShapeDtypeStruct((2, span, members), jnp.float32),
        ],
        compiler_params=params(8),
        cost_estimate=cost(4 * first.size, 8 * first.size),
    )(parity, first, second, low_rate, high_rate)


def observe_kernel(
    rows_ref, rows_column_ref, obs_ref, weight_ref, rate_ref, incoming_ref, edge_ref, last_ref,
    forecast_ref, out_ref, tiles, prior, arriving, halo, through, through_rows, sem,
):
    planes, span, height = rate_ref.shape
    members = out_ref.shape[1]
    count = prior.shape[0]

    def place(k):
        r = rows_ref[k]
        return r // (span * height), r // height % span, r % height

    def fetch(k):
        p, a, b = place(k)
        start = pl.multiple_of(b // 8 * 8, 8)
        return pltpu.make_async_copy(forecast_ref.at[p, a, pl.ds(start, 8), :], tiles.at[k], sem.at[k])

    for k in range(count):
        fetch(k).start()
    product = None
    for p in range(planes):
        product = rate_ref[p] if p == 0 else product * rate_ref[p]
        through[p] = product
    for k in range(count):
        p, a, b = place(k)
        side = jnp.where(b == height - 1, 1, 0)
        at_edge = jnp.where((b == 0) | (b == height - 1), 1.0, 0.0)
        arriving[pl.ds(k, 1), :] = (
            incoming_ref[a, pl.ds(b, 1), :] + at_edge * last_ref[side, pl.ds(a, 1), :]
        )
        halo[pl.ds(k, 1), :] = at_edge * edge_ref[side, p, pl.ds(a, 1), :]
        through_rows[pl.ds(k, 1), :] = through[p, pl.ds(a, 1), :]
    for k in range(count):
        fetch(k).wait()
        _, _, b = place(k)
        prior[pl.ds(k, 1), :] = tiles[k, pl.ds(b % 8, 1), :]
    cell = rows_column_ref[...] % height
    lane = lax.broadcasted_iota(jnp.int32, (count, height), 1)
    share = jnp.sum(jnp.where(lane == cell, through_rows[...], 0.0), axis=1, keepdims=True)
    forecast = prior[...] - halo[...] - share * arriving[...]
    mean = jnp.sum(forecast, axis=1, keepdims=True) * (1.0 / members)
    anomaly = (forecast - mean).astype(jnp.bfloat16).astype(jnp.float32)
    weight = weight_ref[...]
    observed = weight * anomaly
    misfit = weight * (obs_ref[...] - mean)
    projection = jnp.sum(observed * misfit, axis=0, keepdims=True)
    one = projection.astype(jnp.bfloat16).astype(jnp.float32)
    two = (projection - one).astype(jnp.bfloat16).astype(jnp.float32)
    three = projection - one - two
    row = lax.broadcasted_iota(jnp.int32, (EXTRA, members), 0)
    pieces = jnp.where(row == 0, one, jnp.where(row == 1, two, jnp.where(row == 2, three, 0.0)))
    out_ref[...] = jnp.concatenate([observed, pieces], axis=0).astype(jnp.bfloat16)


def observe(obs_rows, obs, weight, recovery, incoming, edge, last, forecast):
    planes, span, height, members = forecast.shape
    count = obs_rows.shape[0]
    vmem = pl.BlockSpec(memory_space=pltpu.VMEM)
    return pl.pallas_call(
        observe_kernel,
        in_specs=[pl.BlockSpec(memory_space=pltpu.SMEM)] + [vmem] * 7 + [pl.BlockSpec(memory_space=pl.ANY)],
        out_specs=vmem,
        out_shape=jax.ShapeDtypeStruct((count + EXTRA, members), jnp.bfloat16),
        scratch_shapes=[
            pltpu.VMEM((count, 8, members), jnp.float32),
            pltpu.VMEM((count, members), jnp.float32),
            pltpu.VMEM((count, members), jnp.float32),
            pltpu.VMEM((count, members), jnp.float32),
            pltpu.VMEM((planes, span, height), jnp.float32),
            pltpu.VMEM((count, height), jnp.float32),
            pltpu.SemaphoreType.DMA((count,)),
        ],
        compiler_params=params(8),
        cost_estimate=cost(40 * count * members, 64 * count * members),
    )(
        obs_rows, obs_rows[:, None], obs[:, None], weight[:, None], recovery, incoming, edge, last,
        forecast,
    )


def anomaly_kernel(first, forecast_ref, rate_ref, incoming_ref, edge_ref, last_ref, *refs):
    anomaly_ref, mean_ref = refs[-2:]
    planes, cells, height, members = forecast_ref.shape
    row = lax.broadcasted_iota(jnp.int32, (height, members), 0)
    for j in range(cells):
        a = (pl.program_id(0) + first) * cells + j
        rates = rate_ref[j]

        def at_edges(low, high):
            return jnp.where(row == 0, low, jnp.where(row == height - 1, high, 0.0))

        arriving = incoming_ref[j] + at_edges(last_ref[0, pl.ds(a, 1), :], last_ref[1, pl.ds(a, 1), :])
        for p in range(planes):
            arriving = rates[:, p : p + 1] * arriving
            halo = at_edges(edge_ref[0, p, pl.ds(a, 1), :], edge_ref[1, p, pl.ds(a, 1), :])
            forecast = forecast_ref[p, j] - arriving - halo
            mean = jnp.sum(forecast, axis=1, keepdims=True) * (1.0 / members)
            anomaly_ref[p, j] = (forecast - mean).astype(jnp.bfloat16)
            mean_ref[p, j] = jnp.broadcast_to(mean, (height, mean_ref.shape[-1]))


def anomalies(forecast, rates, incoming, edge, last, part, parts, held=None):
    planes, span, height, members = forecast.shape
    step = 2 if span % (2 * parts) == 0 else 1
    count = span // parts // step
    first = part * count
    wide = min(128, members)

    def block(width):
        return pl.BlockSpec((planes, step, height, width), lambda i: (0, i + first, 0, 0))

    whole = pl.BlockSpec(memory_space=pltpu.VMEM)
    in_specs = [
        block(members),
        pl.BlockSpec((step, height, planes), lambda i: (i + first, 0, 0)),
        pl.BlockSpec((step, height, members), lambda i: (i + first, 0, 0)),
        whole,
        whole,
    ]
    args = [forecast, rates, incoming, edge, last]
    alias = {}
    if held is not None:
        in_specs += [pl.BlockSpec(memory_space=pl.ANY)] * 2
        args += list(held)
        alias = {5: 0, 6: 1}
    size = forecast.size // parts
    return pl.pallas_call(
        functools.partial(anomaly_kernel, first),
        grid=(count,),
        in_specs=in_specs,
        out_specs=[block(members), block(wide)],
        out_shape=[
            jax.ShapeDtypeStruct(forecast.shape, jnp.bfloat16),
            jax.ShapeDtypeStruct((planes, span, height, wide), jnp.float32),
        ],
        input_output_aliases=alias,
        compiler_params=params(24),
        cost_estimate=cost(10 * size, 8 * size),
    )(*args)


def halves(x):
    big = x.astype(jnp.bfloat16)
    return big, (x - big.astype(jnp.float32)).astype(jnp.bfloat16)


def fine_dot(a, b, dims=NN):
    a_big, a_small = halves(a)
    b_big, b_small = halves(b)
    return dot(a_big, b_big, dims) + (dot(a_big, b_small, dims) + dot(a_small, b_big, dims))


def update_kernel(
    picked, gathered_ref, order_row_ref, order_column_ref, anomaly_ref, mean_ref, out_ref,
    gram, factor, anomalies_held, means_held, results, in_sem, mean_sem, out_sem,
):
    total, members = gathered_ref.shape
    chunks, chunk = anomalies_held.shape[:2]
    bf16, f32 = jnp.bfloat16, jnp.float32

    def rows(c):
        return pl.ds(c * chunk, chunk)

    def fetch(c):
        return (
            pltpu.make_async_copy(anomaly_ref.at[rows(c)], anomalies_held.at[c], in_sem.at[c]),
            pltpu.make_async_copy(mean_ref.at[rows(c)], means_held.at[c], mean_sem.at[c]),
        )

    for c in range(chunks):
        for copy in fetch(c):
            copy.start()

    row = lax.broadcasted_iota(jnp.int32, (members, members), 0)
    column = lax.broadcasted_iota(jnp.int32, (members, members), 1)
    select = jnp.where(order_row_ref[...] == row, 1.0, 0.0).astype(bf16)
    select_t = jnp.where(order_column_ref[...] == column, 1.0, 0.0).astype(bf16)
    block = picked + EXTRA
    gathered = gathered_ref[...]
    place = lax.broadcasted_iota(jnp.int32, (total, members), 0) % block
    observed = jnp.where(place < picked, gathered.astype(f32), 0.0).astype(bf16)
    ordered_t = dot(select_t, observed, NT).astype(bf16)
    slot = lax.broadcasted_iota(jnp.int32, (16, total), 1) % block
    pieces = dot(jnp.where(slot >= picked, 1.0, 0.0).astype(bf16), gathered)
    piece_one = pieces.astype(bf16)
    piece_two, piece_three = halves(pieces - piece_one.astype(f32))
    projection = dot(piece_one, select) + (dot(piece_two, select) + dot(piece_three, select))
    diagonal = row == column
    full = dot(ordered_t, ordered_t, NT) + jnp.where(diagonal, members - 1.0, 0.0)
    on_diagonal = jnp.where(diagonal, full, 0.0)
    scale_row = lax.rsqrt(jnp.sum(on_diagonal, axis=0, keepdims=True))
    scale_column = lax.rsqrt(jnp.sum(on_diagonal, axis=1, keepdims=True))
    unit = full * scale_row * scale_column
    gram[...] = full
    lower = row > column

    def lower_part(residual):
        return jnp.where(lower, residual, jnp.where(diagonal, 0.5 * residual, 0.0))

    identity = jnp.where(diagonal, 1.0, 0.0)
    factor[...] = identity - jnp.where(lower, unit, 0.0)
    unit_big = unit.astype(bf16)
    for _ in range(2):
        inverse = factor[...]
        inverse_big = inverse.astype(bf16)
        half_way = dot(inverse_big, unit_big).astype(bf16)
        residual = dot(half_way, inverse_big, NT) - identity
        factor[...] = inverse - dot(lower_part(residual).astype(bf16), inverse_big)

    def refine(carried):
        step, _ = carried
        inverse = factor[...]
        residual = fine_dot(fine_dot(inverse, unit), inverse, NT) - identity
        factor[...] = inverse - dot(lower_part(residual).astype(bf16), inverse.astype(bf16))
        return step + 1, jnp.sum(residual * residual)

    def unfinished(carried):
        step, error = carried
        return (step < 8) & (error > 0.04) & (error < 64.0)

    _, error = lax.while_loop(unfinished, refine, (0, jnp.float32(1.0)))
    factor[...] = factor[...] * scale_row

    @pl.when(jnp.logical_not(error <= 0.04))
    def _():
        factor[...] = identity

        def eliminate(k, carry):
            held = gram[...]
            pivot_row = gram[pl.ds(k, 1), :]
            pivot = jnp.sum(jnp.where(column[:1] == k, pivot_row, 0.0), axis=1, keepdims=True)
            pivot_column = jnp.sum(jnp.where(column == k, held, 0.0), axis=1, keepdims=True)
            share = jnp.where(row[:, :1] > k, pivot_column / pivot, 0.0)
            factor[...] = factor[...] - share * factor[pl.ds(k, 1), :]
            gram[...] = held - share * pivot_row
            return carry

        lax.fori_loop(0, members, eliminate, 0)
        pivots = jnp.sum(jnp.where(diagonal, gram[...], 0.0), axis=1, keepdims=True)
        factor[...] = factor[...] * lax.rsqrt(pivots)

    inverse = factor[...]
    coefficients = fine_dot(projection, inverse, NT)
    shift = fine_dot(coefficients, inverse)[:1]
    transform_t = ((members - 1.0) ** 0.5 * inverse + shift).astype(bf16)
    weights_t = dot(select, dot(transform_t, select, NT).astype(bf16)).astype(bf16)
    stores = []
    for c in range(chunks):
        for copy in fetch(c):
            copy.wait()
        update = dot(anomalies_held[c], weights_t, NT)
        mean = means_held[c]
        mean = jnp.concatenate([mean] * (members // mean.shape[1]), axis=1)
        results[c] = (mean + update).astype(bf16)
        store = pltpu.make_async_copy(results.at[c], out_ref.at[rows(c)], out_sem.at[c])
        store.start()
        stores.append(store)
    for store in stores:
        store.wait()


def updated(picked, gathered, member_order, anomaly, mean):
    count, members = anomaly.shape
    chunks = 8
    while count % (16 * chunks):
        chunks //= 2
    chunk = count // chunks
    vmem, hbm = pl.BlockSpec(memory_space=pltpu.VMEM), pl.BlockSpec(memory_space=pl.ANY)
    return pl.pallas_call(
        functools.partial(update_kernel, picked),
        in_specs=[vmem] * 3 + [hbm] * 2,
        out_specs=hbm,
        out_shape=jax.ShapeDtypeStruct((count, members), jnp.bfloat16),
        scratch_shapes=[
            pltpu.VMEM((members, members), jnp.float32),
            pltpu.VMEM((members, members), jnp.float32),
            pltpu.VMEM((chunks, chunk, members), jnp.bfloat16),
            pltpu.VMEM((chunks, chunk, mean.shape[1]), jnp.float32),
            pltpu.VMEM((chunks, chunk, members), jnp.bfloat16),
            pltpu.SemaphoreType.DMA((chunks,)),
            pltpu.SemaphoreType.DMA((chunks,)),
            pltpu.SemaphoreType.DMA((chunks,)),
        ],
        compiler_params=params(48),
        cost_estimate=cost(2 * count * members * members, 5 * count * members),
    )(gathered, member_order[None, :], member_order[:, None], anomaly, mean)


def pairs(count, first):
    low = [(i, i + 1) for i in range(first, count - 1, 2)]
    return low + [(j, i) for i, j in low]


def downstream(value, rate):
    count = lax.axis_size("stream")
    steps = [(i, i + 1) for i in range(count - 1)]
    incoming = lax.ppermute(value, "stream", steps)
    for _ in range(count - 2):
        incoming = lax.ppermute(rate * incoming + value, "stream", steps)
    return incoming


def gather_rows(rows, axes):
    for axis in axes:
        count = lax.axis_size(axis)
        if count & (count - 1):
            rows = lax.all_gather(rows, axis, axis=0, tiled=True)
            continue
        apart = count // 2
        while apart:
            other = lax.ppermute(rows, axis, [(i, i ^ apart) for i in range(count)])
            rows = jnp.concatenate([rows, other], axis=0)
            apart //= 2
    return rows


def shards(source, inflow, recovery, obs_rows, obs, observation_weight, member_order):
    planes, span, height, members = source.shape
    levels = lax.axis_size("height")
    parity = lax.axis_index("height") % 2

    def edge_row(at):
        return lax.dynamic_slice_in_dim(source, at, 1, axis=2)[:, :, 0]

    second = lax.ppermute(edge_row(jnp.where(parity == 0, 0, height - 1)), "height", pairs(levels, 1))
    first = lax.ppermute(edge_row(jnp.where(parity == 0, height - 1, 0)), "height", pairs(levels, 0))
    rates = jnp.transpose(recovery, (1, 2, 0))
    held = march(source, inflow, rates, 0, 2)
    forecast, local_end = march(source, inflow, rates, 1, 2, held)
    total = jnp.prod(recovery, axis=0)[..., None] if lax.axis_size("stream") > 2 else None
    incoming = downstream(local_end, total)
    edge, edge_end = edge_march(parity[None], first, second, rates[:, 0], rates[:, height - 1])
    total_edge = None if total is None else jnp.stack([total[:, 0], total[:, height - 1]])
    last = downstream(edge_end, total_edge)
    rows = observe(obs_rows, obs, observation_weight, recovery, incoming, edge, last, forecast)
    gathered = gather_rows(rows, ("height", "span", "stream"))
    parts = 4 if span % 4 == 0 else 1
    held = None
    for part in range(parts):
        held = anomalies(forecast, rates, incoming, edge, last, part, parts, held)
    anomaly, mean = held
    analysis = updated(
        obs_rows.shape[0], gathered, member_order,
        anomaly.reshape(-1, members), mean.reshape(-1, mean.shape[-1]),
    )
    return analysis.reshape(source.shape)


def solution(mesh):
    placed = (
        P("stream", "span", "height", None),
        P("stream", "span", "height", None),
        P("stream", "span", "height"),
        P(("stream", "span", "height")),
        P(("stream", "span", "height")),
        P(("stream", "span", "height")),
        P(),
    )
    return jax.shard_map(
        shards,
        mesh=mesh,
        in_specs=placed,
        out_specs=P("stream", "span", "height", None),
        check_vma=False,
    )
```

time: 302 us -> 129 us (0.43)
  other arithmetic: 114 us -> 0.02 us
  waiting for transfers between devices: 90.9 us -> 13.9 us
  Pallas kernels: 0 us -> 76.5 us
  blocking collectives: 41.8 us -> 0 us
  between operations: 15 us -> 0.43 us
  matrix products: 10 us -> 0 us
  starting transfers between devices: 8.19 us -> 17.9 us
    psum x1 -> x0, waiting for transfers between devices: 84.9 us -> none  [shards(): lax.psum((gram_local, projection), ('stream', 'span', 'height'))]
    pallas_call x0 -> x9, Pallas kernels: none -> 76.5 us  [the longest x1 46 us: updated(): pl.pallas_call(functools.partial(update_kernel, picked), in_specs=[vmem]...]
    another operation x10 -> x0, other arithmetic: 54.8 us -> none  [the longest x6 34 us: lower_cholesky(): return jnp.linalg.cholesky(matrix)]
    psum x1 -> x0, blocking collectives: 41.8 us -> none  [shards(): lax.psum((gram_local, projection), ('stream', 'span', 'height'))]
    dynamic_update_slice x16 -> x0, other arithmetic: 32.8 us -> none  [shards(): lax.scan(march_plane, zero_plane, (recovery, smoothed))]
    unnamed x10 -> x29, local copies, waits for them, and re-layouts: 1.94 us -> 17.5 us
    add x3 -> x0, other arithmetic: 13.1 us -> none  [the longest x1 12 us: shards(): centre + vertical_mix * (padded[:, :, 2:].astype(jnp.float32) + padded[:,...]
    mul x16 -> x0, local copies, waits for them, and re-layouts: 11.2 us -> none  [march_plane(): advanced = plane_rate[..., None] * carried + plane_term]
  transfers between devices with their start and end apart: 4 -> 9, of which waited for: 4 -> 6; matrix products, arithmetic and copies ran while one was open for 1% -> 2% of each run, Pallas kernels for 0% -> 17%
where the time goes in v1:
time: 129 us
  Pallas kernels  76.5 us (59%)
  local copies, waits for them, and re-layouts  20.2 us (16%)
  starting transfers between devices  17.9 us (14%)
  waiting for transfers between devices  13.9 us (11%)
    pallas_call x1, Pallas kernels, updated(): pl.pallas_call(functools.partial(update_kernel, picked), in_specs=[vmem]...  46 us
    pallas_call x4, Pallas kernels, anomalies(): pl.pallas_call(functools.partial(anomaly_kernel, first), grid=(count,), i...  21.8 us
    unnamed x29, local copies, waits for them, and re-layouts  17.5 us
    ppermute x5, starting transfers between devices, gather_rows(): other = lax.ppermute(rows, axis, [(i, i ^ apart) for i in range(count)])  11.1 us
    ppermute x5, waiting for transfers between devices, gather_rows(): other = lax.ppermute(rows, axis, [(i, i ^ apart) for i in range(count)])  11 us
    pallas_call x2, Pallas kernels, march(): pl.pallas_call(march_kernel, grid=(count,), in_specs=in_specs, out_specs=...  5.32 us
    ppermute x2, starting transfers between devices, downstream(): incoming = lax.ppermute(value, 'stream', steps)  3.67 us
    pallas_call x1, Pallas kernels, observe(): pl.pallas_call(observe_kernel, in_specs=[pl.BlockSpec(memory_space=pltpu....  3.24 us
  transfers between devices with their start and end apart: 9, of which 6 were waited for; matrix products, arithmetic and copies ran while one was open for 2% of the time, Pallas kernels for 17%

profile of v1, /device:TPU:0, one launch (start us, length us, event | category | flops | bytes accessed | tf_op | source)
XLA Modules:
  0.0 128.9 jit_solution(17050845373289828690)
XLA Ops:
  0.0 1.0 copy.20
  1.0 0.0 copy-start.4
  1.1 2.2 %copy-done.4 = bf16[16,16,32,256]{3,2,1,0:T(8,128)(2,1)S(1)} copy-done((bf16[16,16,32,256]{3,2,1,0:T(8,128)(2,1)S(1)}, bf16[16,16,32,256]{3,2,1,0:T(8,128)(2,1)}, u32[]{:S(2)}) %copy-start.4) | copy-done | bytes 4194328
  3.2 2.2 %copy-done.5 = bf16[16,16,32,256]{3,2,1,0:T(8,128)(2,1)S(1)} copy-done((bf16[16,16,32,256]{3,2,1,0:T(8,128)(2,1)S(1)}, bf16[16,16,32,256]{3,2,1,0:T(8,128)(2,1)}, u32[]{:S(2)}) %copy-start.5) | copy-done | bytes 4194328
  5.4 2.6 %shard_map.73 = (f32[16,16,32,256]{3,2,1,0:T(8,128)S(1)}, f32[16,32,256]{2,1,0:T(8,128)S(1)}) custom-call(bf16[16,16,32,256]{3,2,1,0:T(8,128)(2,1)S(1)} %copy-done.4, bf16[16,16,32,256]{3,2,1,0:T(8,128)(2,1)S(1)} %copy-done.5, f32[16,32,16]{2,1,0:T(8,128)S(1)} %bitcast.20), custom_call_target="tpu_custom_call" | custom-call | flops 10485760 | bytes 8388608 | tf_op jit(solution)/shard_map/pallas_call | solution.py:63
  8.1 0.0 copy-start.8
  8.1 0.0 copy-start.9
  8.1 0.0 copy-start.10
  8.1 0.0 copy-start.6
  8.1 2.7 %shard_map.74 = (f32[16,16,32,256]{3,2,1,0:T(8,128)S(1)}, f32[16,32,256]{2,1,0:T(8,128)S(1)}) custom-call(bf16[16,16,32,256]{3,2,1,0:T(8,128)(2,1)S(1)} %copy-done.4, bf16[16,16,32,256]{3,2,1,0:T(8,128)(2,1)S(1)} %copy-done.5, f32[16,32,16]{2,1,0:T(8,128)S(1)} %bitcast.21, ...), custom_call_target="tpu_custom_call", output_to_operand_aliasing={{0}: (3, {}), {1}: (4, {})} | custom-call | flops 10485760 | bytes 8388608 | tf_op jit(solution)/shard_map/pallas_call | solution.py:63
  10.8 0.0 copy-start
  10.8 3.3 %copy-done = f32[16,16,32,256]{3,2,1,0:T(8,128)} copy-done((f32[16,16,32,256]{3,2,1,0:T(8,128)}, f32[16,16,32,256]{3,2,1,0:T(8,128)S(1)}, u32[]{:S(2)}) %copy-start) | copy-done | bytes 8388632
  14.1 2.4 %collective-permute-start = (f32[16,32,256]{2,1,0:T(8,128)S(1)}, f32[16,32,256]{2,1,0:T(8,128)S(1)}, u32[]{:S(2)}, u32[]{:S(2)}) collective-permute-start(f32[16,32,256]{2,1,0:T(8,128)S(1)} %get-tuple-element.21), channel_id=1, source_target_pairs={{0,16},{1,17},{2,18},{3,19},{4,20},{5,21},{6,22},{7,23},{8,24},{9,... | collective-permute-start | bytes 1572872 | tf_op jit(solution)/shard_map/ppermute | solution.py:407
  16.5 2.2 %constant_dynamic-slice_fusion = (bf16[16,16,1,256]{3,2,1,0:T(2,128)(2,1)S(1)}, bf16[16,16,1,256]{3,2,1,0:T(2,128)(2,1)S(1)}) fusion(bf16[16,16,32,256]{3,2,1,0:T(8,128)(2,1)} %source_ref.3, s32[]{:T(128)S(6)} %select_n.18, s32[]{:T(128)S(6)} %select_n.17), kind=kLoop, calls=%fused_computation.16 | loop fusion | bytes 524296 | tf_op jit(solution)/shard_map/dynamic_slice | solution.py:433
  18.7 2.5 %collective-permute-start.1 = (bf16[16,16,256]{2,1,0:T(8,128)(2,1)S(1)}, bf16[16,16,256]{2,1,0:T(8,128)(2,1)S(1)}, u32[]{:S(2)}, u32[]{:S(2)}) collective-permute-start(bf16[16,16,256]{2,1,0:T(8,128)(2,1)S(1)} %bitcast.32), channel_id=1, source_target_pairs={{0,1},{2,3},{1,0},{3,2},{4,5},{6,7},{5,4},{7,6},{8,9},{10,11},{9,8... | collective-permute-start | bytes 393224 | tf_op jit(solution)/shard_map/ppermute | solution.py:436
  21.2 0.7 collective-permute-start.2
  21.9 2.3 %collective-permute-done.1.first_ref = bf16[16,16,256]{2,1,0:T(8,128)(2,1)S(1)} collective-permute-done((bf16[16,16,256]{2,1,0:T(8,128)(2,1)S(1)}, bf16[16,16,256]{2,1,0:T(8,128)(2,1)S(1)}, u32[]{:S(2)}, u32[]{:S(2)}) %collective-permute-start.1) | collective-permute-done | bytes 131104 | tf_op jit(solution)/shard_map/ppermute | solution.py:436
  24.2 0.0 collective-permute-done.2.second_ref
  24.2 0.2 shard_map.75
  24.4 1.3 %collective-permute-start.3 = (f32[2,16,256]{2,1,0:T(8,128)S(1)}, f32[2,16,256]{2,1,0:T(8,128)S(1)}, u32[]{:S(2)}, u32[]{:S(2)}) collective-permute-start(f32[2,16,256]{2,1,0:T(8,128)S(1)} %get-tuple-element.23), channel_id=1, source_target_pairs={{0,16},{1,17},{2,18},{3,19},{4,20},{5,21},{6,22},{7,23},{8,24},{9,... | collective-permute-start | bytes 98312 | tf_op jit(solution)/shard_map/ppermute | solution.py:407
  25.7 0.0 copy-done.8
  25.7 0.1 copy.23.rows_column_ref
  25.8 0.0 copy-done.9
  25.8 0.1 copy.24.obs_ref
  25.9 0.1 copy.25.weight_ref
  26.0 0.6 collective-permute-done.3.last_ref
  26.5 0.0 collective-permute-done.incoming_ref
  26.5 3.4 %copy-done.1 = f32[16,16,32,256]{3,2,1,0:T(8,128)S(1)} copy-done((f32[16,16,32,256]{3,2,1,0:T(8,128)S(1)}, f32[16,16,32,256]{3,2,1,0:T(8,128)}, u32[]{:S(2)}) %copy-start.1) | copy-done | bytes 8388632
  29.9 3.2 %shard_map.76 = bf16[40,256]{1,0:T(8,128)(2,1)S(1)} custom-call(s32[32]{0:T(128)S(1)} %copy-done.8, s32[32,1]{1,0:T(8,128)S(1)} %copy.23.rows_column_ref, f32[32,1]{1,0:T(8,128)S(1)} %copy.24.obs_ref, f32[32,1]{1,0:T(8,128)S(1)} %copy.25.weight_ref, f32[16,16,32]{2,1,0:T(8,128)S(1)} %copy-done.6, f32[16,32,256]{2,1,0:T(8,128)S(1)} %collective-permute-done.incoming_ref, ...), custom_call_target="tpu_custom_call" | custom-call | flops 327680 | bytes 524288 | tf_op jit(solution)/shard_map/pallas_call | solution.py:169
  33.2 6.5 %collective-permute-start.4 = (bf16[40,256]{1,0:T(8,128)(2,1)S(1)}, bf16[40,256]{1,0:T(8,128)(2,1)S(1)}, u32[]{:S(2)}, u32[]{:S(2)}) collective-permute-start(bf16[40,256]{1,0:T(8,128)(2,1)S(1)} %shard_map.76), channel_id=1, source_target_pairs={{0,2},{1,3},{2,0},{3,1},{4,6},{5,7},{6,4},{7,5},{8,10},{9,11},{10,... | collective-permute-start | bytes 61448 | tf_op jit(solution)/shard_map/ppermute | solution.py:421
  39.7 1.8 %collective-permute-done.4 = bf16[40,256]{1,0:T(8,128)(2,1)S(1)} collective-permute-done((bf16[40,256]{1,0:T(8,128)(2,1)S(1)}, bf16[40,256]{1,0:T(8,128)(2,1)S(1)}, u32[]{:S(2)}, u32[]{:S(2)}) %collective-permute-start.4) | collective-permute-done | bytes 20512 | tf_op jit(solution)/shard_map/ppermute | solution.py:421
  41.5 1.5 %collective-permute-start.5 = (bf16[80,256]{1,0:T(8,128)(2,1)S(1)}, bf16[80,256]{1,0:T(8,128)(2,1)S(1)}, u32[]{:S(2)}, u32[]{:S(2)}) collective-permute-start(bf16[80,256]{1,0:T(8,128)(2,1)S(1)} %pad_maximum_fusion.2), channel_id=1, source_target_pairs={{0,1},{1,0},{2,3},{3,2},{4,5},{5,4},{6,7},{7,6},{8,9},{9,8},{10,11... | collective-permute-start | bytes 122888 | tf_op jit(solution)/shard_map/ppermute | solution.py:421
  42.9 2.5 %collective-permute-done.5 = bf16[80,256]{1,0:T(8,128)(2,1)S(1)} collective-permute-done((bf16[80,256]{1,0:T(8,128)(2,1)S(1)}, bf16[80,256]{1,0:T(8,128)(2,1)S(1)}, u32[]{:S(2)}, u32[]{:S(2)}) %collective-permute-start.5) | collective-permute-done | bytes 40992 | tf_op jit(solution)/shard_map/ppermute | solution.py:421
  45.5 1.5 %collective-permute-start.6 = (bf16[160,256]{1,0:T(8,128)(2,1)S(1)}, bf16[160,256]{1,0:T(8,128)(2,1)S(1)}, u32[]{:S(2)}, u32[]{:S(2)}) collective-permute-start(bf16[160,256]{1,0:T(8,128)(2,1)S(1)} %pad_maximum_fusion.1), channel_id=1, source_target_pairs={{0,8},{4,12},{8,0},{12,4},{1,9},{5,13},{9,1},{13,5},{2,10},{6,14},... | collective-permute-start | bytes 245768 | tf_op jit(solution)/shard_map/ppermute | solution.py:421
  47.0 2.9 %collective-permute-done.6 = bf16[160,256]{1,0:T(8,128)(2,1)S(1)} collective-permute-done((bf16[160,256]{1,0:T(8,128)(2,1)S(1)}, bf16[160,256]{1,0:T(8,128)(2,1)S(1)}, u32[]{:S(2)}, u32[]{:S(2)}) %collective-permute-start.6) | collective-permute-done | bytes 81952 | tf_op jit(solution)/shard_map/ppermute | solution.py:421
  49.9 1.6 %collective-permute-start.7 = (bf16[320,256]{1,0:T(8,128)(2,1)S(1)}, bf16[320,256]{1,0:T(8,128)(2,1)S(1)}, u32[]{:S(2)}, u32[]{:S(2)}) collective-permute-start(bf16[320,256]{1,0:T(8,128)(2,1)S(1)} %pad_maximum_fusion), channel_id=1, source_target_pairs={{0,4},{4,0},{8,12},{12,8},{1,5},{5,1},{9,13},{13,9},{2,6},{6,2},{1... | collective-permute-start | bytes 491528 | tf_op jit(solution)/shard_map/ppermute | solution.py:421
  51.5 3.8 %collective-permute-done.7 = bf16[320,256]{1,0:T(8,128)(2,1)S(1)} collective-permute-done((bf16[320,256]{1,0:T(8,128)(2,1)S(1)}, bf16[320,256]{1,0:T(8,128)(2,1)S(1)}, u32[]{:S(2)}, u32[]{:S(2)}) %collective-permute-start.7) | collective-permute-done | bytes 163872 | tf_op jit(solution)/shard_map/ppermute | solution.py:421
  55.3 0.1 collective-permute-start.8
  55.4 0.0 copy-done.7
  55.4 0.1 copy.26.order_column_ref
  55.6 3.4 %copy-done.2 = f32[16,16,32,256]{3,2,1,0:T(8,128)S(1)} copy-done((f32[16,16,32,256]{3,2,1,0:T(8,128)S(1)}, f32[16,16,32,256]{3,2,1,0:T(8,128)}, u32[]{:S(2)}) %copy-start.2) | copy-done | bytes 8388632
  58.9 5.4 %shard_map.77 = (bf16[16,16,32,256]{3,2,1,0:T(8,128)(2,1)S(1)}, f32[16,16,32,128]{3,2,1,0:T(8,128)S(1)}) custom-call(f32[16,16,32,256]{3,2,1,0:T(8,128)S(1)} %copy-done.2, f32[16,32,16]{2,1,0:T(8,128)S(1)} %bitcast.23, f32[16,32,256]{2,1,0:T(8,128)S(1)} %collective-permute-done.incoming_ref, f32[2,16,16,256]{3,2,1,0:T(8,128)S(1)} %get-tuple-element.22.edge_ref, ...), custom_call_target="tpu_custom_call" | custom-call | flops 5242880 | bytes 4194304 | tf_op jit(solution)/shard_map/pallas_call | solution.py:237
  64.4 5.5 %shard_map.78 = (bf16[16,16,32,256]{3,2,1,0:T(8,128)(2,1)S(1)}, f32[16,16,32,128]{3,2,1,0:T(8,128)S(1)}) custom-call(f32[16,16,32,256]{3,2,1,0:T(8,128)S(1)} %copy-done.2, f32[16,32,16]{2,1,0:T(8,128)S(1)} %bitcast.24, f32[16,32,256]{2,1,0:T(8,128)S(1)} %collective-permute-done.incoming_ref, ...), custom_call_target="tpu_custom_call", output_to_operand_aliasing={{0}: (5, {}), {1}: (6, {})} | custom-call | flops 5242880 | bytes 4194304 | tf_op jit(solution)/shard_map/pallas_call | solution.py:237
  69.9 5.5 %shard_map.79 = (bf16[16,16,32,256]{3,2,1,0:T(8,128)(2,1)S(1)}, f32[16,16,32,128]{3,2,1,0:T(8,128)S(1)}) custom-call(f32[16,16,32,256]{3,2,1,0:T(8,128)S(1)} %copy-done.2, f32[16,32,16]{2,1,0:T(8,128)S(1)} %bitcast.25, f32[16,32,256]{2,1,0:T(8,128)S(1)} %collective-permute-done.incoming_ref, ...), custom_call_target="tpu_custom_call", output_to_operand_aliasing={{0}: (5, {}), {1}: (6, {})} | custom-call | flops 5242880 | bytes 4194304 | tf_op jit(solution)/shard_map/pallas_call | solution.py:237
  75.3 5.5 %shard_map.80 = (bf16[16,16,32,256]{3,2,1,0:T(8,128)(2,1)S(1)}, f32[16,16,32,128]{3,2,1,0:T(8,128)S(1)}) custom-call(f32[16,16,32,256]{3,2,1,0:T(8,128)S(1)} %copy-done.2, f32[16,32,16]{2,1,0:T(8,128)S(1)} %bitcast.26, f32[16,32,256]{2,1,0:T(8,128)S(1)} %collective-permute-done.incoming_ref, ...), custom_call_target="tpu_custom_call", output_to_operand_aliasing={{0}: (5, {}), {1}: (6, {})} | custom-call | flops 5242880 | bytes 4194304 | tf_op jit(solution)/shard_map/pallas_call | solution.py:237
  80.8 1.9 %copy-done.3 = f32[16,16,32,128]{3,2,1,0:T(8,128)} copy-done((f32[16,16,32,128]{3,2,1,0:T(8,128)}, f32[16,16,32,128]{3,2,1,0:T(8,128)S(1)}, u32[]{:S(2)}) %copy-start.3) | copy-done | bytes 4194328
  82.8 0.0 collective-permute-done.8
  82.8 46.0 %shard_map.81 = bf16[8192,256]{1,0:T(8,128)(2,1)} custom-call(bf16[1280,256]{1,0:T(8,128)(2,1)S(1)} %constant_dynamic-update-slice_fusion.5.gathered_ref, s32[1,256]{1,0:T(1,128)S(1)} %bitcast.30, s32[256,1]{1,0:T(8,128)S(1)} %copy.26.order_column_ref, bf16[8192,256]{1,0:T(8,128)(2,1)S(1)} %bitcast.18, f32[8192,128]{1,0:T(8,128)} %bitcast.19), custom_call_target="tpu_custom_call" | custom-call | flops 1073741824 | bytes 10485760 | tf_op jit(solution)/shard_map/pallas_call | solution.py:379
  (19 shorter events, 0.2 us)
Async XLA Ops:
  1.0 2.2 %copy-start.4 = (bf16[16,16,32,256]{3,2,1,0:T(8,128)(2,1)S(1)}, bf16[16,16,32,256]{3,2,1,0:T(8,128)(2,1)}, u32[]{:S(2)}) copy-start(bf16[16,16,32,256]{3,2,1,0:T(8,128)(2,1)} %source_ref.3) | copy-start | bytes 12582916
  3.2 2.2 %copy-start.5 = (bf16[16,16,32,256]{3,2,1,0:T(8,128)(2,1)S(1)}, bf16[16,16,32,256]{3,2,1,0:T(8,128)(2,1)}, u32[]{:S(2)}) copy-start(bf16[16,16,32,256]{3,2,1,0:T(8,128)(2,1)} %inflow_ref.3) | copy-start | bytes 12582916
  8.1 17.6 %copy-start.8 = (s32[32]{0:T(128)S(1)}, s32[32]{0:T(128)}, u32[]{:S(2)}) copy-start(s32[32]{0:T(128)} %rows_ref.1) | copy-start | bytes 388
  8.1 17.7 %copy-start.9 = (f32[32]{0:T(128)S(1)}, f32[32]{0:T(128)}, u32[]{:S(2)}) copy-start(f32[32]{0:T(128)} %param.11) | copy-start | bytes 388
  8.1 17.8 %copy-start.10 = (f32[32]{0:T(128)S(1)}, f32[32]{0:T(128)}, u32[]{:S(2)}) copy-start(f32[32]{0:T(128)} %param.12) | copy-start | bytes 388
  8.1 18.4 %copy-start.6 = (f32[16,16,32]{2,1,0:T(8,128)S(1)}, f32[16,16,32]{2,1,0:T(8,128)}, u32[]{:S(2)}) copy-start(f32[16,16,32]{2,1,0:T(8,128)} %rate_ref.1) | copy-start | bytes 98308
  10.8 3.3 %copy-start = (f32[16,16,32,256]{3,2,1,0:T(8,128)}, f32[16,16,32,256]{3,2,1,0:T(8,128)S(1)}, u32[]{:S(2)}) copy-start(f32[16,16,32,256]{3,2,1,0:T(8,128)S(1)} %get-tuple-element.24.forecast_ref) | copy-start | bytes 25165828
  14.1 12.5 %collective-permute-start = (f32[16,32,256]{2,1,0:T(8,128)S(1)}, f32[16,32,256]{2,1,0:T(8,128)S(1)}, u32[]{:S(2)}, u32[]{:S(2)}) collective-permute-start(f32[16,32,256]{2,1,0:T(8,128)S(1)} %get-tuple-element.21), channel_id=1, source_target_pairs={{0,16},{1,17},{2,18},{3,19},{4,20},{5,21},{6,22},{7,23},{8,24},{9,... | collective-permute-start | bytes 1572872 | tf_op jit(solution)/shard_map/ppermute | solution.py:407
  18.7 5.5 %collective-permute-start.1 = (bf16[16,16,256]{2,1,0:T(8,128)(2,1)S(1)}, bf16[16,16,256]{2,1,0:T(8,128)(2,1)S(1)}, u32[]{:S(2)}, u32[]{:S(2)}) collective-permute-start(bf16[16,16,256]{2,1,0:T(8,128)(2,1)S(1)} %bitcast.32), channel_id=1, source_target_pairs={{0,1},{2,3},{1,0},{3,2},{4,5},{6,7},{5,4},{7,6},{8,9},{10,11},{9,8... | collective-permute-start | bytes 393224 | tf_op jit(solution)/shard_map/ppermute | solution.py:436
  21.2 3.0 %collective-permute-start.2 = (bf16[16,16,256]{2,1,0:T(8,128)(2,1)S(1)}, bf16[16,16,256]{2,1,0:T(8,128)(2,1)S(1)}, u32[]{:S(2)}, u32[]{:S(2)}) collective-permute-start(bf16[16,16,256]{2,1,0:T(8,128)(2,1)S(1)} %bitcast.33), channel_id=1, source_target_pairs={{1,2},{2,1},{5,6},{6,5},{9,10},{10,9},{13,14},{14,13},{17,18},{18,... | collective-permute-start | bytes 393224 | tf_op jit(solution)/shard_map/ppermute | solution.py:435
  24.4 2.1 %collective-permute-start.3 = (f32[2,16,256]{2,1,0:T(8,128)S(1)}, f32[2,16,256]{2,1,0:T(8,128)S(1)}, u32[]{:S(2)}, u32[]{:S(2)}) collective-permute-start(f32[2,16,256]{2,1,0:T(8,128)S(1)} %get-tuple-element.23), channel_id=1, source_target_pairs={{0,16},{1,17},{2,18},{3,19},{4,20},{5,21},{6,22},{7,23},{8,24},{9,... | collective-permute-start | bytes 98312 | tf_op jit(solution)/shard_map/ppermute | solution.py:407
  26.5 3.4 %copy-start.1 = (f32[16,16,32,256]{3,2,1,0:T(8,128)S(1)}, f32[16,16,32,256]{3,2,1,0:T(8,128)}, u32[]{:S(2)}) copy-start(f32[16,16,32,256]{3,2,1,0:T(8,128)} %copy-done) | copy-start | bytes 25165828
  29.9 25.5 %copy-start.7 = (s32[256]{0:T(256)S(1)}, s32[256]{0:T(256)}, u32[]{:S(2)}) copy-start(s32[256]{0:T(256)} %param.13) | copy-start | bytes 3076
  33.2 8.3 %collective-permute-start.4 = (bf16[40,256]{1,0:T(8,128)(2,1)S(1)}, bf16[40,256]{1,0:T(8,128)(2,1)S(1)}, u32[]{:S(2)}, u32[]{:S(2)}) collective-permute-start(bf16[40,256]{1,0:T(8,128)(2,1)S(1)} %shard_map.76), channel_id=1, source_target_pairs={{0,2},{1,3},{2,0},{3,1},{4,6},{5,7},{6,4},{7,5},{8,10},{9,11},{10,... | collective-permute-start | bytes 61448 | tf_op jit(solution)/shard_map/ppermute | solution.py:421
  41.5 4.0 %collective-permute-start.5 = (bf16[80,256]{1,0:T(8,128)(2,1)S(1)}, bf16[80,256]{1,0:T(8,128)(2,1)S(1)}, u32[]{:S(2)}, u32[]{:S(2)}) collective-permute-start(bf16[80,256]{1,0:T(8,128)(2,1)S(1)} %pad_maximum_fusion.2), channel_id=1, source_target_pairs={{0,1},{1,0},{2,3},{3,2},{4,5},{5,4},{6,7},{7,6},{8,9},{9,8},{10,11... | collective-permute-start | bytes 122888 | tf_op jit(solution)/shard_map/ppermute | solution.py:421
  45.5 4.4 %collective-permute-start.6 = (bf16[160,256]{1,0:T(8,128)(2,1)S(1)}, bf16[160,256]{1,0:T(8,128)(2,1)S(1)}, u32[]{:S(2)}, u32[]{:S(2)}) collective-permute-start(bf16[160,256]{1,0:T(8,128)(2,1)S(1)} %pad_maximum_fusion.1), channel_id=1, source_target_pairs={{0,8},{4,12},{8,0},{12,4},{1,9},{5,13},{9,1},{13,5},{2,10},{6,14},... | collective-permute-start | bytes 245768 | tf_op jit(solution)/shard_map/ppermute | solution.py:421
  49.9 5.4 %collective-permute-start.7 = (bf16[320,256]{1,0:T(8,128)(2,1)S(1)}, bf16[320,256]{1,0:T(8,128)(2,1)S(1)}, u32[]{:S(2)}, u32[]{:S(2)}) collective-permute-start(bf16[320,256]{1,0:T(8,128)(2,1)S(1)} %pad_maximum_fusion), channel_id=1, source_target_pairs={{0,4},{4,0},{8,12},{12,8},{1,5},{5,1},{9,13},{13,9},{2,6},{6,2},{1... | collective-permute-start | bytes 491528 | tf_op jit(solution)/shard_map/ppermute | solution.py:421
  55.3 27.5 %collective-permute-start.8 = (bf16[640,256]{1,0:T(8,128)(2,1)S(1)}, bf16[640,256]{1,0:T(8,128)(2,1)S(1)}, u32[]{:S(2)}, u32[]{:S(2)}) collective-permute-start(bf16[640,256]{1,0:T(8,128)(2,1)S(1)} %get-tuple-element.37), channel_id=1, source_target_pairs={{0,16},{16,0},{1,17},{17,1},{2,18},{18,2},{3,19},{19,3},{4,20},{20... | collective-permute-start | bytes 983048 | tf_op jit(solution)/shard_map/ppermute | solution.py:421
  55.6 3.4 %copy-start.2 = (f32[16,16,32,256]{3,2,1,0:T(8,128)S(1)}, f32[16,16,32,256]{3,2,1,0:T(8,128)}, u32[]{:S(2)}) copy-start(f32[16,16,32,256]{3,2,1,0:T(8,128)} %copy-done) | copy-start | bytes 25165828
  80.8 2.0 %copy-start.3 = (f32[16,16,32,128]{3,2,1,0:T(8,128)}, f32[16,16,32,128]{3,2,1,0:T(8,128)S(1)}, u32[]{:S(2)}) copy-start(f32[16,16,32,128]{3,2,1,0:T(8,128)S(1)} %get-tuple-element.32) | copy-start | bytes 12582916

commit v2 on v1

v2 whole, which is shorter than its diff:
```python
import functools

import jax
import jax.numpy as jnp
from jax import lax
from jax.experimental import pallas as pl
from jax.experimental.pallas import tpu as pltpu
from jax.sharding import PartitionSpec as P

vertical_mix = 0.25
MIB = 1024 * 1024
NT = (((1,), (1,)), ((), ()))
NN = (((1,), (0,)), ((), ()))
LIMIT = 40
EXTRA = 8


def dot(a, b, dims=NN):
    return lax.dot_general(a, b, dims, preferred_element_type=jnp.float32)


def params(mib):
    return pltpu.CompilerParams(vmem_limit_bytes=mib * MIB)


def cost(elements, nbytes):
    return pl.CostEstimate(flops=1000 * elements, bytes_accessed=nbytes, transcendentals=0)


def border_kernel(high_ref, source_ref, out_ref, held, sems):
    planes, span, rows, members = held.shape
    height = source_ref.shape[2]
    high = high_ref[0] == 1
    start = pl.multiple_of(jnp.where(high, height - rows, 0), rows)
    count = sems.shape[0]
    step = planes // count

    def fetch(c):
        part = pl.ds(c * step, step)
        return pltpu.make_async_copy(
            source_ref.at[part, :, pl.ds(start, rows), :], held.at[part], sems.at[c]
        )

    for c in range(count):
        fetch(c).start()
    for c in range(count):
        fetch(c).wait()
        for p in range(c * step, (c + 1) * step):
            block = held[p].astype(jnp.float32)
            low = jnp.concatenate([block[a, :1] for a in range(span)], axis=0)
            top = jnp.concatenate([block[a, rows - 1 :] for a in range(span)], axis=0)
            out_ref[p] = jnp.where(high, top, low).astype(jnp.bfloat16)


def border(source, high):
    planes, span, height, members = source.shape
    count = 4 if planes % 4 == 0 else 1
    return pl.pallas_call(
        border_kernel,
        in_specs=[pl.BlockSpec(memory_space=pltpu.SMEM), pl.BlockSpec(memory_space=pltpu.HBM)],
        out_specs=pl.BlockSpec(memory_space=pltpu.VMEM),
        out_shape=jax.ShapeDtypeStruct((planes, span, members), jnp.bfloat16),
        scratch_shapes=[
            pltpu.VMEM((planes, span, 16, members), jnp.bfloat16),
            pltpu.SemaphoreType.DMA((count,)),
        ],
        compiler_params=params(LIMIT),
        cost_estimate=cost(source.size // 2, source.size),
    )(high, source)


def place_of(r, shape):
    _, span, height = shape
    return r // (span * height), r // height % span, r % height


def march_kernel(part, cells, has_more, *refs):
    if has_more:
        (rows_ref, rows_column_ref, source_ref, rate_ref, recovery_ref, picks_in_ref, inflow_ref,
         end_ref, picks_ref, share_ref, deficits, tiles, tiles_wide, through_rows, through, sems) = refs
    else:
        rows_ref, source_ref, rate_ref, end_ref, picks_ref, deficits = refs
    planes, step, height, members = source_ref.shape
    count = picks_ref.shape[0]
    at = pl.program_id(0)
    shape = recovery_ref.shape if has_more else (planes, cells, height)

    def fetch(k):
        p, a, b = place_of(rows_ref[k], shape)
        start = pl.multiple_of(b // 16 * 16, 16)
        return pltpu.make_async_copy(inflow_ref.at[p, a, pl.ds(start, 16), :], tiles.at[k], sems.at[k])

    if has_more:

        @pl.when(at == 0)
        def _():
            for k in range(count):
                fetch(k).start()

    row = lax.broadcasted_iota(jnp.int32, (height, members), 0)
    inner_low = jnp.where(row == 0, 0.0, vertical_mix)
    inner_high = jnp.where(row == height - 1, 0.0, vertical_mix)
    for j in range(step):
        rates = rate_ref[j]
        deficit = None
        for p in range(planes):
            x = source_ref[p, j].astype(jnp.float32)
            term = (1.0 - 2.0 * vertical_mix) * x
            term = term + inner_low * pltpu.roll(x, 1, 0)
            term = term + inner_high * pltpu.roll(x, height - 1, 0)
            deficit = term if p == 0 else rates[:, p : p + 1] * deficit + term
            deficits[p, at * step + j] = deficit
        end_ref[j] = deficit

    @pl.when(at == pl.num_programs(0) - 1)
    def _():
        local = deficits.shape[1]
        for k in range(count):
            p, a, b = place_of(rows_ref[k], (planes, cells, height))
            here = a - part * local
            inside = jnp.where((here >= 0) & (here < local), -1.0, 0.0)
            here = jnp.clip(here, 0, local - 1)
            picks_ref[pl.ds(k, 1), :] = inside * deficits[p, here, pl.ds(b, 1), :]
        if has_more:
            product = None
            for p in range(planes):
                product = recovery_ref[p] if p == 0 else product * recovery_ref[p]
                through[p] = product
            for k in range(count):
                p, a, _ = place_of(rows_ref[k], shape)
                through_rows[pl.ds(k, 1), :] = through[p, pl.ds(a, 1), :]
            cell = rows_column_ref[...] % height
            lane = lax.broadcasted_iota(jnp.int32, (count, height), 1)
            share = jnp.sum(jnp.where(lane == cell, through_rows[...], 0.0), axis=1, keepdims=True)
            share_ref[...] = jnp.broadcast_to(share, share_ref.shape)
            for k in range(count):
                fetch(k).wait()
            tiles_wide[...] = tiles[...].astype(jnp.float32)
            for k in range(count):
                _, _, b = place_of(rows_ref[k], shape)
                picks_ref[pl.ds(k, 1), :] = (
                    picks_ref[pl.ds(k, 1), :] + picks_in_ref[pl.ds(k, 1), :] + tiles_wide[k, pl.ds(b % 16, 1), :]
                )


def march(source, rates, obs_rows, part, parts, more=()):
    planes, span, height, members = source.shape
    observed = obs_rows.shape[0]
    local = span // parts
    step = 2 if local % 2 == 0 else 1
    count = local // step
    first = part * count
    vmem, hbm = pl.BlockSpec(memory_space=pltpu.VMEM), pl.BlockSpec(memory_space=pltpu.HBM)
    smem = pl.BlockSpec(memory_space=pltpu.SMEM)
    in_specs = [
        pl.BlockSpec((planes, step, height, members), lambda i: (0, i + first, 0, 0)),
        pl.BlockSpec((step, height, planes), lambda i: (i + first, 0, 0)),
    ]
    out_specs = [pl.BlockSpec((step, height, members), lambda i: (i, 0, 0)), vmem]
    out_shape = [
        jax.ShapeDtypeStruct((local, height, members), jnp.float32),
        jax.ShapeDtypeStruct((observed, members), jnp.float32),
    ]
    scratch = [pltpu.VMEM((planes, local, height, members), jnp.float32)]
    args = [obs_rows, source, rates]
    in_specs = [smem] + in_specs
    if more:
        recovery, picks, inflow = more
        in_specs = [smem, vmem] + in_specs[1:] + [vmem, vmem, hbm]
        args = [obs_rows, obs_rows[:, None], source, rates, recovery, picks, inflow]
        out_specs.append(vmem)
        out_shape.append(jax.ShapeDtypeStruct((observed, members), jnp.float32))
        scratch += [
            pltpu.VMEM((observed, 16, members), jnp.bfloat16),
            pltpu.VMEM((observed, 16, members), jnp.float32),
            pltpu.VMEM((observed, height), jnp.float32),
            pltpu.VMEM((planes, span, height), jnp.float32),
            pltpu.SemaphoreType.DMA((observed,)),
        ]
    size = source.size // parts
    return pl.pallas_call(
        functools.partial(march_kernel, part, span, bool(more)),
        grid=(count,),
        in_specs=in_specs,
        out_specs=out_specs,
        out_shape=out_shape,
        scratch_shapes=scratch,
        compiler_params=params(LIMIT),
        cost_estimate=cost(3 * size, 4 * size),
    )(*args)


def edge_kernel(parity_ref, first_ref, second_ref, low_rate_ref, high_rate_ref, term_ref, edge_ref, last_ref):
    planes = first_ref.shape[0]
    even = parity_ref[0] == 0
    low, high = None, None
    for p in range(planes):
        one = vertical_mix * first_ref[p].astype(jnp.float32)
        two = vertical_mix * second_ref[p].astype(jnp.float32)
        low_term = jnp.where(even, two, one)
        high_term = jnp.where(even, one, two)
        term_ref[0, p] = low_term
        term_ref[1, p] = high_term
        low = low_term if p == 0 else low_rate_ref[:, p : p + 1] * low + low_term
        high = high_term if p == 0 else high_rate_ref[:, p : p + 1] * high + high_term
        edge_ref[0, p] = low
        edge_ref[1, p] = high
    last_ref[0] = low
    last_ref[1] = high


def edge_march(parity, first, second, low_rate, high_rate):
    planes, span, members = first.shape
    vmem = pl.BlockSpec(memory_space=pltpu.VMEM)
    return pl.pallas_call(
        edge_kernel,
        in_specs=[pl.BlockSpec(memory_space=pltpu.SMEM)] + [vmem] * 4,
        out_specs=[vmem] * 3,
        out_shape=[
            jax.ShapeDtypeStruct((2, planes, span, members), jnp.float32),
            jax.ShapeDtypeStruct((2, planes, span, members), jnp.float32),
            jax.ShapeDtypeStruct((2, span, members), jnp.float32),
        ],
        compiler_params=params(LIMIT),
        cost_estimate=cost(first.size, 8 * first.size),
    )(parity, first, second, low_rate, high_rate)


def observe_kernel(
    rows_ref, obs_ref, weight_ref, picks_ref, share_ref, incoming_ref, edge_ref, last_ref,
    out_ref, arriving, halo,
):
    planes = edge_ref.shape[1]
    span, height, members = incoming_ref.shape
    count = picks_ref.shape[0]
    for k in range(count):
        p, a, b = place_of(rows_ref[k], (planes, span, height))
        side = jnp.where(b == height - 1, 1, 0)
        at_edge = jnp.where((b == 0) | (b == height - 1), 1.0, 0.0)
        arriving[pl.ds(k, 1), :] = (
            incoming_ref[a, pl.ds(b, 1), :] + at_edge * last_ref[side, pl.ds(a, 1), :]
        )
        halo[pl.ds(k, 1), :] = at_edge * edge_ref[side, p, pl.ds(a, 1), :]
    forecast = picks_ref[...] - halo[...] - share_ref[...] * arriving[...]
    mean = jnp.sum(forecast, axis=1, keepdims=True) * (1.0 / members)
    anomaly = (forecast - mean).astype(jnp.bfloat16).astype(jnp.float32)
    weight = weight_ref[...]
    observed = weight * anomaly
    misfit = weight * (obs_ref[...] - mean)
    projection = jnp.sum(observed * misfit, axis=0, keepdims=True)
    one = projection.astype(jnp.bfloat16).astype(jnp.float32)
    two = (projection - one).astype(jnp.bfloat16).astype(jnp.float32)
    three = projection - one - two
    row = lax.broadcasted_iota(jnp.int32, (EXTRA, members), 0)
    pieces = jnp.where(row == 0, one, jnp.where(row == 1, two, jnp.where(row == 2, three, 0.0)))
    out_ref[...] = jnp.concatenate([observed, pieces], axis=0).astype(jnp.bfloat16)


def observe(obs_rows, obs, weight, picks, share, incoming, edge, last):
    count, members = picks.shape
    vmem = pl.BlockSpec(memory_space=pltpu.VMEM)
    return pl.pallas_call(
        observe_kernel,
        in_specs=[pl.BlockSpec(memory_space=pltpu.SMEM)] + [vmem] * 7,
        out_specs=vmem,
        out_shape=jax.ShapeDtypeStruct((count + EXTRA, members), jnp.bfloat16),
        scratch_shapes=[pltpu.VMEM((count, members), jnp.float32)] * 2,
        compiler_params=params(LIMIT),
        cost_estimate=cost(40 * count * members, 64 * count * members),
    )(obs_rows, obs[:, None], weight[:, None], picks, share, incoming, edge, last)


def forecast_kernel(first, source_ref, inflow_ref, rate_ref, incoming_ref, term_ref, last_ref, *refs):
    out_ref = refs[-1]
    planes, step, height, members = source_ref.shape
    row = lax.broadcasted_iota(jnp.int32, (height, members), 0)
    for j in range(step):
        a = (pl.program_id(0) + first) * step + j
        rates = rate_ref[j]

        def outside(low, high):
            return jnp.where(row == 0, low, jnp.where(row == height - 1, high, 0.0))

        deficit = incoming_ref[j] + outside(last_ref[0, pl.ds(a, 1), :], last_ref[1, pl.ds(a, 1), :])
        for p in range(planes):
            x = vertical_mix * source_ref[p, j].astype(jnp.float32)
            below = jnp.where(row == 0, term_ref[0, p, pl.ds(a, 1), :], pltpu.roll(x, 1, 0))
            above = jnp.where(row == height - 1, term_ref[1, p, pl.ds(a, 1), :], pltpu.roll(x, height - 1, 0))
            term = (1.0 / vertical_mix - 2.0) * x + (below + above)
            deficit = rates[:, p : p + 1] * deficit + term
            out_ref[p, j] = (inflow_ref[p, j].astype(jnp.float32) - deficit).astype(jnp.bfloat16)


def forecasts(source, inflow, rates, incoming, term, last, part, parts, held=None):
    planes, span, height, members = source.shape
    local = span // parts
    step = 2 if local % 2 == 0 else 1
    count = local // step
    first = part * count
    block = pl.BlockSpec((planes, step, height, members), lambda i: (0, i + first, 0, 0))
    vmem = pl.BlockSpec(memory_space=pltpu.VMEM)
    in_specs = [
        block,
        block,
        pl.BlockSpec((step, height, planes), lambda i: (i + first, 0, 0)),
        pl.BlockSpec((step, height, members), lambda i: (i + first, 0, 0)),
        vmem,
        vmem,
    ]
    args = [source, inflow, rates, incoming, term, last]
    alias = {}
    if held is not None:
        in_specs.append(pl.BlockSpec(memory_space=pltpu.HBM))
        args.append(held)
        alias = {6: 0}
    size = source.size // parts
    return pl.pallas_call(
        functools.partial(forecast_kernel, first),
        grid=(count,),
        in_specs=in_specs,
        out_specs=block,
        out_shape=pltpu.HBM(source.shape, jnp.bfloat16),
        input_output_aliases=alias,
        compiler_params=params(LIMIT),
        cost_estimate=cost(4 * size, 6 * size),
    )(*args)


def halves(x):
    big = x.astype(jnp.bfloat16)
    return big, (x - big.astype(jnp.float32)).astype(jnp.bfloat16)


def fine_dot(a, b, dims=NN):
    a_big, a_small = halves(a)
    b_big, b_small = halves(b)
    return dot(a_big, b_big, dims) + (dot(a_big, b_small, dims) + dot(a_small, b_big, dims))


def update_kernel(
    picked, gathered_ref, order_row_ref, order_column_ref, forecast_ref, out_ref,
    gram, factor, forecasts_held, results, in_sem, out_sem,
):
    total, members = gathered_ref.shape
    chunks = forecasts_held.shape[0]
    cells = forecasts_held.shape[1:4]
    bf16, f32 = jnp.bfloat16, jnp.float32

    step = cells[0]

    def rows(c):
        return pl.ds(c * step, step)

    def fetch(c):
        return pltpu.make_async_copy(forecast_ref.at[rows(c)], forecasts_held.at[c], in_sem.at[c])

    for c in range(chunks):
        fetch(c).start()

    row = lax.broadcasted_iota(jnp.int32, (members, members), 0)
    column = lax.broadcasted_iota(jnp.int32, (members, members), 1)
    select = jnp.where(order_row_ref[...] == row, 1.0, 0.0).astype(bf16)
    select_t = jnp.where(order_column_ref[...] == column, 1.0, 0.0).astype(bf16)
    block = picked + EXTRA
    gathered = gathered_ref[...]
    place = lax.broadcasted_iota(jnp.int32, (total, members), 0) % block
    observed = jnp.where(place < picked, gathered.astype(f32), 0.0).astype(bf16)
    ordered_t = dot(select_t, observed, NT).astype(bf16)
    slot = lax.broadcasted_iota(jnp.int32, (16, total), 1) % block
    pieces = dot(jnp.where(slot >= picked, 1.0, 0.0).astype(bf16), gathered)
    piece_one = pieces.astype(bf16)
    piece_two, piece_three = halves(pieces - piece_one.astype(f32))
    projection = dot(piece_one, select) + (dot(piece_two, select) + dot(piece_three, select))
    diagonal = row == column
    full = dot(ordered_t, ordered_t, NT) + jnp.where(diagonal, members - 1.0, 0.0)
    on_diagonal = jnp.where(diagonal, full, 0.0)
    scale_row = lax.rsqrt(jnp.sum(on_diagonal, axis=0, keepdims=True))
    scale_column = lax.rsqrt(jnp.sum(on_diagonal, axis=1, keepdims=True))
    unit = full * scale_row * scale_column
    gram[...] = full
    lower = row > column

    def lower_part(residual):
        return jnp.where(lower, residual, jnp.where(diagonal, 0.5 * residual, 0.0))

    identity = jnp.where(diagonal, 1.0, 0.0)
    factor[...] = identity - jnp.where(lower, unit, 0.0)
    unit_big = unit.astype(bf16)
    for _ in range(2):
        inverse = factor[...]
        inverse_big = inverse.astype(bf16)
        half_way = dot(inverse_big, unit_big).astype(bf16)
        residual = dot(half_way, inverse_big, NT) - identity
        factor[...] = inverse - dot(lower_part(residual).astype(bf16), inverse_big)

    def refine(carried):
        step, _ = carried
        inverse = factor[...]
        residual = fine_dot(fine_dot(inverse, unit), inverse, NT) - identity
        factor[...] = inverse - dot(lower_part(residual).astype(bf16), inverse.astype(bf16))
        return step + 1, jnp.sum(residual * residual)

    def unfinished(carried):
        step, error = carried
        return (step < 8) & (error > 0.04) & (error < 64.0)

    _, error = lax.while_loop(unfinished, refine, (0, jnp.float32(1.0)))
    factor[...] = factor[...] * scale_row

    @pl.when(jnp.logical_not(error <= 0.04))
    def _():
        factor[...] = identity

        def eliminate(k, carry):
            held = gram[...]
            pivot_row = gram[pl.ds(k, 1), :]
            pivot = jnp.sum(jnp.where(column[:1] == k, pivot_row, 0.0), axis=1, keepdims=True)
            pivot_column = jnp.sum(jnp.where(column == k, held, 0.0), axis=1, keepdims=True)
            share = jnp.where(row[:, :1] > k, pivot_column / pivot, 0.0)
            factor[...] = factor[...] - share * factor[pl.ds(k, 1), :]
            gram[...] = held - share * pivot_row
            return carry

        lax.fori_loop(0, members, eliminate, 0)
        pivots = jnp.sum(jnp.where(diagonal, gram[...], 0.0), axis=1, keepdims=True)
        factor[...] = factor[...] * lax.rsqrt(pivots)

    inverse = factor[...]
    coefficients = fine_dot(projection, inverse, NT)
    shift = fine_dot(coefficients, inverse)[:1]
    transform_t = (members - 1.0) ** 0.5 * inverse + shift
    transform_t = transform_t + (1.0 - jnp.sum(transform_t, axis=1, keepdims=True)) * (1.0 / members)
    transform_t = transform_t.astype(bf16)
    weights_t = dot(select, dot(transform_t, select, NT).astype(bf16)).astype(bf16)
    stores = []
    for c in range(chunks):
        fetch(c).wait()
        forecast = forecasts_held[c].reshape(-1, members)
        results[c] = dot(forecast, weights_t, NT).astype(bf16).reshape(cells + (members,))
        store = pltpu.make_async_copy(results.at[c], out_ref.at[rows(c)], out_sem.at[c])
        store.start()
        stores.append(store)
    for store in stores:
        store.wait()


def updated(picked, gathered, member_order, forecast):
    planes, span, height, members = forecast.shape
    count = planes * span * height
    chunks = 8
    while planes % chunks:
        chunks //= 2
    held = (chunks, planes // chunks, span, height, members)
    vmem, hbm = pl.BlockSpec(memory_space=pltpu.VMEM), pl.BlockSpec(memory_space=pltpu.HBM)
    return pl.pallas_call(
        functools.partial(update_kernel, picked),
        in_specs=[vmem] * 3 + [hbm],
        out_specs=hbm,
        out_shape=jax.ShapeDtypeStruct(forecast.shape, jnp.bfloat16),
        scratch_shapes=[
            pltpu.VMEM((members, members), jnp.float32),
            pltpu.VMEM((members, members), jnp.float32),
            pltpu.VMEM(held, jnp.bfloat16),
            pltpu.VMEM(held, jnp.bfloat16),
            pltpu.SemaphoreType.DMA((chunks,)),
            pltpu.SemaphoreType.DMA((chunks,)),
        ],
        compiler_params=params(LIMIT),
        cost_estimate=cost(4 * count * members, 5 * count * members),
    )(gathered, member_order[None, :], member_order[:, None], forecast)


def pairs(count, first):
    low = [(i, i + 1) for i in range(first, count - 1, 2)]
    return low + [(j, i) for i, j in low]


def downstream(value, rate):
    count = lax.axis_size("stream")
    steps = [(i, i + 1) for i in range(count - 1)]
    incoming = lax.ppermute(value, "stream", steps)
    for _ in range(count - 2):
        incoming = lax.ppermute(rate * incoming + value, "stream", steps)
    return incoming


def exchanges(axes):
    for axis in axes:
        count = lax.axis_size(axis)
        if count & (count - 1):
            yield functools.partial(lax.all_gather, axis_name=axis, axis=0, tiled=True)
            continue
        apart = count // 2
        while apart:
            steps = [(i, i ^ apart) for i in range(count)]

            def swap(rows, axis=axis, steps=steps):
                return jnp.concatenate([rows, lax.ppermute(rows, axis, steps)], axis=0)

            yield swap
            apart //= 2


def shards(source, inflow, recovery, obs_rows, obs, observation_weight, member_order):
    planes, span, height, members = source.shape
    levels = lax.axis_size("height")
    parity = (lax.axis_index("height") % 2)[None]
    together = lax.optimization_barrier

    source = pltpu.with_memory_space_constraint(source, pltpu.HBM)
    inflow = pltpu.with_memory_space_constraint(inflow, pltpu.HBM)
    row = border(source, 1 - parity)
    first = lax.ppermute(row, "height", pairs(levels, 0))
    held_recovery, row = together((recovery, row))
    rates = jnp.transpose(held_recovery, (1, 2, 0))
    end_one, picks = march(source, rates, obs_rows, 0, 2)
    high, _ = together((parity, picks))
    row = border(source, high)
    row, first = together((row, first))
    second = lax.ppermute(row, "height", pairs(levels, 1))
    held_rates, picks, row = together((rates, picks, row))
    end_two, picks, share = march(source, held_rates, obs_rows, 1, 2, (recovery, picks, inflow))
    local_end = jnp.concatenate([end_one, end_two], axis=0)
    local_end, second = together((local_end, second))
    total = jnp.prod(recovery, axis=0)[..., None] if lax.axis_size("stream") > 2 else None
    incoming = downstream(local_end, total)
    term, edge, edge_end = edge_march(parity, first, second, rates[:, 0], rates[:, height - 1])
    total_edge = None if total is None else jnp.stack([total[:, 0], total[:, height - 1]])
    last = downstream(edge_end, total_edge)
    rows = observe(obs_rows, obs, observation_weight, picks, share, incoming, edge, last)
    parts = 4 if span % 4 == 0 else 1
    forecast = None
    part = 0
    for swap in exchanges(("height", "span", "stream")):
        swapped = swap(rows)
        if part < parts:
            held_source, rows = together((source, rows))
            forecast = forecasts(held_source, inflow, rates, incoming, term, last, part, parts, forecast)
            swapped, forecast = together((swapped, forecast))
            part += 1
        rows = swapped
    for part in range(part, parts):
        forecast = forecasts(source, inflow, rates, incoming, term, last, part, parts, forecast)
    forecast = pltpu.with_memory_space_constraint(forecast, pltpu.HBM)
    return updated(obs_rows.shape[0], rows, member_order, forecast)


def solution(mesh):
    placed = (
        P("stream", "span", "height", None),
        P("stream", "span", "height", None),
        P("stream", "span", "height"),
        P(("stream", "span", "height")),
        P(("stream", "span", "height")),
        P(("stream", "span", "height")),
        P(),
    )
    return jax.shard_map(
        shards,
        mesh=mesh,
        in_specs=placed,
        out_specs=P("stream", "span", "height", None),
        check_vma=False,
    )
```

time: 129 us -> 92.3 us (0.72)
  local copies, waits for them, and re-layouts: 20.2 us -> 0.57 us
  waiting for transfers between devices: 13.9 us -> 2.86 us
  Pallas kernels: 76.5 us -> 72.4 us
  starting transfers between devices: 17.9 us -> 15.6 us
    unnamed x29 -> x10, local copies, waits for them, and re-layouts: 17.5 us -> 0.03 us
    ppermute x7, waiting for transfers between devices: 13.3 us -> 2.21 us  [the longest x5 2.2 us: swap(): return jnp.concatenate([rows, lax.ppermute(rows, axis, steps)], axis=0)]
    dynamic_slice x1 -> x0, local copies, waits for them, and re-layouts: 2.22 us -> none  [edge_row(): return lax.dynamic_slice_in_dim(source, at, 1, axis=2)[:, :, 0]]
    pallas_call x1, Pallas kernels: 3.24 us -> 1.26 us  [observe(): pl.pallas_call(observe_kernel, in_specs=[pl.BlockSpec(memory_space=pltpu....]
    pallas_call x6 -> x8, Pallas kernels: 27.2 us -> 25.3 us  [the longest x4 12.3 us: forecasts(): pl.pallas_call(functools.partial(forecast_kernel, first), grid=(count,),...]
    ppermute x7, starting transfers between devices: 14.3 us -> 12.9 us  [the longest x5 9.1 us: swap(): return jnp.concatenate([rows, lax.ppermute(rows, axis, steps)], axis=0)]
  transfers between devices with their start and end apart: 9 -> 9, of which waited for: 6 -> 3; matrix products, arithmetic and copies ran while one was open for 2% -> 1% of each run, Pallas kernels for 17% -> 26%
where the time goes in v2:
time: 92.3 us; the launch traced here: 91.9 us
  Pallas kernels  72.4 us (78%)
  starting transfers between devices  15.6 us (17%)
  waiting for transfers between devices  2.86 us (3%)
    pallas_call x1, Pallas kernels, updated(): pl.pallas_call(functools.partial(update_kernel, picked), in_specs=[vmem]...  45.7 us
    pallas_call x4, Pallas kernels, forecasts(): pl.pallas_call(functools.partial(forecast_kernel, first), grid=(count,),...  12.3 us
    pallas_call x2, Pallas kernels, march(): pl.pallas_call(functools.partial(march_kernel, part, span, bool(more)), g...  9.59 us
    ppermute x5, starting transfers between devices, swap(): return jnp.concatenate([rows, lax.ppermute(rows, axis, steps)], axis=0)  9.1 us
    pallas_call x2, Pallas kernels, border(): pl.pallas_call(border_kernel, in_specs=[pl.BlockSpec(memory_space=pltpu.S...  3.33 us
    ppermute x1, starting transfers between devices, shards(): first = lax.ppermute(row, 'height', pairs(levels, 0))  3.09 us
    ppermute x2, starting transfers between devices, downstream(): incoming = lax.ppermute(value, 'stream', steps)  2.78 us
    ppermute x5, waiting for transfers between devices, swap(): return jnp.concatenate([rows, lax.ppermute(rows, axis, steps)], axis=0)  2.2 us
  transfers between devices with their start and end apart: 9, of which 3 were waited for; matrix products, arithmetic and copies ran while one was open for 1% of the time, Pallas kernels for 26%

profile of v2, /device:TPU:0, one launch (start us, length us, event | category | flops | bytes accessed | tf_op | source)
XLA Modules:
  0.0 91.9 jit_solution(10722635066641637182)
XLA Ops:
  0.0 0.0 copy-start
  0.0 0.0 copy-start.2
  0.0 1.7 %shard_map.73 = bf16[16,16,256]{2,1,0:T(8,128)(2,1)S(1)} custom-call(s32[1]{0:T(128)S(6)} %sub.3.high_ref, bf16[16,16,32,256]{3,2,1,0:T(8,128)(2,1)} %source_ref.7), custom_call_target="tpu_custom_call" | custom-call | flops 1048576000 | bytes 2097152 | tf_op jit(solution)/shard_map/pallas_call | solution.py:58
  1.7 3.1 %collective-permute-start = (bf16[16,16,256]{2,1,0:T(8,128)(2,1)S(1)}, bf16[16,16,256]{2,1,0:T(8,128)(2,1)S(1)}, u32[]{:S(2)}, u32[]{:S(2)}) collective-permute-start(bf16[16,16,256]{2,1,0:T(8,128)(2,1)S(1)} %shard_map.73), channel_id=1, source_target_pairs={{0,1},{2,3},{1,0},{3,2},{4,5},{6,7},{5,4},{7,6},{8,9},{10,11},{9,8... | collective-permute-start | bytes 393224 | tf_op jit(solution)/shard_map/ppermute | solution.py:513
  4.8 0.0 copy-done
  4.8 0.1 copy.15
  4.9 0.0 copy-done.2
  4.9 4.0 %shard_map.74 = (f32[8,32,256]{2,1,0:T(8,128)S(1)}, f32[32,256]{1,0:T(8,128)S(1)}) custom-call(s32[32]{0:T(128)S(1)} %copy-done.2, bf16[16,16,32,256]{3,2,1,0:T(8,128)(2,1)} %source_ref.7, f32[16,32,16]{2,1,0:T(8,128)S(1)} %bitcast.9), custom_call_target="tpu_custom_call" | custom-call | flops 3145728000 | bytes 4194304 | tf_op jit(solution)/shard_map/pallas_call | solution.py:181
  9.0 0.1 copy.16.refs_1_
  9.1 1.6 %shard_map.75 = bf16[16,16,256]{2,1,0:T(8,128)(2,1)S(1)} custom-call(s32[1]{0:T(128)} %bitcast.3.high_ref.parity_ref, bf16[16,16,32,256]{3,2,1,0:T(8,128)(2,1)} %source_ref.7), custom_call_target="tpu_custom_call" | custom-call | flops 1048576000 | bytes 2097152 | tf_op jit(solution)/shard_map/pallas_call | solution.py:58
  10.7 0.0 copy-start.3
  10.7 0.0 copy-start.4
  10.7 0.0 collective-permute-done.first_ref
  10.8 0.7 collective-permute-start.1
  11.4 5.6 %shard_map.76 = (f32[8,32,256]{2,1,0:T(8,128)S(1)}, f32[32,256]{1,0:T(8,128)S(1)}, f32[32,256]{1,0:T(8,128)S(1)}) custom-call(s32[32]{0:T(128)S(1)} %copy-done.2, s32[32,1]{1,0:T(8,128)S(1)} %copy.16.refs_1_, bf16[16,16,32,256]{3,2,1,0:T(8,128)(2,1)} %source_ref.7, f32[16,32,16]{2,1,0:T(8,128)S(1)} %bitcast.10, f32[16,16,32]{2,1,0:T(8,128)S(1)} %copy-done, ...), custom_call_target="tpu_custom_call" | custom-call | flops 3145728000 | bytes 4194304 | tf_op jit(solution)/shard_map/pallas_call | solution.py:181
  17.0 0.0 collective-permute-done.1.second_ref
  17.1 1.5 %collective-permute-start.2 = (f32[16,32,256]{2,1,0:T(8,128)S(1)}, f32[16,32,256]{2,1,0:T(8,128)S(1)}, u32[]{:S(2)}, u32[]{:S(2)}) collective-permute-start(f32[16,32,256]{2,1,0:T(8,128)S(1)} %pad_maximum_fusion.1), channel_id=1, source_target_pairs={{0,16},{1,17},{2,18},{3,19},{4,20},{5,21},{6,22},{7,23},{8,24},{9,... | collective-permute-start | bytes 1572872 | tf_op jit(solution)/shard_map/ppermute | solution.py:481
  18.6 0.2 shard_map.77
  18.7 1.3 %collective-permute-start.3 = (f32[2,16,256]{2,1,0:T(8,128)S(1)}, f32[2,16,256]{2,1,0:T(8,128)S(1)}, u32[]{:S(2)}, u32[]{:S(2)}) collective-permute-start(f32[2,16,256]{2,1,0:T(8,128)S(1)} %get-tuple-element.47), channel_id=1, source_target_pairs={{0,16},{1,17},{2,18},{3,19},{4,20},{5,21},{6,22},{7,23},{8,24},{9,... | collective-permute-start | bytes 98312 | tf_op jit(solution)/shard_map/ppermute | solution.py:481
  20.0 0.0 copy-done.3
  20.1 0.1 copy.17.obs_ref
  20.1 0.0 copy-done.4
  20.1 0.1 copy.18.weight_ref
  20.2 0.7 collective-permute-done.3.last_ref
  20.9 0.0 collective-permute-done.2.incoming_ref
  20.9 1.3 %shard_map.78 = bf16[40,256]{1,0:T(8,128)(2,1)S(1)} custom-call(s32[32]{0:T(128)S(1)} %copy-done.2, f32[32,1]{1,0:T(8,128)S(1)} %copy.17.obs_ref, f32[32,1]{1,0:T(8,128)S(1)} %copy.18.weight_ref, f32[32,256]{1,0:T(8,128)S(1)} %get-tuple-element.39.picks_ref, f32[32,256]{1,0:T(8,128)S(1)} %get-tuple-element.40.share_ref, ...), custom_call_target="tpu_custom_call" | custom-call | flops 327680000 | bytes 524288 | tf_op jit(solution)/shard_map/pallas_call | solution.py:262
  22.2 3.9 %collective-permute-start.4 = (bf16[40,256]{1,0:T(8,128)(2,1)S(1)}, bf16[40,256]{1,0:T(8,128)(2,1)S(1)}, u32[]{:S(2)}, u32[]{:S(2)}) collective-permute-start(bf16[40,256]{1,0:T(8,128)(2,1)S(1)} %shard_map.78), channel_id=1, source_target_pairs={{0,2},{1,3},{2,0},{3,1},{4,6},{5,7},{6,4},{7,5},{8,10},{9,11},{10,... | collective-permute-start | bytes 61448 | tf_op jit(solution)/shard_map/ppermute | solution.py:498
  26.1 3.1 %shard_map.79.refs_0_ = bf16[16,16,32,256]{3,2,1,0:T(8,128)(2,1)} custom-call(bf16[16,16,32,256]{3,2,1,0:T(8,128)(2,1)} %source_ref.7, bf16[16,16,32,256]{3,2,1,0:T(8,128)(2,1)} %inflow_ref.7, f32[16,32,16]{2,1,0:T(8,128)S(1)} %bitcast.12, f32[16,32,256]{2,1,0:T(8,128)S(1)} %collective-permute-done.2.incoming_ref, ...), custom_call_target="tpu_custom_call" | custom-call | flops 2097152000 | bytes 3145728 | tf_op jit(solution)/shard_map/pallas_call | solution.py:317
  29.1 0.0 collective-permute-done.4
  29.2 2.0 %collective-permute-start.5 = (bf16[80,256]{1,0:T(8,128)(2,1)S(1)}, bf16[80,256]{1,0:T(8,128)(2,1)S(1)}, u32[]{:S(2)}, u32[]{:S(2)}) collective-permute-start(bf16[80,256]{1,0:T(8,128)(2,1)S(1)} %pad_maximum_fusion.5), channel_id=1, source_target_pairs={{0,1},{1,0},{2,3},{3,2},{4,5},{5,4},{6,7},{7,6},{8,9},{9,8},{10,11... | collective-permute-start | bytes 122888 | tf_op jit(solution)/shard_map/ppermute | solution.py:498
  31.1 3.1 %shard_map.80.refs_0_ = bf16[16,16,32,256]{3,2,1,0:T(8,128)(2,1)} custom-call(bf16[16,16,32,256]{3,2,1,0:T(8,128)(2,1)} %source_ref.7, bf16[16,16,32,256]{3,2,1,0:T(8,128)(2,1)} %inflow_ref.7, f32[16,32,16]{2,1,0:T(8,128)S(1)} %bitcast.13, f32[16,32,256]{2,1,0:T(8,128)S(1)} %collective-permute-done.2.incoming_ref, ...), custom_call_target="tpu_custom_call", output_to_operand_aliasing={{}: (6, {})} | custom-call | flops 2097152000 | bytes 3145728 | tf_op jit(solution)/shard_map/pallas_call | solution.py:317
  34.2 0.0 collective-permute-done.5
  34.2 1.6 %collective-permute-start.6 = (bf16[160,256]{1,0:T(8,128)(2,1)S(1)}, bf16[160,256]{1,0:T(8,128)(2,1)S(1)}, u32[]{:S(2)}, u32[]{:S(2)}) collective-permute-start(bf16[160,256]{1,0:T(8,128)(2,1)S(1)} %pad_maximum_fusion.4), channel_id=1, source_target_pairs={{0,8},{4,12},{8,0},{12,4},{1,9},{5,13},{9,1},{13,5},{2,10},{6,14},... | collective-permute-start | bytes 245768 | tf_op jit(solution)/shard_map/ppermute | solution.py:498
  35.8 3.1 %shard_map.81.refs_0_ = bf16[16,16,32,256]{3,2,1,0:T(8,128)(2,1)} custom-call(bf16[16,16,32,256]{3,2,1,0:T(8,128)(2,1)} %source_ref.7, bf16[16,16,32,256]{3,2,1,0:T(8,128)(2,1)} %inflow_ref.7, f32[16,32,16]{2,1,0:T(8,128)S(1)} %bitcast.14, f32[16,32,256]{2,1,0:T(8,128)S(1)} %collective-permute-done.2.incoming_ref, ...), custom_call_target="tpu_custom_call", output_to_operand_aliasing={{}: (6, {})} | custom-call | flops 2097152000 | bytes 3145728 | tf_op jit(solution)/shard_map/pallas_call | solution.py:317
  38.9 0.0 collective-permute-done.6
  38.9 0.0 copy-start.1
  38.9 1.6 %collective-permute-start.7 = (bf16[320,256]{1,0:T(8,128)(2,1)S(1)}, bf16[320,256]{1,0:T(8,128)(2,1)S(1)}, u32[]{:S(2)}, u32[]{:S(2)}) collective-permute-start(bf16[320,256]{1,0:T(8,128)(2,1)S(1)} %pad_maximum_fusion.3), channel_id=1, source_target_pairs={{0,4},{4,0},{8,12},{12,8},{1,5},{5,1},{9,13},{13,9},{2,6},{6,2},{1... | collective-permute-start | bytes 491528 | tf_op jit(solution)/shard_map/ppermute | solution.py:498
  40.5 3.1 %shard_map.82.forecast_ref = bf16[16,16,32,256]{3,2,1,0:T(8,128)(2,1)} custom-call(bf16[16,16,32,256]{3,2,1,0:T(8,128)(2,1)} %source_ref.7, bf16[16,16,32,256]{3,2,1,0:T(8,128)(2,1)} %inflow_ref.7, f32[16,32,16]{2,1,0:T(8,128)S(1)} %bitcast.15, f32[16,32,256]{2,1,0:T(8,128)S(1)} %collective-permute-done.2.incoming_ref, ...), custom_call_target="tpu_custom_call", output_to_operand_aliasing={{}: (6, {})} | custom-call | flops 2097152000 | bytes 3145728 | tf_op jit(solution)/shard_map/pallas_call | solution.py:317
  43.6 0.7 collective-permute-done.7
  44.3 0.1 collective-permute-start.8
  44.4 0.0 copy-done.1
  44.4 0.1 copy.19.order_column_ref
  44.6 1.5 %collective-permute-done.8 = bf16[640,256]{1,0:T(8,128)(2,1)S(1)} collective-permute-done((bf16[640,256]{1,0:T(8,128)(2,1)S(1)}, bf16[640,256]{1,0:T(8,128)(2,1)S(1)}, u32[]{:S(2)}, u32[]{:S(2)}) %collective-permute-start.8) | collective-permute-done | bytes 327712 | tf_op jit(solution)/shard_map/ppermute | solution.py:498
  46.1 45.7 %shard_map.83 = bf16[16,16,32,256]{3,2,1,0:T(8,128)(2,1)} custom-call(bf16[1280,256]{1,0:T(8,128)(2,1)S(1)} %pad_maximum_fusion.gathered_ref, s32[1,256]{1,0:T(1,128)S(1)} %bitcast.19, s32[256,1]{1,0:T(8,128)S(1)} %copy.19.order_column_ref, bf16[16,16,32,256]{3,2,1,0:T(8,128)(2,1)} %shard_map.82.forecast_ref), custom_call_target="tpu_custom_call" | custom-call | flops 8388608000 | bytes 10485760 | tf_op jit(solution)/shard_map/pallas_call | solution.py:455
  (7 shorter events, 0.1 us)
Async XLA Ops:
  0.0 4.8 %copy-start = (f32[16,16,32]{2,1,0:T(8,128)S(1)}, f32[16,16,32]{2,1,0:T(8,128)}, u32[]{:S(2)}) copy-start(f32[16,16,32]{2,1,0:T(8,128)} %refs_4_.1) | copy-start | bytes 98308
  0.0 4.9 %copy-start.2 = (s32[32]{0:T(128)S(1)}, s32[32]{0:T(128)}, u32[]{:S(2)}) copy-start(s32[32]{0:T(128)} %rows_ref.1) | copy-start | bytes 388
  1.7 9.1 %collective-permute-start = (bf16[16,16,256]{2,1,0:T(8,128)(2,1)S(1)}, bf16[16,16,256]{2,1,0:T(8,128)(2,1)S(1)}, u32[]{:S(2)}, u32[]{:S(2)}) collective-permute-start(bf16[16,16,256]{2,1,0:T(8,128)(2,1)S(1)} %shard_map.73), channel_id=1, source_target_pairs={{0,1},{2,3},{1,0},{3,2},{4,5},{6,7},{5,4},{7,6},{8,9},{10,11},{9,8... | collective-permute-start | bytes 393224 | tf_op jit(solution)/shard_map/ppermute | solution.py:513
  10.7 9.3 %copy-start.3 = (f32[32]{0:T(128)S(1)}, f32[32]{0:T(128)}, u32[]{:S(2)}) copy-start(f32[32]{0:T(128)} %param.11) | copy-start | bytes 388
  10.7 9.4 %copy-start.4 = (f32[32]{0:T(128)S(1)}, f32[32]{0:T(128)}, u32[]{:S(2)}) copy-start(f32[32]{0:T(128)} %param.12) | copy-start | bytes 388
  10.8 6.3 %collective-permute-start.1 = (bf16[16,16,256]{2,1,0:T(8,128)(2,1)S(1)}, bf16[16,16,256]{2,1,0:T(8,128)(2,1)S(1)}, u32[]{:S(2)}, u32[]{:S(2)}) collective-permute-start(bf16[16,16,256]{2,1,0:T(8,128)(2,1)S(1)} %shard_map.75), channel_id=1, source_target_pairs={{1,2},{2,1},{5,6},{6,5},{9,10},{10,9},{13,14},{14,13},{17,18},{18,... | collective-permute-start | bytes 393224 | tf_op jit(solution)/shard_map/ppermute | solution.py:520
  17.1 3.8 %collective-permute-start.2 = (f32[16,32,256]{2,1,0:T(8,128)S(1)}, f32[16,32,256]{2,1,0:T(8,128)S(1)}, u32[]{:S(2)}, u32[]{:S(2)}) collective-permute-start(f32[16,32,256]{2,1,0:T(8,128)S(1)} %pad_maximum_fusion.1), channel_id=1, source_target_pairs={{0,16},{1,17},{2,18},{3,19},{4,20},{5,21},{6,22},{7,23},{8,24},{9,... | collective-permute-start | bytes 1572872 | tf_op jit(solution)/shard_map/ppermute | solution.py:481
  18.7 2.1 %collective-permute-start.3 = (f32[2,16,256]{2,1,0:T(8,128)S(1)}, f32[2,16,256]{2,1,0:T(8,128)S(1)}, u32[]{:S(2)}, u32[]{:S(2)}) collective-permute-start(f32[2,16,256]{2,1,0:T(8,128)S(1)} %get-tuple-element.47), channel_id=1, source_target_pairs={{0,16},{1,17},{2,18},{3,19},{4,20},{5,21},{6,22},{7,23},{8,24},{9,... | collective-permute-start | bytes 98312 | tf_op jit(solution)/shard_map/ppermute | solution.py:481
  22.2 7.0 %collective-permute-start.4 = (bf16[40,256]{1,0:T(8,128)(2,1)S(1)}, bf16[40,256]{1,0:T(8,128)(2,1)S(1)}, u32[]{:S(2)}, u32[]{:S(2)}) collective-permute-start(bf16[40,256]{1,0:T(8,128)(2,1)S(1)} %shard_map.78), channel_id=1, source_target_pairs={{0,2},{1,3},{2,0},{3,1},{4,6},{5,7},{6,4},{7,5},{8,10},{9,11},{10,... | collective-permute-start | bytes 61448 | tf_op jit(solution)/shard_map/ppermute | solution.py:498
  29.2 5.1 %collective-permute-start.5 = (bf16[80,256]{1,0:T(8,128)(2,1)S(1)}, bf16[80,256]{1,0:T(8,128)(2,1)S(1)}, u32[]{:S(2)}, u32[]{:S(2)}) collective-permute-start(bf16[80,256]{1,0:T(8,128)(2,1)S(1)} %pad_maximum_fusion.5), channel_id=1, source_target_pairs={{0,1},{1,0},{2,3},{3,2},{4,5},{5,4},{6,7},{7,6},{8,9},{9,8},{10,11... | collective-permute-start | bytes 122888 | tf_op jit(solution)/shard_map/ppermute | solution.py:498
  34.2 4.7 %collective-permute-start.6 = (bf16[160,256]{1,0:T(8,128)(2,1)S(1)}, bf16[160,256]{1,0:T(8,128)(2,1)S(1)}, u32[]{:S(2)}, u32[]{:S(2)}) collective-permute-start(bf16[160,256]{1,0:T(8,128)(2,1)S(1)} %pad_maximum_fusion.4), channel_id=1, source_target_pairs={{0,8},{4,12},{8,0},{12,4},{1,9},{5,13},{9,1},{13,5},{2,10},{6,14},... | collective-permute-start | bytes 245768 | tf_op jit(solution)/shard_map/ppermute | solution.py:498
  38.9 5.5 %copy-start.1 = (s32[256]{0:T(256)S(1)}, s32[256]{0:T(256)}, u32[]{:S(2)}) copy-start(s32[256]{0:T(256)} %param.13) | copy-start | bytes 3076
  38.9 5.4 %collective-permute-start.7 = (bf16[320,256]{1,0:T(8,128)(2,1)S(1)}, bf16[320,256]{1,0:T(8,128)(2,1)S(1)}, u32[]{:S(2)}, u32[]{:S(2)}) collective-permute-start(bf16[320,256]{1,0:T(8,128)(2,1)S(1)} %pad_maximum_fusion.3), channel_id=1, source_target_pairs={{0,4},{4,0},{8,12},{12,8},{1,5},{5,1},{9,13},{13,9},{2,6},{6,2},{1... | collective-permute-start | bytes 491528 | tf_op jit(solution)/shard_map/ppermute | solution.py:498
  44.3 1.7 %collective-permute-start.8 = (bf16[640,256]{1,0:T(8,128)(2,1)S(1)}, bf16[640,256]{1,0:T(8,128)(2,1)S(1)}, u32[]{:S(2)}, u32[]{:S(2)}) collective-permute-start(bf16[640,256]{1,0:T(8,128)(2,1)S(1)} %pad_maximum_fusion.2), channel_id=1, source_target_pairs={{0,16},{16,0},{1,17},{17,1},{2,18},{18,2},{3,19},{19,3},{4,20},{20... | collective-permute-start | bytes 983048 | tf_op jit(solution)/shard_map/ppermute | solution.py:498

commit v3 on v2

v3 whole, which is shorter than its diff:
```python
import functools

import jax
import jax.numpy as jnp
from jax import lax
from jax.experimental import pallas as pl
from jax.experimental.pallas import tpu as pltpu
from jax.sharding import PartitionSpec as P

vertical_mix = 0.25
MIB = 1024 * 1024
NT = (((1,), (1,)), ((), ()))
NN = (((1,), (0,)), ((), ()))
LIMIT = 24
CUTS = (0, 3, 7, 11, 16)
EXTRA = 8


def dot(a, b, dims=NN):
    return lax.dot_general(a, b, dims, preferred_element_type=jnp.float32)


def params(mib):
    return pltpu.CompilerParams(vmem_limit_bytes=mib * MIB)


def cost(elements, nbytes):
    return pl.CostEstimate(flops=1000 * elements, bytes_accessed=nbytes, transcendentals=0)


def take_border(out_ref, p, block, high):
    span, rows, _ = block.shape
    block = block.astype(jnp.float32)
    low = jnp.concatenate([block[a, :1] for a in range(span)], axis=0)
    top = jnp.concatenate([block[a, rows - 1 :] for a in range(span)], axis=0)
    out_ref[p] = jnp.where(high, top, low).astype(jnp.bfloat16)


def far_border_kernel(high_ref, source_ref, out_ref, held, sems):
    planes, span, rows, members = held.shape
    height = source_ref.shape[2]
    high = high_ref[0] == 1
    start = pl.multiple_of(jnp.where(high, height - rows, 0), rows)
    count = sems.shape[0]
    step = planes // count

    def fetch(c):
        part = pl.ds(c * step, step)
        return pltpu.make_async_copy(
            source_ref.at[part, :, pl.ds(start, rows), :], held.at[part], sems.at[c]
        )

    for c in range(count):
        fetch(c).start()
    for c in range(count):
        fetch(c).wait()
        for p in range(c * step, (c + 1) * step):
            take_border(out_ref, p, held[p], high)


def near_border_kernel(high_ref, source_ref, out_ref):
    high = high_ref[0] == 1
    height = source_ref.shape[2]
    start = pl.multiple_of(jnp.where(high, height - 16, 0), 16)
    for p in range(source_ref.shape[0]):
        take_border(out_ref, p, source_ref[p, :, pl.ds(start, 16), :], high)


def border(source, high, near):
    planes, span, height, members = source.shape
    count = 4 if planes % 4 == 0 else 1
    vmem = pl.BlockSpec(memory_space=pltpu.VMEM)
    scratch = [
        pltpu.VMEM((planes, span, 16, members), jnp.bfloat16),
        pltpu.SemaphoreType.DMA((count,)),
    ]
    return pl.pallas_call(
        near_border_kernel if near else far_border_kernel,
        in_specs=[pl.BlockSpec(memory_space=pltpu.SMEM), vmem if near else pl.BlockSpec(memory_space=pltpu.HBM)],
        out_specs=vmem,
        out_shape=jax.ShapeDtypeStruct((planes, span, members), jnp.bfloat16),
        scratch_shapes=[] if near else scratch,
        compiler_params=params(LIMIT),
        cost_estimate=cost(source.size // 2, source.size),
    )(high, source)


def place_of(r, shape):
    _, span, height = shape
    return r // (span * height), r // height % span, r % height


def group_of(span, height):
    cells = max(1, min(span, 256 // height))
    while span % cells:
        cells -= 1
    return cells


def stencil(rows, height):
    row = lax.broadcasted_iota(jnp.int32, (rows, rows), 0)
    column = lax.broadcasted_iota(jnp.int32, (rows, rows), 1)
    apart = jnp.where(row // height == column // height, jnp.abs(row - column), 2)
    entry = jnp.where(apart == 0, 1.0 - 2.0 * vertical_mix, jnp.where(apart == 1, vertical_mix, 0.0))
    return entry.astype(jnp.bfloat16)


def upright(row):
    count = row.shape[1]
    place = lax.broadcasted_iota(jnp.int32, (count, count), 0)
    lane = lax.broadcasted_iota(jnp.int32, (count, count), 1)
    return jnp.sum(jnp.where(place == lane, row, jnp.zeros_like(row)), axis=1, keepdims=True)


def march_kernel(start, last, *refs):
    if last:
        (rows_ref, rows_row_ref, source_ref, rate_ref, state_ref, recovery_ref, picks_in_ref, inflow_ref,
         end_ref, picks_ref, share_ref, deficits, tiles, through_rows, through) = refs
    else:
        (rows_ref, source_ref, recovery_ref, end_ref, picks_ref, rate_ref, low_rate_ref, high_rate_ref,
         deficits) = refs
    planes, _, members = deficits.shape
    shape = source_ref.shape[:3]
    _, span, height = shape
    count = picks_ref.shape[0]
    cells = group_of(span, height)
    group = cells * height
    if not last:
        blocks = [jnp.transpose(recovery_ref[:, a, :]) for a in range(span)]
        for a in range(span):
            rate_ref[a * height : (a + 1) * height] = blocks[a]
        low_rate_ref[...] = jnp.concatenate([block[:1] for block in blocks], axis=0)
        high_rate_ref[...] = jnp.concatenate([block[height - 1 :] for block in blocks], axis=0)
    mix = stencil(group, height)
    for p in range(planes):
        for c in range(span // cells):
            part = slice(c * group, (c + 1) * group)
            term = dot(mix, source_ref[start + p, c * cells : (c + 1) * cells].reshape(group, members))
            if p == 0 and not last:
                deficits[p, part] = term
            else:
                before = state_ref[part] if p == 0 else deficits[p - 1, part]
                deficits[p, part] = rate_ref[part, start + p : start + p + 1] * before + term
    end_ref[...] = deficits[planes - 1]
    for k in range(count):
        p, a, b = place_of(rows_ref[k], shape)
        inside = jnp.where((p >= start) & (p < start + planes), -1.0, 0.0)
        here = jnp.clip(p - start, 0, planes - 1)
        picks_ref[pl.ds(k, 1), :] = inside * deficits[here, pl.ds(a * height + b, 1), :]
    if last:
        product = None
        for p in range(shape[0]):
            product = recovery_ref[p] if p == 0 else product * recovery_ref[p]
            through[p] = product
        for k in range(count):
            p, a, _ = place_of(rows_ref[k], shape)
            through_rows[pl.ds(k, 1), :] = through[p, pl.ds(a, 1), :]
        cell = upright(rows_row_ref[...].astype(jnp.float32)).astype(jnp.int32) % height
        lane = lax.broadcasted_iota(jnp.int32, (count, height), 1)
        share = jnp.sum(jnp.where(lane == cell, through_rows[...], 0.0), axis=1, keepdims=True)
        share_ref[...] = jnp.broadcast_to(share, share_ref.shape)
        for k in range(count):
            p, a, b = place_of(rows_ref[k], shape)
            first = pl.multiple_of(b // 16 * 16, 16)
            tiles[k] = inflow_ref[p, a, pl.ds(first, 16), :].astype(jnp.float32)
        for k in range(count):
            _, _, b = place_of(rows_ref[k], shape)
            picks_ref[pl.ds(k, 1), :] = (
                picks_ref[pl.ds(k, 1), :] + picks_in_ref[pl.ds(k, 1), :] + tiles[k, pl.ds(b % 16, 1), :]
            )


def march(source, rates, obs_rows, start, stop, more=()):
    shape = source.shape
    _, span, height, members = shape
    observed = obs_rows.shape[0]
    planes, cells = stop - start, span * height
    vmem, smem = pl.BlockSpec(memory_space=pltpu.VMEM), pl.BlockSpec(memory_space=pltpu.SMEM)
    out_shape = [
        jax.ShapeDtypeStruct((cells, members), jnp.float32),
        jax.ShapeDtypeStruct((observed, members), jnp.float32),
    ]
    scratch = [pltpu.VMEM((planes, cells, members), jnp.float32)]
    args = [obs_rows, source, rates]
    in_specs = [smem, vmem, vmem]
    if not more:
        out_shape += [
            jax.ShapeDtypeStruct((cells, shape[0]), jnp.float32),
            jax.ShapeDtypeStruct((span, shape[0]), jnp.float32),
            jax.ShapeDtypeStruct((span, shape[0]), jnp.float32),
        ]
    else:
        state, recovery, picks, inflow = more
        in_specs = [smem] + [vmem] * 7
        args = [obs_rows, obs_rows[None, :], source, rates, state, recovery, picks, inflow]
        out_shape.append(jax.ShapeDtypeStruct((observed, members), jnp.float32))
        scratch += [
            pltpu.VMEM((observed, 16, members), jnp.float32),
            pltpu.VMEM((observed, height), jnp.float32),
            pltpu.VMEM(shape[:3], jnp.float32),
        ]
    size = planes * cells * members
    return pl.pallas_call(
        functools.partial(march_kernel, start, bool(more)),
        in_specs=in_specs,
        out_specs=[vmem] * len(out_shape),
        out_shape=out_shape,
        scratch_shapes=scratch,
        compiler_params=params(LIMIT),
        cost_estimate=cost(3 * size, 4 * size),
    )(*args)


def edge_kernel(
    parity_ref, first_ref, second_ref, low_rate_ref, high_rate_ref, end_ref, term_ref, edge_ref, leaving_ref
):
    planes, span, members = first_ref.shape
    height = leaving_ref.shape[1]
    even = parity_ref[0] == 0
    low, high = None, None
    for p in range(planes):
        one = vertical_mix * first_ref[p].astype(jnp.float32)
        two = vertical_mix * second_ref[p].astype(jnp.float32)
        low_term = jnp.where(even, two, one)
        high_term = jnp.where(even, one, two)
        term_ref[0, p] = low_term
        term_ref[1, p] = high_term
        low = low_term if p == 0 else low_rate_ref[:, p : p + 1] * low + low_term
        high = high_term if p == 0 else high_rate_ref[:, p : p + 1] * high + high_term
        edge_ref[0, p] = low
        edge_ref[1, p] = high
    row = lax.broadcasted_iota(jnp.int32, (height, members), 0)
    for a in range(span):
        share = jnp.where(row == 0, low[a : a + 1], jnp.where(row == height - 1, high[a : a + 1], 0.0))
        leaving_ref[a] = end_ref[a * height : (a + 1) * height] + share


def edge_march(parity, first, second, low_rate, high_rate, end):
    planes, span, members = first.shape
    vmem = pl.BlockSpec(memory_space=pltpu.VMEM)
    return pl.pallas_call(
        edge_kernel,
        in_specs=[pl.BlockSpec(memory_space=pltpu.SMEM)] + [vmem] * 5,
        out_specs=[vmem] * 3,
        out_shape=[
            jax.ShapeDtypeStruct((2, planes, span, members), jnp.float32),
            jax.ShapeDtypeStruct((2, planes, span, members), jnp.float32),
            jax.ShapeDtypeStruct((span, end.shape[0] // span, members), jnp.float32),
        ],
        compiler_params=params(LIMIT),
        cost_estimate=cost(first.size, 8 * first.size),
    )(parity, first, second, low_rate, high_rate, end)


def observe_kernel(
    rows_ref, obs_ref, weight_ref, picks_ref, share_ref, incoming_ref, edge_ref, out_ref, arriving, halo
):
    planes = edge_ref.shape[1]
    span, height, members = incoming_ref.shape
    count = picks_ref.shape[0]
    for k in range(count):
        p, a, b = place_of(rows_ref[k], (planes, span, height))
        side = jnp.where(b == height - 1, 1, 0)
        at_edge = jnp.where((b == 0) | (b == height - 1), 1.0, 0.0)
        arriving[pl.ds(k, 1), :] = incoming_ref[a, pl.ds(b, 1), :]
        halo[pl.ds(k, 1), :] = at_edge * edge_ref[side, p, pl.ds(a, 1), :]
    forecast = picks_ref[...] - halo[...] - share_ref[...] * arriving[...]
    mean = jnp.sum(forecast, axis=1, keepdims=True) * (1.0 / members)
    anomaly = (forecast - mean).astype(jnp.bfloat16).astype(jnp.float32)
    weight = upright(weight_ref[...])
    observed = weight * anomaly
    misfit = weight * (upright(obs_ref[...]) - mean)
    projection = jnp.sum(observed * misfit, axis=0, keepdims=True)
    one = projection.astype(jnp.bfloat16).astype(jnp.float32)
    two = (projection - one).astype(jnp.bfloat16).astype(jnp.float32)
    three = projection - one - two
    row = lax.broadcasted_iota(jnp.int32, (EXTRA, members), 0)
    pieces = jnp.where(row == 0, one, jnp.where(row == 1, two, jnp.where(row == 2, three, 0.0)))
    out_ref[...] = jnp.concatenate([observed, pieces], axis=0).astype(jnp.bfloat16)


def observe(obs_rows, obs, weight, picks, share, incoming, edge):
    count, members = picks.shape
    vmem = pl.BlockSpec(memory_space=pltpu.VMEM)
    return pl.pallas_call(
        observe_kernel,
        in_specs=[pl.BlockSpec(memory_space=pltpu.SMEM)] + [vmem] * 6,
        out_specs=vmem,
        out_shape=jax.ShapeDtypeStruct((count + EXTRA, members), jnp.bfloat16),
        scratch_shapes=[pltpu.VMEM((count, members), jnp.float32)] * 2,
        compiler_params=params(LIMIT),
        cost_estimate=cost(40 * count * members, 64 * count * members),
    )(obs_rows, obs[None, :], weight[None, :], picks, share, incoming, edge)


def forecast_kernel(start, planes, source_ref, inflow_ref, rate_ref, state_ref, term_ref, *refs):
    out_ref, end_ref = refs[-2:]
    _, span, height, members = source_ref.shape
    cells = group_of(span, height)
    group = cells * height
    mix = stencil(group, height)
    row = lax.broadcasted_iota(jnp.int32, (height, members), 0)
    for p in range(start, start + planes):
        before = state_ref if p == start else end_ref
        for c in range(span // cells):
            term = dot(mix, source_ref[p, c * cells : (c + 1) * cells].reshape(group, members))
            for a in range(c * cells, (c + 1) * cells):
                part = slice(a * height, (a + 1) * height)
                low, high = term_ref[0, p, a : a + 1, :], term_ref[1, p, a : a + 1, :]
                halo = jnp.where(row == 0, low, jnp.where(row == height - 1, high, 0.0))
                deficit = rate_ref[part, p : p + 1] * before[part] + (
                    term[a * height - c * group : (a + 1) * height - c * group] + halo
                )
                end_ref[part] = deficit
                out_ref[p - start, a] = (inflow_ref[p, a].astype(jnp.float32) - deficit).astype(jnp.bfloat16)


def forecasts(source, inflow, rates, state, term, start, stop):
    planes = stop - start
    vmem = pl.BlockSpec(memory_space=pltpu.VMEM)
    size = state.size * planes
    return pl.pallas_call(
        functools.partial(forecast_kernel, start, planes),
        in_specs=[vmem] * 5,
        out_specs=[vmem, vmem],
        out_shape=[
            pltpu.VMEM((planes,) + source.shape[1:], jnp.bfloat16),
            jax.ShapeDtypeStruct(state.shape, jnp.float32),
        ],
        compiler_params=params(LIMIT),
        cost_estimate=cost(4 * size, 6 * size),
    )(source, inflow, rates, state, term)


def halves(x):
    big = x.astype(jnp.bfloat16)
    return big, (x - big.astype(jnp.float32)).astype(jnp.bfloat16)


def fine_dot(a, b, dims=NN):
    a_big, a_small = halves(a)
    b_big, b_small = halves(b)
    return dot(a_big, b_big, dims) + (dot(a_big, b_small, dims) + dot(a_small, b_big, dims))


def update_kernel(picked, gathered_ref, order_ref, *refs):
    forecast_refs = refs[:-5]
    out_ref, gram, factor, results, out_sem = refs[-5:]
    total, members = gathered_ref.shape
    bf16, f32 = jnp.bfloat16, jnp.float32
    row = lax.broadcasted_iota(jnp.int32, (members, members), 0)
    column = lax.broadcasted_iota(jnp.int32, (members, members), 1)
    select = jnp.where(order_ref[...] == row, 1.0, 0.0).astype(bf16)
    select_t = jnp.where(upright(order_ref[...].astype(f32)) == column.astype(f32), 1.0, 0.0).astype(bf16)
    block = picked + EXTRA
    gathered = gathered_ref[...]
    place = lax.broadcasted_iota(jnp.int32, (total, members), 0) % block
    observed = jnp.where(place < picked, gathered.astype(f32), 0.0).astype(bf16)
    ordered_t = dot(select_t, observed, NT).astype(bf16)
    slot = lax.broadcasted_iota(jnp.int32, (16, total), 1) % block
    pieces = dot(jnp.where(slot >= picked, 1.0, 0.0).astype(bf16), gathered)
    piece_one = pieces.astype(bf16)
    piece_two, piece_three = halves(pieces - piece_one.astype(f32))
    projection = dot(piece_one, select) + (dot(piece_two, select) + dot(piece_three, select))
    diagonal = row == column
    full = dot(ordered_t, ordered_t, NT) + jnp.where(diagonal, members - 1.0, 0.0)
    on_diagonal = jnp.where(diagonal, full, 0.0)
    scale_row = lax.rsqrt(jnp.sum(on_diagonal, axis=0, keepdims=True))
    scale_column = lax.rsqrt(jnp.sum(on_diagonal, axis=1, keepdims=True))
    unit = full * scale_row * scale_column
    gram[...] = full
    lower = row > column

    def lower_part(residual):
        return jnp.where(lower, residual, jnp.where(diagonal, 0.5 * residual, 0.0))

    identity = jnp.where(diagonal, 1.0, 0.0)
    factor[...] = identity - jnp.where(lower, unit, 0.0)
    unit_big = unit.astype(bf16)
    for _ in range(2):
        inverse = factor[...]
        inverse_big = inverse.astype(bf16)
        half_way = dot(inverse_big, unit_big).astype(bf16)
        residual = dot(half_way, inverse_big, NT) - identity
        factor[...] = inverse - dot(lower_part(residual).astype(bf16), inverse_big)

    def refine(carried):
        step, _ = carried
        inverse = factor[...]
        residual = fine_dot(fine_dot(inverse, unit), inverse, NT) - identity
        factor[...] = inverse - dot(lower_part(residual).astype(bf16), inverse.astype(bf16))
        return step + 1, jnp.sum(residual * residual)

    def unfinished(carried):
        step, error = carried
        return (step < 8) & (error > 0.04) & (error < 64.0)

    _, error = lax.while_loop(unfinished, refine, (0, jnp.float32(1.0)))
    factor[...] = factor[...] * scale_row

    @pl.when(jnp.logical_not(error <= 0.04))
    def _():
        factor[...] = identity

        def eliminate(k, carry):
            held = gram[...]
            pivot_row = gram[pl.ds(k, 1), :]
            pivot = jnp.sum(jnp.where(column[:1] == k, pivot_row, 0.0), axis=1, keepdims=True)
            pivot_column = jnp.sum(jnp.where(column == k, held, 0.0), axis=1, keepdims=True)
            share = jnp.where(row[:, :1] > k, pivot_column / pivot, 0.0)
            factor[...] = factor[...] - share * factor[pl.ds(k, 1), :]
            gram[...] = held - share * pivot_row
            return carry

        lax.fori_loop(0, members, eliminate, 0)
        pivots = jnp.sum(jnp.where(diagonal, gram[...], 0.0), axis=1, keepdims=True)
        factor[...] = factor[...] * lax.rsqrt(pivots)

    inverse = factor[...]
    coefficients = fine_dot(projection, inverse, NT)
    shift = fine_dot(coefficients, inverse)[:1]
    transform_t = (members - 1.0) ** 0.5 * inverse + shift
    transform_t = transform_t + (1.0 - jnp.sum(transform_t, axis=1, keepdims=True)) * (1.0 / members)
    transform_t = transform_t.astype(bf16)
    weights_t = dot(select, dot(transform_t, select, NT).astype(bf16)).astype(bf16)
    stores = []
    for ref in forecast_refs:
        for p in range(ref.shape[0]):
            at = len(stores)
            forecast = ref[p].reshape(-1, members)
            results[at] = dot(forecast, weights_t, NT).astype(bf16).reshape(ref.shape[1:])
            store = pltpu.make_async_copy(results.at[at], out_ref.at[at], out_sem.at[at])
            store.start()
            stores.append(store)
    for store in stores:
        store.wait()


def updated(picked, gathered, member_order, forecasts, shape):
    planes, span, height, members = shape
    size = planes * span * height * members
    vmem = pl.BlockSpec(memory_space=pltpu.VMEM)
    return pl.pallas_call(
        functools.partial(update_kernel, picked),
        in_specs=[vmem] * (2 + len(forecasts)),
        out_specs=pl.BlockSpec(memory_space=pltpu.HBM),
        out_shape=jax.ShapeDtypeStruct(shape, jnp.bfloat16),
        scratch_shapes=[
            pltpu.VMEM((members, members), jnp.float32),
            pltpu.VMEM((members, members), jnp.float32),
            pltpu.VMEM(shape, jnp.bfloat16),
            pltpu.SemaphoreType.DMA((planes,)),
        ],
        compiler_params=params(LIMIT),
        cost_estimate=cost(4 * size, 5 * size),
    )(gathered, member_order[None, :], *forecasts)


def pairs(count, first):
    low = [(i, i + 1) for i in range(first, count - 1, 2)]
    return low + [(j, i) for i, j in low]


def downstream(value, rate):
    count = lax.axis_size("stream")
    steps = [(i, i + 1) for i in range(count - 1)]
    incoming = lax.ppermute(value, "stream", steps)
    for _ in range(count - 2):
        incoming = lax.ppermute(rate * incoming + value, "stream", steps)
    return incoming


def exchanges(axes):
    for axis in axes:
        count = lax.axis_size(axis)
        if count & (count - 1):
            yield functools.partial(lax.all_gather, axis_name=axis, axis=0, tiled=True)
            continue
        apart = count // 2
        while apart:
            steps = [(i, i ^ apart) for i in range(count)]

            def swap(rows, axis=axis, steps=steps):
                return jnp.concatenate([rows, lax.ppermute(rows, axis, steps)], axis=0)

            yield swap
            apart //= 2


def shards(source, inflow, recovery, obs_rows, obs, observation_weight, member_order):
    planes, span, height, members = source.shape
    levels = lax.axis_size("height")
    parity = (lax.axis_index("height") % 2)[None]
    together = lax.optimization_barrier

    row = border(pltpu.with_memory_space_constraint(source, pltpu.HBM), 1 - parity, False)
    source = pltpu.with_memory_space_constraint(source, pltpu.VMEM)
    inflow = pltpu.with_memory_space_constraint(inflow, pltpu.VMEM)
    first = lax.ppermute(row, "height", pairs(levels, 0))
    middle = (planes + 1) // 2
    held_recovery, row = together((recovery, row))
    state, picks, rates, low_rate, high_rate = march(source, held_recovery, obs_rows, 0, middle)
    high, _ = together((parity, picks))
    row = border(source, high, True)
    row, first = together((row, first))
    second = lax.ppermute(row, "height", pairs(levels, 1))
    held_rates, picks, row = together((rates, picks, row))
    end, picks, share = march(source, held_rates, obs_rows, middle, planes, (state, recovery, picks, inflow))
    end, second = together((end, second))
    term, edge, leaving = edge_march(parity, first, second, low_rate, high_rate, end)
    total = jnp.prod(recovery, axis=0)[..., None] if lax.axis_size("stream") > 2 else None
    incoming = downstream(leaving, total)
    rows = observe(obs_rows, obs, observation_weight, picks, share, incoming, edge)
    state = incoming.reshape(span * height, members)
    cuts = [planes * part // 16 for part in CUTS]
    parts = []
    for swap in exchanges(("height", "span", "stream")):
        swapped = swap(rows)
        if len(cuts) > 1:
            state, rows = together((state, rows))
            forecast, state = forecasts(source, inflow, rates, state, term, cuts[0], cuts[1])
            swapped, state, forecast = together((swapped, state, forecast))
            parts.append(forecast)
            cuts = cuts[1:]
        rows = swapped
    while len(cuts) > 1:
        forecast, state = forecasts(source, inflow, rates, state, term, cuts[0], cuts[1])
        parts.append(forecast)
        cuts = cuts[1:]
    return updated(obs_rows.shape[0], rows, member_order, parts, source.shape)


def solution(mesh):
    placed = (
        P("stream", "span", "height", None),
        P("stream", "span", "height", None),
        P("stream", "span", "height"),
        P(("stream", "span", "height")),
        P(("stream", "span", "height")),
        P(("stream", "span", "height")),
        P(),
    )
    return jax.shard_map(
        shards,
        mesh=mesh,
        in_specs=placed,
        out_specs=P("stream", "span", "height", None),
        check_vma=False,
    )
```

time: 92.3 us -> 83.2 us (0.901)
  Pallas kernels: 72.4 us -> 55.3 us
  waiting for transfers between devices: 2.86 us -> 11.2 us
    pallas_call x8, Pallas kernels: 25.3 us -> 10.5 us  [the longest x2 4.65 us: march(): pl.pallas_call(functools.partial(march_kernel, start, bool(more)), in_spe...]
    ppermute x5, waiting for transfers between devices: 2.2 us -> 8.49 us  [swap(): return jnp.concatenate([rows, lax.ppermute(rows, axis, steps)], axis=0)]
    pallas_call x1, Pallas kernels: 45.7 us -> 43.4 us  [updated(): pl.pallas_call(functools.partial(update_kernel, picked), in_specs=[vmem]...]
    ppermute x5, starting transfers between devices: 9.1 us -> 11.2 us  [swap(): return jnp.concatenate([rows, lax.ppermute(rows, axis, steps)], axis=0)]
    ppermute x2 -> x1, starting transfers between devices: 2.78 us -> 1.32 us  [downstream(): incoming = lax.ppermute(value, 'stream', steps)]
    ppermute x1, waiting for transfers between devices: 0.01 us -> 1.26 us  [shards(): first = lax.ppermute(row, 'height', pairs(levels, 0))]
  transfers between devices with their start and end apart: 9 -> 8, of which waited for: 3 -> 7; matrix products, arithmetic and copies ran while one was open for 1% -> 0% of each run, Pallas kernels for 26% -> 11%
where the time goes in v3:
time: 83.2 us; the launch traced here: 83 us
  Pallas kernels  55.3 us (66%)
  starting transfers between devices  16.3 us (20%)
  waiting for transfers between devices  11.2 us (13%)
    pallas_call x1, Pallas kernels, updated(): pl.pallas_call(functools.partial(update_kernel, picked), in_specs=[vmem]...  43.4 us
    ppermute x5, starting transfers between devices, swap(): return jnp.concatenate([rows, lax.ppermute(rows, axis, steps)], axis=0)  11.2 us
    ppermute x5, waiting for transfers between devices, swap(): return jnp.concatenate([rows, lax.ppermute(rows, axis, steps)], axis=0)  8.49 us
    pallas_call x2, Pallas kernels, march(): pl.pallas_call(functools.partial(march_kernel, start, bool(more)), in_spe...  4.65 us
    pallas_call x4, Pallas kernels, forecasts(): pl.pallas_call(functools.partial(forecast_kernel, start, planes), in_spec...  3.68 us
    ppermute x1, starting transfers between devices, shards(): first = lax.ppermute(row, 'height', pairs(levels, 0))  3.1 us
    pallas_call x2, Pallas kernels, border(): pl.pallas_call(near_border_kernel if near else far_border_kernel, in_spec...  2.19 us
  transfers between devices with their start and end apart: 8, of which 7 were waited for; matrix products, arithmetic and copies ran while one was open for 0% of the time, Pallas kernels for 11%

profile of v3, /device:TPU:0, one launch (start us, length us, event | category | flops | bytes accessed | tf_op | source)
XLA Modules:
  0.0 83.0 jit_solution(6300512171246333792)
XLA Ops:
  0.0 0.0 copy-start
  0.0 0.0 copy-start.2
  0.0 0.0 copy-start.4
  0.0 1.8 %shard_map.73 = bf16[16,16,256]{2,1,0:T(8,128)(2,1)S(1)} custom-call(s32[1]{0:T(128)S(6)} %sub.3.high_ref, bf16[16,16,32,256]{3,2,1,0:T(8,128)(2,1)} %source_ref.11), custom_call_target="tpu_custom_call" | custom-call | flops 1048576000 | bytes 2097152 | tf_op jit(solution)/shard_map/pallas_call | solution.py:77
  1.8 3.1 %collective-permute-start = (bf16[16,16,256]{2,1,0:T(8,128)(2,1)S(1)}, bf16[16,16,256]{2,1,0:T(8,128)(2,1)S(1)}, u32[]{:S(2)}, u32[]{:S(2)}) collective-permute-start(bf16[16,16,256]{2,1,0:T(8,128)(2,1)S(1)} %shard_map.73), channel_id=1, source_target_pairs={{0,1},{2,3},{1,0},{3,2},{4,5},{6,7},{5,4},{7,6},{8,9},{10,11},{9,8... | collective-permute-start | bytes 393224 | tf_op jit(solution)/shard_map/ppermute | solution.py:499
  4.9 0.0 copy-done
  4.9 0.0 copy-done.2
  4.9 0.0 copy-done.4
  4.9 1.8 %shard_map.74 = (f32[512,256]{1,0:T(8,128)S(1)}, f32[32,256]{1,0:T(8,128)S(1)}, f32[512,16]{1,0:T(8,128)S(1)}, f32[16,16]{1,0:T(8,128)S(1)}, f32[16,16]{1,0:T(8,128)S(1)}) custom-call(s32[32]{0:T(128)S(1)} %copy-done.4, bf16[16,16,32,256]{3,2,1,0:T(8,128)(2,1)S(1)} %copy-done, f32[16,16,32]{2,1,0:T(8,128)S(1)} %copy-done.2), custom_call_target="tpu_custom_call" | custom-call | flops 3145728000 | bytes 4194304 | tf_op jit(solution)/shard_map/pallas_call | solution.py:203
  6.7 0.0 copy-start.1
  6.7 0.4 shard_map.75
  7.1 1.3 %collective-permute-done.first_ref = bf16[16,16,256]{2,1,0:T(8,128)(2,1)S(1)} collective-permute-done((bf16[16,16,256]{2,1,0:T(8,128)(2,1)S(1)}, bf16[16,16,256]{2,1,0:T(8,128)(2,1)S(1)}, u32[]{:S(2)}, u32[]{:S(2)}) %collective-permute-start) | collective-permute-done | bytes 131104 | tf_op jit(solution)/shard_map/ppermute | solution.py:499
  8.4 0.7 collective-permute-start.1
  9.1 0.0 copy-done.1
  9.1 0.0 copy-start.5
  9.1 0.0 copy-start.6
  9.1 2.8 %shard_map.76 = (f32[512,256]{1,0:T(8,128)S(1)}, f32[32,256]{1,0:T(8,128)S(1)}, f32[32,256]{1,0:T(8,128)S(1)}) custom-call(s32[32]{0:T(128)S(1)} %copy-done.4, s32[1,32]{1,0:T(1,128)S(1)} %bitcast.8, bf16[16,16,32,256]{3,2,1,0:T(8,128)(2,1)S(1)} %copy-done, f32[512,16]{1,0:T(8,128)S(1)} %get-tuple-element.51.refs_3_.rate_ref, ...), custom_call_target="tpu_custom_call" | custom-call | flops 3145728000 | bytes 4194304 | tf_op jit(solution)/shard_map/pallas_call | solution.py:203
  11.9 0.0 collective-permute-done.1.second_ref
  12.0 0.2 shard_map.77
  12.1 1.3 %collective-permute-start.2 = (f32[16,32,256]{2,1,0:T(8,128)S(1)}, f32[16,32,256]{2,1,0:T(8,128)S(1)}, u32[]{:S(2)}, u32[]{:S(2)}) collective-permute-start(f32[16,32,256]{2,1,0:T(8,128)S(1)} %get-tuple-element.62), channel_id=1, source_target_pairs={{0,16},{1,17},{2,18},{3,19},{4,20},{5,21},{6,22},{7,23},{8,24},{9,... | collective-permute-start | bytes 1572872 | tf_op jit(solution)/shard_map/ppermute | solution.py:467
  13.5 1.5 %collective-permute-done.2.incoming_ref = f32[16,32,256]{2,1,0:T(8,128)S(1)} collective-permute-done((f32[16,32,256]{2,1,0:T(8,128)S(1)}, f32[16,32,256]{2,1,0:T(8,128)S(1)}, u32[]{:S(2)}, u32[]{:S(2)}) %collective-permute-start.2) | collective-permute-done | bytes 524320 | tf_op jit(solution)/shard_map/ppermute | solution.py:467
  15.0 0.0 copy-done.5
  15.0 0.0 copy-done.6
  15.0 1.2 %shard_map.78 = bf16[40,256]{1,0:T(8,128)(2,1)S(1)} custom-call(s32[32]{0:T(128)S(1)} %copy-done.4, f32[1,32]{1,0:T(1,128)S(1)} %bitcast.9, f32[1,32]{1,0:T(1,128)S(1)} %bitcast.10, f32[32,256]{1,0:T(8,128)S(1)} %get-tuple-element.54.picks_ref, f32[32,256]{1,0:T(8,128)S(1)} %get-tuple-element.55.share_ref, ...), custom_call_target="tpu_custom_call" | custom-call | flops 327680000 | bytes 524288 | tf_op jit(solution)/shard_map/pallas_call | solution.py:285
  16.1 6.1 %collective-permute-start.3 = (bf16[40,256]{1,0:T(8,128)(2,1)S(1)}, bf16[40,256]{1,0:T(8,128)(2,1)S(1)}, u32[]{:S(2)}, u32[]{:S(2)}) collective-permute-start(bf16[40,256]{1,0:T(8,128)(2,1)S(1)} %shard_map.78), channel_id=1, source_target_pairs={{0,2},{1,3},{2,0},{3,1},{4,6},{5,7},{6,4},{7,5},{8,10},{9,11},{10,... | collective-permute-start | bytes 61448 | tf_op jit(solution)/shard_map/ppermute | solution.py:484
  22.3 0.6 shard_map.79
  22.9 1.2 %collective-permute-done.3 = bf16[40,256]{1,0:T(8,128)(2,1)S(1)} collective-permute-done((bf16[40,256]{1,0:T(8,128)(2,1)S(1)}, bf16[40,256]{1,0:T(8,128)(2,1)S(1)}, u32[]{:S(2)}, u32[]{:S(2)}) %collective-permute-start.3) | collective-permute-done | bytes 20512 | tf_op jit(solution)/shard_map/ppermute | solution.py:484
  24.0 1.9 %collective-permute-start.4 = (bf16[80,256]{1,0:T(8,128)(2,1)S(1)}, bf16[80,256]{1,0:T(8,128)(2,1)S(1)}, u32[]{:S(2)}, u32[]{:S(2)}) collective-permute-start(bf16[80,256]{1,0:T(8,128)(2,1)S(1)} %pad_maximum_fusion.4), channel_id=1, source_target_pairs={{0,1},{1,0},{2,3},{3,2},{4,5},{5,4},{6,7},{7,6},{8,9},{9,8},{10,11... | collective-permute-start | bytes 122888 | tf_op jit(solution)/shard_map/ppermute | solution.py:484
  25.9 0.7 shard_map.80
  26.7 1.3 %collective-permute-done.4 = bf16[80,256]{1,0:T(8,128)(2,1)S(1)} collective-permute-done((bf16[80,256]{1,0:T(8,128)(2,1)S(1)}, bf16[80,256]{1,0:T(8,128)(2,1)S(1)}, u32[]{:S(2)}, u32[]{:S(2)}) %collective-permute-start.4) | collective-permute-done | bytes 40992 | tf_op jit(solution)/shard_map/ppermute | solution.py:484
  28.0 1.5 %collective-permute-start.5 = (bf16[160,256]{1,0:T(8,128)(2,1)S(1)}, bf16[160,256]{1,0:T(8,128)(2,1)S(1)}, u32[]{:S(2)}, u32[]{:S(2)}) collective-permute-start(bf16[160,256]{1,0:T(8,128)(2,1)S(1)} %pad_maximum_fusion.3), channel_id=1, source_target_pairs={{0,8},{4,12},{8,0},{12,4},{1,9},{5,13},{9,1},{13,5},{2,10},{6,14},... | collective-permute-start | bytes 245768 | tf_op jit(solution)/shard_map/ppermute | solution.py:484
  29.6 0.7 shard_map.81
  30.3 2.2 %collective-permute-done.5 = bf16[160,256]{1,0:T(8,128)(2,1)S(1)} collective-permute-done((bf16[160,256]{1,0:T(8,128)(2,1)S(1)}, bf16[160,256]{1,0:T(8,128)(2,1)S(1)}, u32[]{:S(2)}, u32[]{:S(2)}) %collective-permute-start.5) | collective-permute-done | bytes 81952 | tf_op jit(solution)/shard_map/ppermute | solution.py:484
  32.5 1.6 %collective-permute-start.6 = (bf16[320,256]{1,0:T(8,128)(2,1)S(1)}, bf16[320,256]{1,0:T(8,128)(2,1)S(1)}, u32[]{:S(2)}, u32[]{:S(2)}) collective-permute-start(bf16[320,256]{1,0:T(8,128)(2,1)S(1)} %pad_maximum_fusion.2), channel_id=1, source_target_pairs={{0,4},{4,0},{8,12},{12,8},{1,5},{5,1},{9,13},{13,9},{2,6},{6,2},{1... | collective-permute-start | bytes 491528 | tf_op jit(solution)/shard_map/ppermute | solution.py:484
  34.1 1.6 %shard_map.82 = (bf16[5,16,32,256]{3,2,1,0:T(8,128)(2,1)S(1)}, f32[512,256]{1,0:T(8,128)}) custom-call(bf16[16,16,32,256]{3,2,1,0:T(8,128)(2,1)S(1)} %copy-done, bf16[16,16,32,256]{3,2,1,0:T(8,128)(2,1)S(1)} %copy-done.1, f32[512,16]{1,0:T(8,128)S(1)} %get-tuple-element.51.refs_3_.rate_ref, f32[512,256]{1,0:T(8,128)S(1)} %get-tuple-element.80.state_ref, ...), custom_call_target="tpu_custom_call" | custom-call | flops 2621440000 | bytes 3932160 | tf_op jit(solution)/shard_map/pallas_call | solution.py:322
  35.7 0.0 copy-start.3
  35.7 2.2 %collective-permute-done.6 = bf16[320,256]{1,0:T(8,128)(2,1)S(1)} collective-permute-done((bf16[320,256]{1,0:T(8,128)(2,1)S(1)}, bf16[320,256]{1,0:T(8,128)(2,1)S(1)}, u32[]{:S(2)}, u32[]{:S(2)}) %collective-permute-start.6) | collective-permute-done | bytes 163872 | tf_op jit(solution)/shard_map/ppermute | solution.py:484
  37.9 0.1 collective-permute-start.7
  38.0 1.6 %collective-permute-done.7 = bf16[640,256]{1,0:T(8,128)(2,1)S(1)} collective-permute-done((bf16[640,256]{1,0:T(8,128)(2,1)S(1)}, bf16[640,256]{1,0:T(8,128)(2,1)S(1)}, u32[]{:S(2)}, u32[]{:S(2)}) %collective-permute-start.7) | collective-permute-done | bytes 327712 | tf_op jit(solution)/shard_map/ppermute | solution.py:484
  39.6 0.0 copy-done.3
  39.7 43.4 %shard_map.83 = bf16[16,16,32,256]{3,2,1,0:T(8,128)(2,1)} custom-call(bf16[1280,256]{1,0:T(8,128)(2,1)S(1)} %pad_maximum_fusion.gathered_ref, s32[1,256]{1,0:T(1,128)S(1)} %bitcast.7, bf16[3,16,32,256]{3,2,1,0:T(8,128)(2,1)S(1)} %get-tuple-element.83.refs_0_, bf16[4,16,32,256]{3,2,1,0:T(8,128)(2,1)S(1)} %get-tuple-element.84.refs_1_, ...), custom_call_target="tpu_custom_call" | custom-call | flops 8388608000 | bytes 10485760 | tf_op jit(solution)/shard_map/pallas_call | solution.py:443
  (5 shorter events, 0.1 us)
Async XLA Ops:
  0.0 4.9 %copy-start = (bf16[16,16,32,256]{3,2,1,0:T(8,128)(2,1)S(1)}, bf16[16,16,32,256]{3,2,1,0:T(8,128)(2,1)}, u32[]{:S(2)}) copy-start(bf16[16,16,32,256]{3,2,1,0:T(8,128)(2,1)} %source_ref.11) | copy-start | bytes 12582916
  0.0 4.9 %copy-start.2 = (f32[16,16,32]{2,1,0:T(8,128)S(1)}, f32[16,16,32]{2,1,0:T(8,128)}, u32[]{:S(2)}) copy-start(f32[16,16,32]{2,1,0:T(8,128)} %refs_5_.1) | copy-start | bytes 98308
  0.0 4.9 %copy-start.4 = (s32[32]{0:T(128)S(1)}, s32[32]{0:T(128)}, u32[]{:S(2)}) copy-start(s32[32]{0:T(128)} %rows_ref.1) | copy-start | bytes 388
  1.8 6.6 %collective-permute-start = (bf16[16,16,256]{2,1,0:T(8,128)(2,1)S(1)}, bf16[16,16,256]{2,1,0:T(8,128)(2,1)S(1)}, u32[]{:S(2)}, u32[]{:S(2)}) collective-permute-start(bf16[16,16,256]{2,1,0:T(8,128)(2,1)S(1)} %shard_map.73), channel_id=1, source_target_pairs={{0,1},{2,3},{1,0},{3,2},{4,5},{6,7},{5,4},{7,6},{8,9},{10,11},{9,8... | collective-permute-start | bytes 393224 | tf_op jit(solution)/shard_map/ppermute | solution.py:499
  6.7 2.3 %copy-start.1 = (bf16[16,16,32,256]{3,2,1,0:T(8,128)(2,1)S(1)}, bf16[16,16,32,256]{3,2,1,0:T(8,128)(2,1)}, u32[]{:S(2)}) copy-start(bf16[16,16,32,256]{3,2,1,0:T(8,128)(2,1)} %inflow_ref.7) | copy-start | bytes 12582916
  8.4 3.5 %collective-permute-start.1 = (bf16[16,16,256]{2,1,0:T(8,128)(2,1)S(1)}, bf16[16,16,256]{2,1,0:T(8,128)(2,1)S(1)}, u32[]{:S(2)}, u32[]{:S(2)}) collective-permute-start(bf16[16,16,256]{2,1,0:T(8,128)(2,1)S(1)} %shard_map.75), channel_id=1, source_target_pairs={{1,2},{2,1},{5,6},{6,5},{9,10},{10,9},{13,14},{14,13},{17,18},{18,... | collective-permute-start | bytes 393224 | tf_op jit(solution)/shard_map/ppermute | solution.py:506
  9.1 5.9 %copy-start.5 = (f32[32]{0:T(128)S(1)}, f32[32]{0:T(128)}, u32[]{:S(2)}) copy-start(f32[32]{0:T(128)} %param.11) | copy-start | bytes 388
  9.1 5.9 %copy-start.6 = (f32[32]{0:T(128)S(1)}, f32[32]{0:T(128)}, u32[]{:S(2)}) copy-start(f32[32]{0:T(128)} %param.12) | copy-start | bytes 388
  12.1 2.8 %collective-permute-start.2 = (f32[16,32,256]{2,1,0:T(8,128)S(1)}, f32[16,32,256]{2,1,0:T(8,128)S(1)}, u32[]{:S(2)}, u32[]{:S(2)}) collective-permute-start(f32[16,32,256]{2,1,0:T(8,128)S(1)} %get-tuple-element.62), channel_id=1, source_target_pairs={{0,16},{1,17},{2,18},{3,19},{4,20},{5,21},{6,22},{7,23},{8,24},{9,... | collective-permute-start | bytes 1572872 | tf_op jit(solution)/shard_map/ppermute | solution.py:467
  16.1 7.9 %collective-permute-start.3 = (bf16[40,256]{1,0:T(8,128)(2,1)S(1)}, bf16[40,256]{1,0:T(8,128)(2,1)S(1)}, u32[]{:S(2)}, u32[]{:S(2)}) collective-permute-start(bf16[40,256]{1,0:T(8,128)(2,1)S(1)} %shard_map.78), channel_id=1, source_target_pairs={{0,2},{1,3},{2,0},{3,1},{4,6},{5,7},{6,4},{7,5},{8,10},{9,11},{10,... | collective-permute-start | bytes 61448 | tf_op jit(solution)/shard_map/ppermute | solution.py:484
  24.0 4.0 %collective-permute-start.4 = (bf16[80,256]{1,0:T(8,128)(2,1)S(1)}, bf16[80,256]{1,0:T(8,128)(2,1)S(1)}, u32[]{:S(2)}, u32[]{:S(2)}) collective-permute-start(bf16[80,256]{1,0:T(8,128)(2,1)S(1)} %pad_maximum_fusion.4), channel_id=1, source_target_pairs={{0,1},{1,0},{2,3},{3,2},{4,5},{5,4},{6,7},{7,6},{8,9},{9,8},{10,11... | collective-permute-start | bytes 122888 | tf_op jit(solution)/shard_map/ppermute | solution.py:484
  28.0 4.4 %collective-permute-start.5 = (bf16[160,256]{1,0:T(8,128)(2,1)S(1)}, bf16[160,256]{1,0:T(8,128)(2,1)S(1)}, u32[]{:S(2)}, u32[]{:S(2)}) collective-permute-start(bf16[160,256]{1,0:T(8,128)(2,1)S(1)} %pad_maximum_fusion.3), channel_id=1, source_target_pairs={{0,8},{4,12},{8,0},{12,4},{1,9},{5,13},{9,1},{13,5},{2,10},{6,14},... | collective-permute-start | bytes 245768 | tf_op jit(solution)/shard_map/ppermute | solution.py:484
  32.5 5.4 %collective-permute-start.6 = (bf16[320,256]{1,0:T(8,128)(2,1)S(1)}, bf16[320,256]{1,0:T(8,128)(2,1)S(1)}, u32[]{:S(2)}, u32[]{:S(2)}) collective-permute-start(bf16[320,256]{1,0:T(8,128)(2,1)S(1)} %pad_maximum_fusion.2), channel_id=1, source_target_pairs={{0,4},{4,0},{8,12},{12,8},{1,5},{5,1},{9,13},{13,9},{2,6},{6,2},{1... | collective-permute-start | bytes 491528 | tf_op jit(solution)/shard_map/ppermute | solution.py:484
  35.7 4.0 %copy-start.3 = (s32[256]{0:T(256)S(1)}, s32[256]{0:T(256)}, u32[]{:S(2)}) copy-start(s32[256]{0:T(256)} %param.13) | copy-start | bytes 3076
  37.9 1.7 %collective-permute-start.7 = (bf16[640,256]{1,0:T(8,128)(2,1)S(1)}, bf16[640,256]{1,0:T(8,128)(2,1)S(1)}, u32[]{:S(2)}, u32[]{:S(2)}) collective-permute-start(bf16[640,256]{1,0:T(8,128)(2,1)S(1)} %pad_maximum_fusion.1), channel_id=1, source_target_pairs={{0,16},{16,0},{1,17},{17,1},{2,18},{18,2},{3,19},{19,3},{4,20},{20... | collective-permute-start | bytes 983048 | tf_op jit(solution)/shard_map/ppermute | solution.py:484

commit v4 on v3

--- a/solution.py
+++ b/solution.py
@@ -12,7 +12,7 @@
 NT = (((1,), (1,)), ((), ()))
 NN = (((1,), (0,)), ((), ()))
 LIMIT = 24
-CUTS = (0, 3, 7, 11, 16)
+CUTS = (0, 4, 8, 12, 16)
 EXTRA = 8
 
 
@@ -28,61 +28,38 @@
     return pl.CostEstimate(flops=1000 * elements, bytes_accessed=nbytes, transcendentals=0)
 
 
-def take_border(out_ref, p, block, high):
-    span, rows, _ = block.shape
-    block = block.astype(jnp.float32)
-    low = jnp.concatenate([block[a, :1] for a in range(span)], axis=0)
-    top = jnp.concatenate([block[a, rows - 1 :] for a in range(span)], axis=0)
-    out_ref[p] = jnp.where(high, top, low).astype(jnp.bfloat16)
-
-
-def far_border_kernel(high_ref, source_ref, out_ref, held, sems):
-    planes, span, rows, members = held.shape
-    height = source_ref.shape[2]
-    high = high_ref[0] == 1
-    start = pl.multiple_of(jnp.where(high, height - rows, 0), rows)
-    count = sems.shape[0]
-    step = planes // count
-
-    def fetch(c):
-        part = pl.ds(c * step, step)
-        return pltpu.make_async_copy(
-            source_ref.at[part, :, pl.ds(start, rows), :], held.at[part], sems.at[c]
-        )
-
-    for c in range(count):
-        fetch(c).start()
-    for c in range(count):
-        fetch(c).wait()
-        for p in range(c * step, (c + 1) * step):
-            take_border(out_ref, p, held[p], high)
-
-
-def near_border_kernel(high_ref, source_ref, out_ref):
-    high = high_ref[0] == 1
-    height = source_ref.shape[2]
-    start = pl.multiple_of(jnp.where(high, height - 16, 0), 16)
-    for p in range(source_ref.shape[0]):
-        take_border(out_ref, p, source_ref[p, :, pl.ds(start, 16), :], high)
-
-
-def border(source, high, near):
+def border_kernel(parity_ref, source_ref, held_ref, first_ref, second_ref, sems):
+    planes, span, height, _ = source_ref.shape
+    even = parity_ref[0] == 0
+
+    def fetch(p):
+        return pltpu.make_async_copy(source_ref.at[p], held_ref.at[p], sems.at[p])
+
+    for p in range(planes):
+        fetch(p).start()
+    for p in range(planes):
+        fetch(p).wait()
+        low = held_ref[p, :, :16].astype(jnp.float32)
+        top = held_ref[p, :, height - 16 :].astype(jnp.float32)
+        low = jnp.concatenate([low[a, :1] for a in range(span)], axis=0)
+        top = jnp.concatenate([top[a, 15:] for a in range(span)], axis=0)
+        first_ref[p] = jnp.where(even, top, low).astype(jnp.bfloat16)
+        second_ref[p] = jnp.where(even, low, top).astype(jnp.bfloat16)
+
+
+def border(source, parity):
     planes, span, height, members = source.shape
-    count = 4 if planes % 4 == 0 else 1
     vmem = pl.BlockSpec(memory_space=pltpu.VMEM)
-    scratch = [
-        pltpu.VMEM((planes, span, 16, members), jnp.bfloat16),
-        pltpu.SemaphoreType.DMA((count,)),
-    ]
+    row = jax.ShapeDtypeStruct((planes, span, members), jnp.bfloat16)
     return pl.pallas_call(
-        near_border_kernel if near else far_border_kernel,
-        in_specs=[pl.BlockSpec(memory_space=pltpu.SMEM), vmem if near else pl.BlockSpec(memory_space=pltpu.HBM)],
-        out_specs=vmem,
-        out_shape=jax.ShapeDtypeStruct((planes, span, members), jnp.bfloat16),
-        scratch_shapes=[] if near else scratch,
+        border_kernel,
+        in_specs=[pl.BlockSpec(memory_space=pltpu.SMEM), pl.BlockSpec(memory_space=pltpu.HBM)],
+        out_specs=[vmem] * 3,
+        out_shape=[pltpu.VMEM(source.shape, jnp.bfloat16), row, row],
+        scratch_shapes=[pltpu.SemaphoreType.DMA((planes,))],
         compiler_params=params(LIMIT),
-        cost_estimate=cost(source.size // 2, source.size),
-    )(high, source)
+        cost_estimate=cost(source.size, source.size),
+    )(parity, pltpu.with_memory_space_constraint(source, pltpu.HBM))
 
 
 def place_of(r, shape):
@@ -112,103 +89,76 @@
     return jnp.sum(jnp.where(place == lane, row, jnp.zeros_like(row)), axis=1, keepdims=True)
 
 
-def march_kernel(start, last, *refs):
-    if last:
-        (rows_ref, rows_row_ref, source_ref, rate_ref, state_ref, recovery_ref, picks_in_ref, inflow_ref,
-         end_ref, picks_ref, share_ref, deficits, tiles, through_rows, through) = refs
-    else:
-        (rows_ref, source_ref, recovery_ref, end_ref, picks_ref, rate_ref, low_rate_ref, high_rate_ref,
-         deficits) = refs
-    planes, _, members = deficits.shape
+def march_kernel(
+    rows_ref, rows_row_ref, source_ref, recovery_ref, inflow_ref,
+    end_ref, picks_ref, share_ref, rate_ref, low_rate_ref, high_rate_ref,
+    deficits, tiles, through_rows, through,
+):
     shape = source_ref.shape[:3]
-    _, span, height = shape
-    count = picks_ref.shape[0]
+    planes, span, height = shape
+    count, members = picks_ref.shape
     cells = group_of(span, height)
     group = cells * height
-    if not last:
-        blocks = [jnp.transpose(recovery_ref[:, a, :]) for a in range(span)]
-        for a in range(span):
-            rate_ref[a * height : (a + 1) * height] = blocks[a]
-        low_rate_ref[...] = jnp.concatenate([block[:1] for block in blocks], axis=0)
-        high_rate_ref[...] = jnp.concatenate([block[height - 1 :] for block in blocks], axis=0)
+    blocks = [jnp.transpose(recovery_ref[:, a, :]) for a in range(span)]
+    for a in range(span):
+        rate_ref[a * height : (a + 1) * height] = blocks[a]
+    low_rate_ref[...] = jnp.concatenate([block[:1] for block in blocks], axis=0)
+    high_rate_ref[...] = jnp.concatenate([block[height - 1 :] for block in blocks], axis=0)
     mix = stencil(group, height)
+    product = None
     for p in range(planes):
+        product = recovery_ref[p] if p == 0 else product * recovery_ref[p]
+        through[p] = product
         for c in range(span // cells):
             part = slice(c * group, (c + 1) * group)
-            term = dot(mix, source_ref[start + p, c * cells : (c + 1) * cells].reshape(group, members))
-            if p == 0 and not last:
-                deficits[p, part] = term
-            else:
-                before = state_ref[part] if p == 0 else deficits[p - 1, part]
-                deficits[p, part] = rate_ref[part, start + p : start + p + 1] * before + term
+            term = dot(mix, source_ref[p, c * cells : (c + 1) * cells].reshape(group, members))
+            if p > 0:
+                term = rate_ref[part, p : p + 1] * deficits[p - 1, part] + term
+            deficits[p, part] = term
     end_ref[...] = deficits[planes - 1]
     for k in range(count):
         p, a, b = place_of(rows_ref[k], shape)
-        inside = jnp.where((p >= start) & (p < start + planes), -1.0, 0.0)
-        here = jnp.clip(p - start, 0, planes - 1)
-        picks_ref[pl.ds(k, 1), :] = inside * deficits[here, pl.ds(a * height + b, 1), :]
-    if last:
-        product = None
-        for p in range(shape[0]):
-            product = recovery_ref[p] if p == 0 else product * recovery_ref[p]
-            through[p] = product
-        for k in range(count):
-            p, a, _ = place_of(rows_ref[k], shape)
-            through_rows[pl.ds(k, 1), :] = through[p, pl.ds(a, 1), :]
-        cell = upright(rows_row_ref[...].astype(jnp.float32)).astype(jnp.int32) % height
-        lane = lax.broadcasted_iota(jnp.int32, (count, height), 1)
-        share = jnp.sum(jnp.where(lane == cell, through_rows[...], 0.0), axis=1, keepdims=True)
-        share_ref[...] = jnp.broadcast_to(share, share_ref.shape)
-        for k in range(count):
-            p, a, b = place_of(rows_ref[k], shape)
-            first = pl.multiple_of(b // 16 * 16, 16)
-            tiles[k] = inflow_ref[p, a, pl.ds(first, 16), :].astype(jnp.float32)
-        for k in range(count):
-            _, _, b = place_of(rows_ref[k], shape)
-            picks_ref[pl.ds(k, 1), :] = (
-                picks_ref[pl.ds(k, 1), :] + picks_in_ref[pl.ds(k, 1), :] + tiles[k, pl.ds(b % 16, 1), :]
-            )
-
-
-def march(source, rates, obs_rows, start, stop, more=()):
-    shape = source.shape
-    _, span, height, members = shape
+        first = pl.multiple_of(b // 16 * 16, 16)
+        tiles[k] = inflow_ref[p, a, pl.ds(first, 16), :].astype(jnp.float32)
+        through_rows[pl.ds(k, 1), :] = through[p, pl.ds(a, 1), :]
+    for k in range(count):
+        p, a, b = place_of(rows_ref[k], shape)
+        picks_ref[pl.ds(k, 1), :] = (
+            tiles[k, pl.ds(b % 16, 1), :] - deficits[p, pl.ds(a * height + b, 1), :]
+        )
+    cell = upright(rows_row_ref[...].astype(jnp.float32)).astype(jnp.int32) % height
+    lane = lax.broadcasted_iota(jnp.int32, (count, height), 1)
+    share = jnp.sum(jnp.where(lane == cell, through_rows[...], 0.0), axis=1, keepdims=True)
+    share_ref[...] = jnp.broadcast_to(share, share_ref.shape)
+
+
+def march(source, inflow, recovery, obs_rows):
+    planes, span, height, members = source.shape
     observed = obs_rows.shape[0]
-    planes, cells = stop - start, span * height
-    vmem, smem = pl.BlockSpec(memory_space=pltpu.VMEM), pl.BlockSpec(memory_space=pltpu.SMEM)
-    out_shape = [
-        jax.ShapeDtypeStruct((cells, members), jnp.float32),
-        jax.ShapeDtypeStruct((observed, members), jnp.float32),
-    ]
-    scratch = [pltpu.VMEM((planes, cells, members), jnp.float32)]
-    args = [obs_rows, source, rates]
-    in_specs = [smem, vmem, vmem]
-    if not more:
-        out_shape += [
-            jax.ShapeDtypeStruct((cells, shape[0]), jnp.float32),
-            jax.ShapeDtypeStruct((span, shape[0]), jnp.float32),
-            jax.ShapeDtypeStruct((span, shape[0]), jnp.float32),
-        ]
-    else:
-        state, recovery, picks, inflow = more
-        in_specs = [smem] + [vmem] * 7
-        args = [obs_rows, obs_rows[None, :], source, rates, state, recovery, picks, inflow]
-        out_shape.append(jax.ShapeDtypeStruct((observed, members), jnp.float32))
-        scratch += [
-            pltpu.VMEM((observed, 16, members), jnp.float32),
-            pltpu.VMEM((observed, height), jnp.float32),
-            pltpu.VMEM(shape[:3], jnp.float32),
-        ]
-    size = planes * cells * members
+    cells = span * height
+    f32 = jnp.float32
+    vmem = pl.BlockSpec(memory_space=pltpu.VMEM)
     return pl.pallas_call(
-        functools.partial(march_kernel, start, bool(more)),
-        in_specs=in_specs,
-        out_specs=[vmem] * len(out_shape),
-        out_shape=out_shape,
-        scratch_shapes=scratch,
+        march_kernel,
+        in_specs=[pl.BlockSpec(memory_space=pltpu.SMEM)] + [vmem] * 4,
+        out_specs=[vmem] * 6,
+        out_shape=[
+            jax.ShapeDtypeStruct((cells, members), f32),
+            jax.ShapeDtypeStruct((observed, members), f32),
+            jax.ShapeDtypeStruct((observed, members), f32),
+            jax.ShapeDtypeStruct((cells, planes), f32),
+            jax.ShapeDtypeStruct((span, planes), f32),
+            jax.ShapeDtypeStruct((span, planes), f32),
+        ],
+        scratch_shapes=[
+            pltpu.VMEM((planes, cells, members), f32),
+            pltpu.VMEM((observed, 16, members), f32),
+            pltpu.VMEM((observed, height), f32),
+            pltpu.VMEM((planes, span, height), f32),
+        ],
         compiler_params=params(LIMIT),
-        cost_estimate=cost(3 * size, 4 * size),
-    )(*args)
+        cost_estimate=cost(3 * source.size, 4 * source.size),
+    )(obs_rows, obs_rows[None, :], source, recovery, inflow)
 
 
 def edge_kernel(
@@ -470,21 +420,47 @@
     return incoming
 
 
-def exchanges(axes):
-    for axis in axes:
-        count = lax.axis_size(axis)
-        if count & (count - 1):
-            yield functools.partial(lax.all_gather, axis_name=axis, axis=0, tiled=True)
-            continue
-        apart = count // 2
-        while apart:
-            steps = [(i, i ^ apart) for i in range(count)]
-
-            def swap(rows, axis=axis, steps=steps):
-                return jnp.concatenate([rows, lax.ppermute(rows, axis, steps)], axis=0)
-
-            yield swap
-            apart //= 2
+def rounds():
+    steps = []
+    for axis in ("height", "span"):
+        bits = (lax.axis_size(axis) - 1).bit_length()
+        steps.append([(axis, 1 << bit) for bit in reversed(range(bits))])
+    mixed = []
+    while steps[0] or steps[1]:
+        pair = [axis.pop(0) for axis in steps if axis]
+        mixed += [(pair[0], pair[-1]), (pair[-1], pair[0])][: len(pair)]
+    return mixed
+
+
+def exchanges():
+    axes = ("stream", "span", "height")
+    sizes = [lax.axis_size(axis) for axis in axes]
+    if any(size & (size - 1) for size in sizes):
+        yield functools.partial(lax.all_gather, axis_name=axes, axis=0, tiled=True)
+        return
+
+    def flat(place):
+        return (place["stream"] * sizes[1] + place["span"]) * sizes[2] + place["height"]
+
+    places = [
+        {"stream": i // (sizes[1] * sizes[2]), "span": i // sizes[2] % sizes[1], "height": i % sizes[2]}
+        for i in range(sizes[0] * sizes[1] * sizes[2])
+    ]
+    steps = rounds()
+    apart = sizes[0] // 2
+    while apart:
+        steps.append((("stream", apart), ("stream", apart)))
+        apart //= 2
+    for step in steps:
+        moves = []
+        for place in places:
+            axis, bit = step[place["stream"] % 2]
+            moves.append((flat(place), flat(place | {axis: place[axis] ^ bit})))
+
+        def swap(rows, moves=moves):
+            return jnp.concatenate([rows, lax.ppermute(rows, axes, moves)], axis=0)
+
+        yield swap
 
 
 def shards(source, inflow, recovery, obs_rows, obs, observation_weight, member_order):
@@ -493,20 +469,12 @@
     parity = (lax.axis_index("height") % 2)[None]
     together = lax.optimization_barrier
 
-    row = border(pltpu.with_memory_space_constraint(source, pltpu.HBM), 1 - parity, False)
-    source = pltpu.with_memory_space_constraint(source, pltpu.VMEM)
+    source, first, second = border(source, parity)
     inflow = pltpu.with_memory_space_constraint(inflow, pltpu.VMEM)
-    first = lax.ppermute(row, "height", pairs(levels, 0))
-    middle = (planes + 1) // 2
-    held_recovery, row = together((recovery, row))
-    state, picks, rates, low_rate, high_rate = march(source, held_recovery, obs_rows, 0, middle)
-    high, _ = together((parity, picks))
-    row = border(source, high, True)
-    row, first = together((row, first))
-    second = lax.ppermute(row, "height", pairs(levels, 1))
-    held_rates, picks, row = together((rates, picks, row))
-    end, picks, share = march(source, held_rates, obs_rows, middle, planes, (state, recovery, picks, inflow))
-    end, second = together((end, second))
+    first = lax.ppermute(first, "height", pairs(levels, 0))
+    second = lax.ppermute(second, "height", pairs(levels, 1))
+    end, picks, share, rates, low_rate, high_rate = march(source, inflow, recovery, obs_rows)
+    end, first, second = together((end, first, second))
     term, edge, leaving = edge_march(parity, first, second, low_rate, high_rate, end)
     total = jnp.prod(recovery, axis=0)[..., None] if lax.axis_size("stream") > 2 else None
     incoming = downstream(leaving, total)
@@ -514,7 +482,7 @@
     state = incoming.reshape(span * height, members)
     cuts = [planes * part // 16 for part in CUTS]
     parts = []
-    for swap in exchanges(("height", "span", "stream")):
+    for swap in exchanges():
         swapped = swap(rows)
         if len(cuts) > 1:
             state, rows = together((state, rows))

time: 83.2 us -> 80.3 us (0.965)
  Pallas kernels: 55.3 us -> 53.9 us
    pallas_call x4 -> x2, Pallas kernels: 6.84 us -> 5.55 us  [the longest x1 3.1 us: march(): pl.pallas_call(march_kernel, in_specs=[pl.BlockSpec(memory_space=pltpu.SM...]
    ppermute x7, waiting for transfers between devices: 9.75 us -> 8.91 us  [the longest x5 8.9 us: swap(): return jnp.concatenate([rows, lax.ppermute(rows, axes, moves)], axis=0)]
    ppermute x7, starting transfers between devices: 14.9 us -> 14.1 us  [the longest x5 10.4 us: swap(): return jnp.concatenate([rows, lax.ppermute(rows, axes, moves)], axis=0)]
  transfers between devices with their start and end apart: 8 -> 8, of which waited for: 7 -> 6; matrix products, arithmetic and copies ran while one was open for 0% -> 0% of each run, Pallas kernels for 11% -> 8%
where the time goes in v4:
time: 80.3 us; the launch traced here: 80.2 us
  Pallas kernels  53.9 us (67%)
  starting transfers between devices  15.6 us (19%)
  waiting for transfers between devices  10.4 us (13%)
    pallas_call x1, Pallas kernels, updated(): pl.pallas_call(functools.partial(update_kernel, picked), in_specs=[vmem]...  43.4 us
    ppermute x5, starting transfers between devices, swap(): return jnp.concatenate([rows, lax.ppermute(rows, axes, moves)], axis=0)  10.4 us
    ppermute x5, waiting for transfers between devices, swap(): return jnp.concatenate([rows, lax.ppermute(rows, axes, moves)], axis=0)  8.9 us
    pallas_call x4, Pallas kernels, forecasts(): pl.pallas_call(functools.partial(forecast_kernel, start, planes), in_spec...  3.61 us
    pallas_call x1, Pallas kernels, march(): pl.pallas_call(march_kernel, in_specs=[pl.BlockSpec(memory_space=pltpu.SM...  3.1 us
    ppermute x1, starting transfers between devices, shards(): first = lax.ppermute(first, 'height', pairs(levels, 0))  3.09 us
    pallas_call x1, Pallas kernels, border(): pl.pallas_call(border_kernel, in_specs=[pl.BlockSpec(memory_space=pltpu.S...  2.44 us
  transfers between devices with their start and end apart: 8, of which 6 were waited for; matrix products, arithmetic and copies ran while one was open for 0% of the time, Pallas kernels for 8%

profile of v4, /device:TPU:0, one launch (start us, length us, event | category | flops | bytes accessed | tf_op | source)
XLA Modules:
  0.0 80.2 jit_solution(7626910071426674435)
XLA Ops:
  0.0 0.0 copy-start.3
  0.0 0.0 copy-start.1
  0.0 0.0 copy-start
  0.0 2.4 %shard_map.73 = (bf16[16,16,32,256]{3,2,1,0:T(8,128)(2,1)S(1)}, bf16[16,16,256]{2,1,0:T(8,128)(2,1)S(1)}, bf16[16,16,256]{2,1,0:T(8,128)(2,1)S(1)}) custom-call(s32[1]{0:T(128)} %bitcast.3.parity_ref, bf16[16,16,32,256]{3,2,1,0:T(8,128)(2,1)} %source_ref.1), custom_call_target="tpu_custom_call" | custom-call | flops 2097152000 | bytes 2097152 | tf_op jit(solution)/shard_map/pallas_call | solution.py:54
  2.5 3.1 %collective-permute-start = (bf16[16,16,256]{2,1,0:T(8,128)(2,1)S(1)}, bf16[16,16,256]{2,1,0:T(8,128)(2,1)S(1)}, u32[]{:S(2)}, u32[]{:S(2)}) collective-permute-start(bf16[16,16,256]{2,1,0:T(8,128)(2,1)S(1)} %get-tuple-element.46), channel_id=1, source_target_pairs={{0,1},{2,3},{1,0},{3,2},{4,5},{6,7},{5,4},{7,6},{8,9},{10,11},{9,8... | collective-permute-start | bytes 393224 | tf_op jit(solution)/shard_map/ppermute | solution.py:474
  5.6 0.7 collective-permute-start.1
  6.2 0.0 copy-done.3
  6.2 0.0 copy-done.1
  6.2 0.0 copy-done
  6.2 0.0 copy-start.4
  6.3 0.0 copy-start.5
  6.3 3.1 %shard_map.74 = (f32[512,256]{1,0:T(8,128)S(1)}, f32[32,256]{1,0:T(8,128)S(1)}, f32[32,256]{1,0:T(8,128)S(1)}, f32[512,16]{1,0:T(8,128)S(1)}, f32[16,16]{1,0:T(8,128)S(1)}, /*index=5*/f32[16,16]{1,0:T(8,128)S(1)}) custom-call(s32[32]{0:T(128)S(1)} %copy-done.3, s32[1,32]{1,0:T(1,128)S(1)} %bitcast.8, ...), custom_call_target="tpu_custom_call" | custom-call | flops 6291456000 | bytes 8388608 | tf_op jit(solution)/shard_map/pallas_call | solution.py:141
  9.4 0.0 collective-permute-done.first_ref
  9.4 0.0 collective-permute-done.1.second_ref
  9.4 0.2 shard_map.75
  9.6 1.5 %collective-permute-start.2 = (f32[16,32,256]{2,1,0:T(8,128)S(1)}, f32[16,32,256]{2,1,0:T(8,128)S(1)}, u32[]{:S(2)}, u32[]{:S(2)}) collective-permute-start(f32[16,32,256]{2,1,0:T(8,128)S(1)} %get-tuple-element.53), channel_id=1, source_target_pairs={{0,16},{1,17},{2,18},{3,19},{4,20},{5,21},{6,22},{7,23},{8,24},{9,... | collective-permute-start | bytes 1572872 | tf_op jit(solution)/shard_map/ppermute | solution.py:417
  11.1 1.5 %collective-permute-done.2.incoming_ref = f32[16,32,256]{2,1,0:T(8,128)S(1)} collective-permute-done((f32[16,32,256]{2,1,0:T(8,128)S(1)}, f32[16,32,256]{2,1,0:T(8,128)S(1)}, u32[]{:S(2)}, u32[]{:S(2)}) %collective-permute-start.2) | collective-permute-done | bytes 524320 | tf_op jit(solution)/shard_map/ppermute | solution.py:417
  12.6 0.0 copy-done.4
  12.6 0.0 copy-done.5
  12.6 1.2 %shard_map.76 = bf16[40,256]{1,0:T(8,128)(2,1)S(1)} custom-call(s32[32]{0:T(128)S(1)} %copy-done.3, f32[1,32]{1,0:T(1,128)S(1)} %bitcast.9, f32[1,32]{1,0:T(1,128)S(1)} %bitcast.10, f32[32,256]{1,0:T(8,128)S(1)} %get-tuple-element.43.picks_ref, f32[32,256]{1,0:T(8,128)S(1)} %get-tuple-element.44.share_ref, ...), custom_call_target="tpu_custom_call" | custom-call | flops 327680000 | bytes 524288 | tf_op jit(solution)/shard_map/pallas_call | solution.py:235
  13.8 5.5 %collective-permute-start.3 = (bf16[40,256]{1,0:T(8,128)(2,1)S(1)}, bf16[40,256]{1,0:T(8,128)(2,1)S(1)}, u32[]{:S(2)}, u32[]{:S(2)}) collective-permute-start(bf16[40,256]{1,0:T(8,128)(2,1)S(1)} %shard_map.76), channel_id=1, source_target_pairs={{0,2},{1,3},{2,0},{3,1},{4,6},{5,7},{6,4},{7,5},{8,10},{9,11},{10,... | collective-permute-start | bytes 61448 | tf_op jit(solution)/shard_map/ppermute | solution.py:461
  19.2 0.7 shard_map.77
  20.0 1.1 %collective-permute-done.3 = bf16[40,256]{1,0:T(8,128)(2,1)S(1)} collective-permute-done((bf16[40,256]{1,0:T(8,128)(2,1)S(1)}, bf16[40,256]{1,0:T(8,128)(2,1)S(1)}, u32[]{:S(2)}, u32[]{:S(2)}) %collective-permute-start.3) | collective-permute-done | bytes 20512 | tf_op jit(solution)/shard_map/ppermute | solution.py:461
  21.0 1.5 %collective-permute-start.4 = (bf16[80,256]{1,0:T(8,128)(2,1)S(1)}, bf16[80,256]{1,0:T(8,128)(2,1)S(1)}, u32[]{:S(2)}, u32[]{:S(2)}) collective-permute-start(bf16[80,256]{1,0:T(8,128)(2,1)S(1)} %pad_maximum_fusion.4), channel_id=1, source_target_pairs={{0,8},{1,9},{2,10},{3,11},{4,12},{5,13},{6,14},{7,15},{8,0},{9,1},... | collective-permute-start | bytes 122888 | tf_op jit(solution)/shard_map/ppermute | solution.py:461
  22.5 0.7 shard_map.78
  23.2 1.8 %collective-permute-done.4 = bf16[80,256]{1,0:T(8,128)(2,1)S(1)} collective-permute-done((bf16[80,256]{1,0:T(8,128)(2,1)S(1)}, bf16[80,256]{1,0:T(8,128)(2,1)S(1)}, u32[]{:S(2)}, u32[]{:S(2)}) %collective-permute-start.4) | collective-permute-done | bytes 40992 | tf_op jit(solution)/shard_map/ppermute | solution.py:461
  25.0 1.7 %collective-permute-start.5 = (bf16[160,256]{1,0:T(8,128)(2,1)S(1)}, bf16[160,256]{1,0:T(8,128)(2,1)S(1)}, u32[]{:S(2)}, u32[]{:S(2)}) collective-permute-start(bf16[160,256]{1,0:T(8,128)(2,1)S(1)} %pad_maximum_fusion.3), channel_id=1, source_target_pairs={{0,1},{1,0},{2,3},{3,2},{4,5},{5,4},{6,7},{7,6},{8,9},{9,8},{10,11... | collective-permute-start | bytes 245768 | tf_op jit(solution)/shard_map/ppermute | solution.py:461
  26.8 0.7 shard_map.79
  27.5 2.1 %collective-permute-done.5 = bf16[160,256]{1,0:T(8,128)(2,1)S(1)} collective-permute-done((bf16[160,256]{1,0:T(8,128)(2,1)S(1)}, bf16[160,256]{1,0:T(8,128)(2,1)S(1)}, u32[]{:S(2)}, u32[]{:S(2)}) %collective-permute-start.5) | collective-permute-done | bytes 81952 | tf_op jit(solution)/shard_map/ppermute | solution.py:461
  29.6 0.0 copy-start.2
  29.6 1.6 %collective-permute-start.6 = (bf16[320,256]{1,0:T(8,128)(2,1)S(1)}, bf16[320,256]{1,0:T(8,128)(2,1)S(1)}, u32[]{:S(2)}, u32[]{:S(2)}) collective-permute-start(bf16[320,256]{1,0:T(8,128)(2,1)S(1)} %pad_maximum_fusion.2), channel_id=1, source_target_pairs={{0,4},{1,5},{2,6},{3,7},{4,0},{5,1},{6,2},{7,3},{8,12},{9,13},{10,... | collective-permute-start | bytes 491528 | tf_op jit(solution)/shard_map/ppermute | solution.py:461
  31.2 1.5 %shard_map.80 = (bf16[4,16,32,256]{3,2,1,0:T(8,128)(2,1)S(1)}, f32[512,256]{1,0:T(8,128)}) custom-call(bf16[16,16,32,256]{3,2,1,0:T(8,128)(2,1)S(1)} %get-tuple-element.42.source_ref, bf16[16,16,32,256]{3,2,1,0:T(8,128)(2,1)S(1)} %copy-done, f32[512,16]{1,0:T(8,128)S(1)} %get-tuple-element.55.rate_ref, f32[512,256]{1,0:T(8,128)S(1)} %get-tuple-element.72.state_ref, ...), custom_call_target="tpu_custom_call" | custom-call | flops 2097152000 | bytes 3145728 | tf_op jit(solution)/shard_map/pallas_call | solution.py:272
  32.7 2.3 %collective-permute-done.6 = bf16[320,256]{1,0:T(8,128)(2,1)S(1)} collective-permute-done((bf16[320,256]{1,0:T(8,128)(2,1)S(1)}, bf16[320,256]{1,0:T(8,128)(2,1)S(1)}, u32[]{:S(2)}, u32[]{:S(2)}) %collective-permute-start.6) | collective-permute-done | bytes 163872 | tf_op jit(solution)/shard_map/ppermute | solution.py:461
  35.0 0.1 collective-permute-start.7
  35.1 1.6 %collective-permute-done.7 = bf16[640,256]{1,0:T(8,128)(2,1)S(1)} collective-permute-done((bf16[640,256]{1,0:T(8,128)(2,1)S(1)}, bf16[640,256]{1,0:T(8,128)(2,1)S(1)}, u32[]{:S(2)}, u32[]{:S(2)}) %collective-permute-start.7) | collective-permute-done | bytes 327712 | tf_op jit(solution)/shard_map/ppermute | solution.py:461
  36.8 0.0 copy-done.2
  36.8 43.4 %shard_map.81 = bf16[16,16,32,256]{3,2,1,0:T(8,128)(2,1)} custom-call(bf16[1280,256]{1,0:T(8,128)(2,1)S(1)} %pad_maximum_fusion.gathered_ref, s32[1,256]{1,0:T(1,128)S(1)} %bitcast.7, bf16[4,16,32,256]{3,2,1,0:T(8,128)(2,1)S(1)} %get-tuple-element.75.refs_0_, bf16[4,16,32,256]{3,2,1,0:T(8,128)(2,1)S(1)} %get-tuple-element.76.refs_1_, ...), custom_call_target="tpu_custom_call" | custom-call | flops 8388608000 | bytes 10485760 | tf_op jit(solution)/shard_map/pallas_call | solution.py:393
  (5 shorter events, 0.1 us)
Async XLA Ops:
  0.0 6.2 %copy-start.3 = (s32[32]{0:T(128)S(1)}, s32[32]{0:T(128)}, u32[]{:S(2)}) copy-start(s32[32]{0:T(128)} %rows_ref.3) | copy-start | bytes 388
  0.0 6.2 %copy-start.1 = (f32[16,16,32]{2,1,0:T(8,128)S(1)}, f32[16,16,32]{2,1,0:T(8,128)}, u32[]{:S(2)}) copy-start(f32[16,16,32]{2,1,0:T(8,128)} %recovery_ref.1) | copy-start | bytes 98308
  0.0 6.2 %copy-start = (bf16[16,16,32,256]{3,2,1,0:T(8,128)(2,1)S(1)}, bf16[16,16,32,256]{3,2,1,0:T(8,128)(2,1)}, u32[]{:S(2)}) copy-start(bf16[16,16,32,256]{3,2,1,0:T(8,128)(2,1)} %inflow_ref.9) | copy-start | bytes 12582916
  2.5 6.9 %collective-permute-start = (bf16[16,16,256]{2,1,0:T(8,128)(2,1)S(1)}, bf16[16,16,256]{2,1,0:T(8,128)(2,1)S(1)}, u32[]{:S(2)}, u32[]{:S(2)}) collective-permute-start(bf16[16,16,256]{2,1,0:T(8,128)(2,1)S(1)} %get-tuple-element.46), channel_id=1, source_target_pairs={{0,1},{2,3},{1,0},{3,2},{4,5},{6,7},{5,4},{7,6},{8,9},{10,11},{9,8... | collective-permute-start | bytes 393224 | tf_op jit(solution)/shard_map/ppermute | solution.py:474
  5.6 3.8 %collective-permute-start.1 = (bf16[16,16,256]{2,1,0:T(8,128)(2,1)S(1)}, bf16[16,16,256]{2,1,0:T(8,128)(2,1)S(1)}, u32[]{:S(2)}, u32[]{:S(2)}) collective-permute-start(bf16[16,16,256]{2,1,0:T(8,128)(2,1)S(1)} %get-tuple-element.47), channel_id=1, source_target_pairs={{1,2},{2,1},{5,6},{6,5},{9,10},{10,9},{13,14},{14,13},{17,18},{18,... | collective-permute-start | bytes 393224 | tf_op jit(solution)/shard_map/ppermute | solution.py:475
  6.2 6.3 %copy-start.4 = (f32[32]{0:T(128)S(1)}, f32[32]{0:T(128)}, u32[]{:S(2)}) copy-start(f32[32]{0:T(128)} %param.11) | copy-start | bytes 388
  6.3 6.3 %copy-start.5 = (f32[32]{0:T(128)S(1)}, f32[32]{0:T(128)}, u32[]{:S(2)}) copy-start(f32[32]{0:T(128)} %param.12) | copy-start | bytes 388
  9.6 3.0 %collective-permute-start.2 = (f32[16,32,256]{2,1,0:T(8,128)S(1)}, f32[16,32,256]{2,1,0:T(8,128)S(1)}, u32[]{:S(2)}, u32[]{:S(2)}) collective-permute-start(f32[16,32,256]{2,1,0:T(8,128)S(1)} %get-tuple-element.53), channel_id=1, source_target_pairs={{0,16},{1,17},{2,18},{3,19},{4,20},{5,21},{6,22},{7,23},{8,24},{9,... | collective-permute-start | bytes 1572872 | tf_op jit(solution)/shard_map/ppermute | solution.py:417
  13.8 7.2 %collective-permute-start.3 = (bf16[40,256]{1,0:T(8,128)(2,1)S(1)}, bf16[40,256]{1,0:T(8,128)(2,1)S(1)}, u32[]{:S(2)}, u32[]{:S(2)}) collective-permute-start(bf16[40,256]{1,0:T(8,128)(2,1)S(1)} %shard_map.76), channel_id=1, source_target_pairs={{0,2},{1,3},{2,0},{3,1},{4,6},{5,7},{6,4},{7,5},{8,10},{9,11},{10,... | collective-permute-start | bytes 61448 | tf_op jit(solution)/shard_map/ppermute | solution.py:461
  21.0 4.0 %collective-permute-start.4 = (bf16[80,256]{1,0:T(8,128)(2,1)S(1)}, bf16[80,256]{1,0:T(8,128)(2,1)S(1)}, u32[]{:S(2)}, u32[]{:S(2)}) collective-permute-start(bf16[80,256]{1,0:T(8,128)(2,1)S(1)} %pad_maximum_fusion.4), channel_id=1, source_target_pairs={{0,8},{1,9},{2,10},{3,11},{4,12},{5,13},{6,14},{7,15},{8,0},{9,1},... | collective-permute-start | bytes 122888 | tf_op jit(solution)/shard_map/ppermute | solution.py:461
  25.0 4.6 %collective-permute-start.5 = (bf16[160,256]{1,0:T(8,128)(2,1)S(1)}, bf16[160,256]{1,0:T(8,128)(2,1)S(1)}, u32[]{:S(2)}, u32[]{:S(2)}) collective-permute-start(bf16[160,256]{1,0:T(8,128)(2,1)S(1)} %pad_maximum_fusion.3), channel_id=1, source_target_pairs={{0,1},{1,0},{2,3},{3,2},{4,5},{5,4},{6,7},{7,6},{8,9},{9,8},{10,11... | collective-permute-start | bytes 245768 | tf_op jit(solution)/shard_map/ppermute | solution.py:461
  29.6 7.2 %copy-start.2 = (s32[256]{0:T(256)S(1)}, s32[256]{0:T(256)}, u32[]{:S(2)}) copy-start(s32[256]{0:T(256)} %param.13) | copy-start | bytes 3076
  29.6 5.4 %collective-permute-start.6 = (bf16[320,256]{1,0:T(8,128)(2,1)S(1)}, bf16[320,256]{1,0:T(8,128)(2,1)S(1)}, u32[]{:S(2)}, u32[]{:S(2)}) collective-permute-start(bf16[320,256]{1,0:T(8,128)(2,1)S(1)} %pad_maximum_fusion.2), channel_id=1, source_target_pairs={{0,4},{1,5},{2,6},{3,7},{4,0},{5,1},{6,2},{7,3},{8,12},{9,13},{10,... | collective-permute-start | bytes 491528 | tf_op jit(solution)/shard_map/ppermute | solution.py:461
  35.0 1.7 %collective-permute-start.7 = (bf16[640,256]{1,0:T(8,128)(2,1)S(1)}, bf16[640,256]{1,0:T(8,128)(2,1)S(1)}, u32[]{:S(2)}, u32[]{:S(2)}) collective-permute-start(bf16[640,256]{1,0:T(8,128)(2,1)S(1)} %pad_maximum_fusion.1), channel_id=1, source_target_pairs={{0,16},{1,17},{2,18},{3,19},{4,20},{5,21},{6,22},{7,23},{8,24},{9,... | collective-permute-start | bytes 983048 | tf_op jit(solution)/shard_map/ppermute | solution.py:461

commit v5 on v4

--- a/solution.py
+++ b/solution.py
@@ -13,6 +13,7 @@
 NN = (((1,), (0,)), ((), ()))
 LIMIT = 24
 CUTS = (0, 4, 8, 12, 16)
+AXES = ("stream", "span", "height")
 EXTRA = 8
 
 
@@ -202,24 +203,42 @@
     )(parity, first, second, low_rate, high_rate, end)
 
 
-def observe_kernel(
-    rows_ref, obs_ref, weight_ref, picks_ref, share_ref, incoming_ref, edge_ref, out_ref, arriving, halo
-):
-    planes = edge_ref.shape[1]
+def prepare_kernel(height, rows_ref, edge_ref, picks_ref, obs_ref, weight_ref, out_ref, obs_out_ref, weight_out_ref):
+    _, planes, span, _ = edge_ref.shape
+    for k in range(picks_ref.shape[0]):
+        p, a, b = place_of(rows_ref[k], (planes, span, height))
+        side = jnp.where(b == height - 1, 1, 0)
+        at_edge = jnp.where((b == 0) | (b == height - 1), 1.0, 0.0)
+        out_ref[pl.ds(k, 1), :] = picks_ref[pl.ds(k, 1), :] - at_edge * edge_ref[side, p, pl.ds(a, 1), :]
+    obs_out_ref[...] = jnp.broadcast_to(upright(obs_ref[...]), obs_out_ref.shape)
+    weight_out_ref[...] = jnp.broadcast_to(upright(weight_ref[...]), weight_out_ref.shape)
+
+
+def prepare(obs_rows, obs, weight, picks, edge, height):
+    vmem = pl.BlockSpec(memory_space=pltpu.VMEM)
+    out = jax.ShapeDtypeStruct(picks.shape, jnp.float32)
+    return pl.pallas_call(
+        functools.partial(prepare_kernel, height),
+        in_specs=[pl.BlockSpec(memory_space=pltpu.SMEM)] + [vmem] * 4,
+        out_specs=[vmem] * 3,
+        out_shape=[out] * 3,
+        compiler_params=params(LIMIT),
+        cost_estimate=cost(100 * picks.size, 64 * picks.size),
+    )(obs_rows, edge, picks, obs[None, :], weight[None, :])
+
+
+def observe_kernel(rows_ref, obs_ref, weight_ref, picks_ref, share_ref, incoming_ref, out_ref, arriving):
     span, height, members = incoming_ref.shape
     count = picks_ref.shape[0]
     for k in range(count):
-        p, a, b = place_of(rows_ref[k], (planes, span, height))
-        side = jnp.where(b == height - 1, 1, 0)
-        at_edge = jnp.where((b == 0) | (b == height - 1), 1.0, 0.0)
+        _, a, b = place_of(rows_ref[k], (0, span, height))
         arriving[pl.ds(k, 1), :] = incoming_ref[a, pl.ds(b, 1), :]
-        halo[pl.ds(k, 1), :] = at_edge * edge_ref[side, p, pl.ds(a, 1), :]
-    forecast = picks_ref[...] - halo[...] - share_ref[...] * arriving[...]
+    forecast = picks_ref[...] - share_ref[...] * arriving[...]
     mean = jnp.sum(forecast, axis=1, keepdims=True) * (1.0 / members)
     anomaly = (forecast - mean).astype(jnp.bfloat16).astype(jnp.float32)
-    weight = upright(weight_ref[...])
+    weight = weight_ref[...]
     observed = weight * anomaly
-    misfit = weight * (upright(obs_ref[...]) - mean)
+    misfit = weight * (obs_ref[...] - mean)
     projection = jnp.sum(observed * misfit, axis=0, keepdims=True)
     one = projection.astype(jnp.bfloat16).astype(jnp.float32)
     two = (projection - one).astype(jnp.bfloat16).astype(jnp.float32)
@@ -229,22 +248,22 @@
     out_ref[...] = jnp.concatenate([observed, pieces], axis=0).astype(jnp.bfloat16)
 
 
-def observe(obs_rows, obs, weight, picks, share, incoming, edge):
+def observe(obs_rows, obs, weight, picks, share, incoming):
     count, members = picks.shape
     vmem = pl.BlockSpec(memory_space=pltpu.VMEM)
     return pl.pallas_call(
         observe_kernel,
-        in_specs=[pl.BlockSpec(memory_space=pltpu.SMEM)] + [vmem] * 6,
+        in_specs=[pl.BlockSpec(memory_space=pltpu.SMEM)] + [vmem] * 5,
         out_specs=vmem,
         out_shape=jax.ShapeDtypeStruct((count + EXTRA, members), jnp.bfloat16),
-        scratch_shapes=[pltpu.VMEM((count, members), jnp.float32)] * 2,
+        scratch_shapes=[pltpu.VMEM((count, members), jnp.float32)],
         compiler_params=params(LIMIT),
         cost_estimate=cost(40 * count * members, 64 * count * members),
-    )(obs_rows, obs[None, :], weight[None, :], picks, share, incoming, edge)
+    )(obs_rows, obs, weight, picks, share, incoming)
 
 
 def forecast_kernel(start, planes, source_ref, inflow_ref, rate_ref, state_ref, term_ref, *refs):
-    out_ref, end_ref = refs[-2:]
+    out_ref, end_ref = refs[:2]
     _, span, height, members = source_ref.shape
     cells = group_of(span, height)
     group = cells * height
@@ -275,7 +294,7 @@
         out_specs=[vmem, vmem],
         out_shape=[
             pltpu.VMEM((planes,) + source.shape[1:], jnp.bfloat16),
-            jax.ShapeDtypeStruct(state.shape, jnp.float32),
+            pltpu.VMEM(state.shape, jnp.float32),
         ],
         compiler_params=params(LIMIT),
         cost_estimate=cost(4 * size, 6 * size),
@@ -293,92 +312,146 @@
     return dot(a_big, b_big, dims) + (dot(a_big, b_small, dims) + dot(a_small, b_big, dims))
 
 
-def update_kernel(picked, gathered_ref, order_ref, *refs):
-    forecast_refs = refs[:-5]
-    out_ref, gram, factor, results, out_sem = refs[-5:]
-    total, members = gathered_ref.shape
+def split_rows(picked, rows):
+    total, members = rows.shape
+    block = picked + EXTRA
+    place = lax.broadcasted_iota(jnp.int32, (total, members), 0) % block
+    observed = jnp.where(place < picked, rows.astype(jnp.float32), 0.0).astype(jnp.bfloat16)
+    slot = lax.broadcasted_iota(jnp.int32, (16, total), 1) % block
+    return observed, dot(jnp.where(slot >= picked, 1.0, 0.0).astype(jnp.bfloat16), rows)
+
+
+def gram_kernel(picked, rows_ref, order_ref, gram_ref, pieces_ref, select_ref, select_t_ref):
+    members = rows_ref.shape[1]
     bf16, f32 = jnp.bfloat16, jnp.float32
     row = lax.broadcasted_iota(jnp.int32, (members, members), 0)
     column = lax.broadcasted_iota(jnp.int32, (members, members), 1)
-    select = jnp.where(order_ref[...] == row, 1.0, 0.0).astype(bf16)
-    select_t = jnp.where(upright(order_ref[...].astype(f32)) == column.astype(f32), 1.0, 0.0).astype(bf16)
-    block = picked + EXTRA
-    gathered = gathered_ref[...]
-    place = lax.broadcasted_iota(jnp.int32, (total, members), 0) % block
-    observed = jnp.where(place < picked, gathered.astype(f32), 0.0).astype(bf16)
+    order = order_ref[...]
+    select_ref[...] = jnp.where(order == row, 1.0, 0.0).astype(bf16)
+    select_t = jnp.where(upright(order.astype(f32)) == column.astype(f32), 1.0, 0.0).astype(bf16)
+    select_t_ref[...] = select_t
+    observed, pieces_ref[...] = split_rows(picked, rows_ref[...])
     ordered_t = dot(select_t, observed, NT).astype(bf16)
-    slot = lax.broadcasted_iota(jnp.int32, (16, total), 1) % block
-    pieces = dot(jnp.where(slot >= picked, 1.0, 0.0).astype(bf16), gathered)
+    gram_ref[...] = dot(ordered_t, ordered_t, NT) + jnp.where(row == column, members - 1.0, 0.0)
+
+
+def gram_part(picked, rows, member_order):
+    total, members = rows.shape
+    vmem = pl.BlockSpec(memory_space=pltpu.VMEM)
+    square = (members, members)
+    return pl.pallas_call(
+        functools.partial(gram_kernel, picked),
+        in_specs=[vmem] * 2,
+        out_specs=[vmem] * 4,
+        out_shape=[
+            jax.ShapeDtypeStruct(square, jnp.float32),
+            jax.ShapeDtypeStruct((16, members), jnp.float32),
+            jax.ShapeDtypeStruct(square, jnp.bfloat16),
+            jax.ShapeDtypeStruct(square, jnp.bfloat16),
+        ],
+        compiler_params=params(LIMIT),
+        cost_estimate=cost(1000 * members * 4, 4 * total * members),
+    )(rows, member_order[None, :])
+
+
+def update_kernel(picked, rows_ref, gram_ref, pieces_ref, select_ref, select_t_ref, *refs):
+    forecast_refs = refs[:-6]
+    out_ref, gram, factor, weights_t, results, out_sem = refs[-6:]
+    members = rows_ref.shape[1]
+    bf16, f32 = jnp.bfloat16, jnp.float32
+    row = lax.broadcasted_iota(jnp.int32, (members, members), 0)
+    column = lax.broadcasted_iota(jnp.int32, (members, members), 1)
+    diagonal, lower = row == column, row > column
+    identity = jnp.where(diagonal, 1.0, 0.0)
+    select = select_ref[...]
+    observed, pieces = split_rows(picked, rows_ref[...])
+    ordered_t = dot(select_t_ref[...], observed, NT).astype(bf16)
+    full = gram_ref[...] + dot(ordered_t, ordered_t, NT)
+    gram[...] = full
+    pieces = pieces_ref[...] + pieces
     piece_one = pieces.astype(bf16)
     piece_two, piece_three = halves(pieces - piece_one.astype(f32))
     projection = dot(piece_one, select) + (dot(piece_two, select) + dot(piece_three, select))
-    diagonal = row == column
-    full = dot(ordered_t, ordered_t, NT) + jnp.where(diagonal, members - 1.0, 0.0)
     on_diagonal = jnp.where(diagonal, full, 0.0)
     scale_row = lax.rsqrt(jnp.sum(on_diagonal, axis=0, keepdims=True))
     scale_column = lax.rsqrt(jnp.sum(on_diagonal, axis=1, keepdims=True))
     unit = full * scale_row * scale_column
-    gram[...] = full
-    lower = row > column
 
     def lower_part(residual):
-        return jnp.where(lower, residual, jnp.where(diagonal, 0.5 * residual, 0.0))
-
-    identity = jnp.where(diagonal, 1.0, 0.0)
-    factor[...] = identity - jnp.where(lower, unit, 0.0)
+        return jnp.where(lower, residual, jnp.where(diagonal, 0.5 * residual, 0.0)).astype(bf16)
+
+    def refine(inverse, unit):
+        unit_big, unit_small = halves(unit)
+        inverse = inverse.astype(bf16)
+        half_way = dot(inverse, unit_big) + dot(inverse, unit_small)
+        big, small = halves(half_way)
+        residual = dot(big, inverse, NT) + dot(small, inverse, NT) - identity
+        better = inverse.astype(f32) - dot(lower_part(residual), inverse)
+        return better, jnp.sum(residual * residual)
+
+    def finish(inverse):
+        inverse_big, inverse_small = halves(inverse)
+        turned = dot(inverse_big, select, NT) + dot(inverse_small, select, NT)
+        coefficients = fine_dot(projection, inverse, NT)
+        big, small = halves(turned)
+        placed = dot(select, big) + dot(select, small)
+        shift = fine_dot(coefficients, turned)[:1]
+        whole = (members - 1.0) ** 0.5 * placed + shift
+        whole = whole + (1.0 - jnp.sum(whole, axis=1, keepdims=True)) * (1.0 / members)
+        weights_t[...] = whole.astype(bf16)
+
+    inverse = identity - jnp.where(lower, unit, 0.0)
     unit_big = unit.astype(bf16)
     for _ in range(2):
-        inverse = factor[...]
         inverse_big = inverse.astype(bf16)
         half_way = dot(inverse_big, unit_big).astype(bf16)
         residual = dot(half_way, inverse_big, NT) - identity
-        factor[...] = inverse - dot(lower_part(residual).astype(bf16), inverse_big)
-
-    def refine(carried):
-        step, _ = carried
-        inverse = factor[...]
-        residual = fine_dot(fine_dot(inverse, unit), inverse, NT) - identity
-        factor[...] = inverse - dot(lower_part(residual).astype(bf16), inverse.astype(bf16))
-        return step + 1, jnp.sum(residual * residual)
-
-    def unfinished(carried):
-        step, error = carried
-        return (step < 8) & (error > 0.04) & (error < 64.0)
-
-    _, error = lax.while_loop(unfinished, refine, (0, jnp.float32(1.0)))
-    factor[...] = factor[...] * scale_row
+        inverse = inverse - dot(lower_part(residual), inverse_big)
+    inverse, error = refine(inverse, unit)
+    factor[...] = inverse
+    finish(inverse * scale_row)
 
     @pl.when(jnp.logical_not(error <= 0.04))
     def _():
-        factor[...] = identity
-
-        def eliminate(k, carry):
-            held = gram[...]
-            pivot_row = gram[pl.ds(k, 1), :]
-            pivot = jnp.sum(jnp.where(column[:1] == k, pivot_row, 0.0), axis=1, keepdims=True)
-            pivot_column = jnp.sum(jnp.where(column == k, held, 0.0), axis=1, keepdims=True)
-            share = jnp.where(row[:, :1] > k, pivot_column / pivot, 0.0)
-            factor[...] = factor[...] - share * factor[pl.ds(k, 1), :]
-            gram[...] = held - share * pivot_row
-            return carry
-
-        lax.fori_loop(0, members, eliminate, 0)
-        pivots = jnp.sum(jnp.where(diagonal, gram[...], 0.0), axis=1, keepdims=True)
-        factor[...] = factor[...] * lax.rsqrt(pivots)
-
-    inverse = factor[...]
-    coefficients = fine_dot(projection, inverse, NT)
-    shift = fine_dot(coefficients, inverse)[:1]
-    transform_t = (members - 1.0) ** 0.5 * inverse + shift
-    transform_t = transform_t + (1.0 - jnp.sum(transform_t, axis=1, keepdims=True)) * (1.0 / members)
-    transform_t = transform_t.astype(bf16)
-    weights_t = dot(select, dot(transform_t, select, NT).astype(bf16)).astype(bf16)
+        def again(carried):
+            step, _ = carried
+            better, error = refine(factor[...], gram[...] * scale_row * scale_column)
+            factor[...] = better
+            return step + 1, error
+
+        def unfinished(carried):
+            step, error = carried
+            return (step < 8) & (error > 0.04) & (error < 64.0)
+
+        _, last_error = lax.while_loop(unfinished, again, (0, error))
+        factor[...] = factor[...] * scale_row
+
+        @pl.when(jnp.logical_not(last_error <= 0.04))
+        def _():
+            factor[...] = identity
+
+            def eliminate(k, carry):
+                held = gram[...]
+                pivot_row = gram[pl.ds(k, 1), :]
+                pivot = jnp.sum(jnp.where(column[:1] == k, pivot_row, 0.0), axis=1, keepdims=True)
+                pivot_column = jnp.sum(jnp.where(column == k, held, 0.0), axis=1, keepdims=True)
+                share = jnp.where(row[:, :1] > k, pivot_column / pivot, 0.0)
+                factor[...] = factor[...] - share * factor[pl.ds(k, 1), :]
+                gram[...] = held - share * pivot_row
+                return carry
+
+            lax.fori_loop(0, members, eliminate, 0)
+            pivots = jnp.sum(jnp.where(diagonal, gram[...], 0.0), axis=1, keepdims=True)
+            factor[...] = factor[...] * lax.rsqrt(pivots)
+
+        finish(factor[...])
+
     stores = []
     for ref in forecast_refs:
         for p in range(ref.shape[0]):
             at = len(stores)
             forecast = ref[p].reshape(-1, members)
-            results[at] = dot(forecast, weights_t, NT).astype(bf16).reshape(ref.shape[1:])
+            results[at] = dot(forecast, weights_t[...], NT).astype(bf16).reshape(ref.shape[1:])
             store = pltpu.make_async_copy(results.at[at], out_ref.at[at], out_sem.at[at])
             store.start()
             stores.append(store)
@@ -386,24 +459,25 @@
         store.wait()
 
 
-def updated(picked, gathered, member_order, forecasts, shape):
+def updated(picked, rows, part, forecasts, shape):
     planes, span, height, members = shape
     size = planes * span * height * members
     vmem = pl.BlockSpec(memory_space=pltpu.VMEM)
     return pl.pallas_call(
         functools.partial(update_kernel, picked),
-        in_specs=[vmem] * (2 + len(forecasts)),
+        in_specs=[vmem] * (1 + len(part) + len(forecasts)),
         out_specs=pl.BlockSpec(memory_space=pltpu.HBM),
         out_shape=jax.ShapeDtypeStruct(shape, jnp.bfloat16),
         scratch_shapes=[
             pltpu.VMEM((members, members), jnp.float32),
             pltpu.VMEM((members, members), jnp.float32),
+            pltpu.VMEM((members, members), jnp.bfloat16),
             pltpu.VMEM(shape, jnp.bfloat16),
             pltpu.SemaphoreType.DMA((planes,)),
         ],
         compiler_params=params(LIMIT),
         cost_estimate=cost(4 * size, 5 * size),
-    )(gathered, member_order[None, :], *forecasts)
+    )(rows, *part, *forecasts)
 
 
 def pairs(count, first):
@@ -433,34 +507,25 @@
 
 
 def exchanges():
-    axes = ("stream", "span", "height")
-    sizes = [lax.axis_size(axis) for axis in axes]
-    if any(size & (size - 1) for size in sizes):
-        yield functools.partial(lax.all_gather, axis_name=axes, axis=0, tiled=True)
-        return
-
-    def flat(place):
-        return (place["stream"] * sizes[1] + place["span"]) * sizes[2] + place["height"]
-
+    sizes = [lax.axis_size(axis) for axis in AXES]
     places = [
         {"stream": i // (sizes[1] * sizes[2]), "span": i // sizes[2] % sizes[1], "height": i % sizes[2]}
         for i in range(sizes[0] * sizes[1] * sizes[2])
     ]
+
+    def flat(place):
+        return (place["stream"] * sizes[1] + place["span"]) * sizes[2] + place["height"]
+
     steps = rounds()
     apart = sizes[0] // 2
     while apart:
         steps.append((("stream", apart), ("stream", apart)))
         apart //= 2
+    moves = []
     for step in steps:
-        moves = []
-        for place in places:
-            axis, bit = step[place["stream"] % 2]
-            moves.append((flat(place), flat(place | {axis: place[axis] ^ bit})))
-
-        def swap(rows, moves=moves):
-            return jnp.concatenate([rows, lax.ppermute(rows, axes, moves)], axis=0)
-
-        yield swap
+        taken = [(place, *step[place["stream"] % 2]) for place in places]
+        moves.append([(flat(at), flat(at | {axis: at[axis] ^ bit})) for at, axis, bit in taken])
+    return moves
 
 
 def shards(source, inflow, recovery, obs_rows, obs, observation_weight, member_order):
@@ -470,6 +535,7 @@
     together = lax.optimization_barrier
 
     source, first, second = border(source, parity)
+    inflow, first = together((inflow, first))
     inflow = pltpu.with_memory_space_constraint(inflow, pltpu.VMEM)
     first = lax.ppermute(first, "height", pairs(levels, 0))
     second = lax.ppermute(second, "height", pairs(levels, 1))
@@ -478,24 +544,28 @@
     term, edge, leaving = edge_march(parity, first, second, low_rate, high_rate, end)
     total = jnp.prod(recovery, axis=0)[..., None] if lax.axis_size("stream") > 2 else None
     incoming = downstream(leaving, total)
-    rows = observe(obs_rows, obs, observation_weight, picks, share, incoming, edge)
+    picks, obs, weight = prepare(obs_rows, obs, observation_weight, picks, edge, height)
+    rows = observe(obs_rows, obs, weight, picks, share, incoming)
     state = incoming.reshape(span * height, members)
     cuts = [planes * part // 16 for part in CUTS]
     parts = []
-    for swap in exchanges():
-        swapped = swap(rows)
+    *moves, last_moves = exchanges()
+    for pairing in moves:
+        other = lax.ppermute(rows, AXES, pairing)
         if len(cuts) > 1:
             state, rows = together((state, rows))
             forecast, state = forecasts(source, inflow, rates, state, term, cuts[0], cuts[1])
-            swapped, state, forecast = together((swapped, state, forecast))
+            other, state, forecast = together((other, state, forecast))
             parts.append(forecast)
             cuts = cuts[1:]
-        rows = swapped
+        rows = jnp.concatenate([rows, other], axis=0)
     while len(cuts) > 1:
         forecast, state = forecasts(source, inflow, rates, state, term, cuts[0], cuts[1])
         parts.append(forecast)
         cuts = cuts[1:]
-    return updated(obs_rows.shape[0], rows, member_order, parts, source.shape)
+    other = lax.ppermute(rows, AXES, last_moves)
+    part = gram_part(obs_rows.shape[0], rows, member_order)
+    return updated(obs_rows.shape[0], other, part, parts, source.shape)
 
 
 def solution(mesh):

time: 80.3 us -> 79.6 us (level)
  waiting for transfers between devices: 10.4 us -> 8.68 us
  Pallas kernels: 53.9 us -> 55 us
    pallas_call x0 -> x2, Pallas kernels: none -> 1.64 us  [the longest x1 1.02 us: prepare(): pl.pallas_call(functools.partial(prepare_kernel, height), in_specs=[pl.Bl...]
    ppermute x1, waiting for transfers between devices: 1.49 us -> 0.44 us  [downstream(): incoming = lax.ppermute(value, 'stream', steps)]
  transfers between devices with their start and end apart: 8 -> 8, of which waited for: 6 -> 6; matrix products, arithmetic and copies ran while one was open for 0% -> 0% of each run, Pallas kernels for 8% -> 11%
where the time goes in v5:
time: 79.6 us; the launch traced here: 79.5 us
  Pallas kernels  55 us (69%)
  starting transfers between devices  15.5 us (19%)
  waiting for transfers between devices  8.68 us (11%)
    pallas_call x1, Pallas kernels, updated(): pl.pallas_call(functools.partial(update_kernel, picked), in_specs=[vmem]...  43 us
    ppermute x4, starting transfers between devices, shards(): other = lax.ppermute(rows, AXES, pairing)  10.2 us
    ppermute x4, waiting for transfers between devices, shards(): other = lax.ppermute(rows, AXES, pairing)  7.26 us
    pallas_call x4, Pallas kernels, forecasts(): pl.pallas_call(functools.partial(forecast_kernel, start, planes), in_spec...  3.67 us
    pallas_call x1, Pallas kernels, march(): pl.pallas_call(march_kernel, in_specs=[pl.BlockSpec(memory_space=pltpu.SM...  3.1 us
    ppermute x1, starting transfers between devices, shards(): first = lax.ppermute(first, 'height', pairs(levels, 0))  3.09 us
    pallas_call x1, Pallas kernels, border(): pl.pallas_call(border_kernel, in_specs=[pl.BlockSpec(memory_space=pltpu.S...  2.44 us
  transfers between devices with their start and end apart: 8, of which 6 were waited for; matrix products, arithmetic and copies ran while one was open for 0% of the time, Pallas kernels for 11%

profile of v5, /device:TPU:0, one launch (start us, length us, event | category | flops | bytes accessed | tf_op | source)
XLA Modules:
  0.0 79.5 jit_solution(10334978648283309644)
XLA Ops:
  0.0 0.0 copy-start.5
  0.0 0.0 copy-start.1
  0.0 0.0 copy-start
  0.0 2.4 %shard_map.73 = (bf16[16,16,32,256]{3,2,1,0:T(8,128)(2,1)S(1)}, bf16[16,16,256]{2,1,0:T(8,128)(2,1)S(1)}, bf16[16,16,256]{2,1,0:T(8,128)(2,1)S(1)}) custom-call(s32[1]{0:T(128)} %bitcast.parity_ref, bf16[16,16,32,256]{3,2,1,0:T(8,128)(2,1)} %source_ref.1), custom_call_target="tpu_custom_call" | custom-call | flops 2097152000 | bytes 2097152 | tf_op jit(solution)/shard_map/pallas_call | solution.py:55
  2.5 3.1 %collective-permute-start = (bf16[16,16,256]{2,1,0:T(8,128)(2,1)S(1)}, bf16[16,16,256]{2,1,0:T(8,128)(2,1)S(1)}, u32[]{:S(2)}, u32[]{:S(2)}) collective-permute-start(bf16[16,16,256]{2,1,0:T(8,128)(2,1)S(1)} %get-tuple-element.59), channel_id=1, source_target_pairs={{0,1},{2,3},{1,0},{3,2},{4,5},{6,7},{5,4},{7,6},{8,9},{10,11},{9,8... | collective-permute-start | bytes 393224 | tf_op jit(solution)/shard_map/ppermute | solution.py:540
  5.6 0.7 collective-permute-start.1
  6.2 0.0 copy-done.5
  6.2 0.0 copy-done.1
  6.2 0.0 copy-done
  6.2 0.0 copy-start.3
  6.3 0.0 copy-start.4
  6.3 3.1 %shard_map.74 = (f32[512,256]{1,0:T(8,128)S(1)}, f32[32,256]{1,0:T(8,128)S(1)}, f32[32,256]{1,0:T(8,128)S(1)}, f32[512,16]{1,0:T(8,128)S(1)}, f32[16,16]{1,0:T(8,128)S(1)}, /*index=5*/f32[16,16]{1,0:T(8,128)S(1)}) custom-call(s32[32]{0:T(128)S(1)} %copy-done.5, s32[1,32]{1,0:T(1,128)S(1)} %bitcast.10, ...), custom_call_target="tpu_custom_call" | custom-call | flops 6291456000 | bytes 8388608 | tf_op jit(solution)/shard_map/pallas_call | solution.py:142
  9.4 0.0 collective-permute-done.first_ref
  9.4 0.0 collective-permute-done.1.second_ref
  9.4 0.2 shard_map.75
  9.6 1.5 %collective-permute-start.2 = (f32[16,32,256]{2,1,0:T(8,128)S(1)}, f32[16,32,256]{2,1,0:T(8,128)S(1)}, u32[]{:S(2)}, u32[]{:S(2)}) collective-permute-start(f32[16,32,256]{2,1,0:T(8,128)S(1)} %get-tuple-element.72), channel_id=1, source_target_pairs={{0,16},{1,17},{2,18},{3,19},{4,20},{5,21},{6,22},{7,23},{8,24},{9,... | collective-permute-start | bytes 1572872 | tf_op jit(solution)/shard_map/ppermute | solution.py:491
  11.1 0.0 copy-done.3
  11.1 0.0 copy-done.4
  11.1 1.0 %shard_map.76 = (f32[32,256]{1,0:T(8,128)S(1)}, f32[32,256]{1,0:T(8,128)S(1)}, f32[32,256]{1,0:T(8,128)S(1)}) custom-call(s32[32]{0:T(128)S(1)} %copy-done.5, f32[2,16,16,256]{3,2,1,0:T(8,128)S(1)} %get-tuple-element.66.edge_ref, f32[32,256]{1,0:T(8,128)S(1)} %get-tuple-element.67.picks_ref, f32[1,32]{1,0:T(1,128)S(1)} %bitcast.8, f32[1,32]{1,0:T(1,128)S(1)} %bitcast.9), custom_call_target="tpu_custom_call" | custom-call | flops 819200000 | bytes 524288 | tf_op jit(solution)/shard_map/pallas_call | solution.py:220
  12.1 0.4 collective-permute-done.2.incoming_ref
  12.6 1.0 %shard_map.77 = bf16[40,256]{1,0:T(8,128)(2,1)S(1)} custom-call(s32[32]{0:T(128)S(1)} %copy-done.5, f32[32,256]{1,0:T(8,128)S(1)} %get-tuple-element.68.obs_ref, f32[32,256]{1,0:T(8,128)S(1)} %get-tuple-element.69.weight_ref, f32[32,256]{1,0:T(8,128)S(1)} %get-tuple-element.70.picks_ref, f32[32,256]{1,0:T(8,128)S(1)} %get-tuple-element.71.share_ref, ...), custom_call_target="tpu_custom_call" | custom-call | flops 327680000 | bytes 524288 | tf_op jit(solution)/shard_map/pallas_call | solution.py:254
  13.5 5.5 %collective-permute-start.3 = (bf16[40,256]{1,0:T(8,128)(2,1)S(1)}, bf16[40,256]{1,0:T(8,128)(2,1)S(1)}, u32[]{:S(2)}, u32[]{:S(2)}) collective-permute-start(bf16[40,256]{1,0:T(8,128)(2,1)S(1)} %shard_map.77), channel_id=1, source_target_pairs={{0,2},{1,3},{2,0},{3,1},{4,6},{5,7},{6,4},{7,5},{8,10},{9,11},{10,... | collective-permute-start | bytes 61448 | tf_op jit(solution)/shard_map/ppermute | solution.py:554
  19.0 0.7 shard_map.78
  19.8 1.0 %collective-permute-done.3 = bf16[40,256]{1,0:T(8,128)(2,1)S(1)} collective-permute-done((bf16[40,256]{1,0:T(8,128)(2,1)S(1)}, bf16[40,256]{1,0:T(8,128)(2,1)S(1)}, u32[]{:S(2)}, u32[]{:S(2)}) %collective-permute-start.3) | collective-permute-done | bytes 20512 | tf_op jit(solution)/shard_map/ppermute | solution.py:554
  20.8 1.5 %collective-permute-start.4 = (bf16[80,256]{1,0:T(8,128)(2,1)S(1)}, bf16[80,256]{1,0:T(8,128)(2,1)S(1)}, u32[]{:S(2)}, u32[]{:S(2)}) collective-permute-start(bf16[80,256]{1,0:T(8,128)(2,1)S(1)} %constant_dynamic-update-slice_fusion), channel_id=1, source_target_pairs={{0,8},{1,9},{2,10},{3,11},{4,12},{5,13},{6,14},{7,15},{8,0},{9,1},... | collective-permute-start | bytes 122888 | tf_op jit(solution)/shard_map/ppermute | solution.py:554
  22.3 0.7 shard_map.79
  23.1 1.7 %collective-permute-done.4 = bf16[80,256]{1,0:T(8,128)(2,1)S(1)} collective-permute-done((bf16[80,256]{1,0:T(8,128)(2,1)S(1)}, bf16[80,256]{1,0:T(8,128)(2,1)S(1)}, u32[]{:S(2)}, u32[]{:S(2)}) %collective-permute-start.4) | collective-permute-done | bytes 40992 | tf_op jit(solution)/shard_map/ppermute | solution.py:554
  24.8 1.7 %collective-permute-start.5 = (bf16[160,256]{1,0:T(8,128)(2,1)S(1)}, bf16[160,256]{1,0:T(8,128)(2,1)S(1)}, u32[]{:S(2)}, u32[]{:S(2)}) collective-permute-start(bf16[160,256]{1,0:T(8,128)(2,1)S(1)} %constant_dynamic-update-slice_fusion.2), channel_id=1, source_target_pairs={{0,1},{1,0},{2,3},{3,2},{4,5},{5,4},{6,7},{7,6},{8,9},{9,8},{10,11... | collective-permute-start | bytes 245768 | tf_op jit(solution)/shard_map/ppermute | solution.py:554
  26.5 0.7 shard_map.80
  27.3 2.2 %collective-permute-done.5 = bf16[160,256]{1,0:T(8,128)(2,1)S(1)} collective-permute-done((bf16[160,256]{1,0:T(8,128)(2,1)S(1)}, bf16[160,256]{1,0:T(8,128)(2,1)S(1)}, u32[]{:S(2)}, u32[]{:S(2)}) %collective-permute-start.5) | collective-permute-done | bytes 81952 | tf_op jit(solution)/shard_map/ppermute | solution.py:554
  29.5 1.5 %collective-permute-start.6 = (bf16[320,256]{1,0:T(8,128)(2,1)S(1)}, bf16[320,256]{1,0:T(8,128)(2,1)S(1)}, u32[]{:S(2)}, u32[]{:S(2)}) collective-permute-start(bf16[320,256]{1,0:T(8,128)(2,1)S(1)} %constant_dynamic-update-slice_fusion.4), channel_id=1, source_target_pairs={{0,4},{1,5},{2,6},{3,7},{4,0},{5,1},{6,2},{7,3},{8,12},{9,13},{10,... | collective-permute-start | bytes 491528 | tf_op jit(solution)/shard_map/ppermute | solution.py:554
  31.0 0.0 copy-start.2
  31.0 1.5 %shard_map.81 = (bf16[4,16,32,256]{3,2,1,0:T(8,128)(2,1)S(1)}, f32[512,256]{1,0:T(8,128)}) custom-call(bf16[16,16,32,256]{3,2,1,0:T(8,128)(2,1)S(1)} %get-tuple-element.55.source_ref, bf16[16,16,32,256]{3,2,1,0:T(8,128)(2,1)S(1)} %copy-done, f32[512,16]{1,0:T(8,128)S(1)} %get-tuple-element.73.rate_ref, f32[512,256]{1,0:T(8,128)S(1)} %get-tuple-element.94.state_ref, ...), custom_call_target="tpu_custom_call" | custom-call | flops 2097152000 | bytes 3145728 | tf_op jit(solution)/shard_map/pallas_call | solution.py:291
  32.5 2.3 %collective-permute-done.6 = bf16[320,256]{1,0:T(8,128)(2,1)S(1)} collective-permute-done((bf16[320,256]{1,0:T(8,128)(2,1)S(1)}, bf16[320,256]{1,0:T(8,128)(2,1)S(1)}, u32[]{:S(2)}, u32[]{:S(2)}) %collective-permute-start.6) | collective-permute-done | bytes 163872 | tf_op jit(solution)/shard_map/ppermute | solution.py:554
  34.8 0.1 collective-permute-start.7
  34.9 0.0 copy-done.2
  34.9 0.6 shard_map.82
  35.5 1.0 %collective-permute-done.7.rows_ref = bf16[640,256]{1,0:T(8,128)(2,1)S(1)} collective-permute-done((bf16[640,256]{1,0:T(8,128)(2,1)S(1)}, bf16[640,256]{1,0:T(8,128)(2,1)S(1)}, u32[]{:S(2)}, u32[]{:S(2)}) %collective-permute-start.7) | collective-permute-done | bytes 327712 | tf_op jit(solution)/shard_map/ppermute | solution.py:566
  36.5 43.0 %shard_map.83 = bf16[16,16,32,256]{3,2,1,0:T(8,128)(2,1)} custom-call(bf16[640,256]{1,0:T(8,128)(2,1)S(1)} %collective-permute-done.7.rows_ref, f32[256,256]{1,0:T(8,128)S(1)} %get-tuple-element.97.gram_ref, f32[16,256]{1,0:T(8,128)S(1)} %get-tuple-element.98.pieces_ref, bf16[256,256]{1,0:T(8,128)(2,1)S(1)} %get-tuple-element.99.select_ref, ...), custom_call_target="tpu_custom_call" | custom-call | flops 8388608000 | bytes 10485760 | tf_op jit(solution)/shard_map/pallas_call | solution.py:466
  (8 shorter events, 0.1 us)
Async XLA Ops:
  0.0 6.2 %copy-start.5 = (s32[32]{0:T(128)S(1)}, s32[32]{0:T(128)}, u32[]{:S(2)}) copy-start(s32[32]{0:T(128)} %rows_ref.5) | copy-start | bytes 388
  0.0 6.2 %copy-start.1 = (f32[16,16,32]{2,1,0:T(8,128)S(1)}, f32[16,16,32]{2,1,0:T(8,128)}, u32[]{:S(2)}) copy-start(f32[16,16,32]{2,1,0:T(8,128)} %recovery_ref.1) | copy-start | bytes 98308
  0.0 6.2 %copy-start = (bf16[16,16,32,256]{3,2,1,0:T(8,128)(2,1)S(1)}, bf16[16,16,32,256]{3,2,1,0:T(8,128)(2,1)}, u32[]{:S(2)}) copy-start(bf16[16,16,32,256]{3,2,1,0:T(8,128)(2,1)} %inflow_ref.4) | copy-start | bytes 12582916
  2.5 6.9 %collective-permute-start = (bf16[16,16,256]{2,1,0:T(8,128)(2,1)S(1)}, bf16[16,16,256]{2,1,0:T(8,128)(2,1)S(1)}, u32[]{:S(2)}, u32[]{:S(2)}) collective-permute-start(bf16[16,16,256]{2,1,0:T(8,128)(2,1)S(1)} %get-tuple-element.59), channel_id=1, source_target_pairs={{0,1},{2,3},{1,0},{3,2},{4,5},{6,7},{5,4},{7,6},{8,9},{10,11},{9,8... | collective-permute-start | bytes 393224 | tf_op jit(solution)/shard_map/ppermute | solution.py:540
  5.6 3.8 %collective-permute-start.1 = (bf16[16,16,256]{2,1,0:T(8,128)(2,1)S(1)}, bf16[16,16,256]{2,1,0:T(8,128)(2,1)S(1)}, u32[]{:S(2)}, u32[]{:S(2)}) collective-permute-start(bf16[16,16,256]{2,1,0:T(8,128)(2,1)S(1)} %get-tuple-element.60), channel_id=1, source_target_pairs={{1,2},{2,1},{5,6},{6,5},{9,10},{10,9},{13,14},{14,13},{17,18},{18,... | collective-permute-start | bytes 393224 | tf_op jit(solution)/shard_map/ppermute | solution.py:541
  6.2 4.8 %copy-start.3 = (f32[32]{0:T(128)S(1)}, f32[32]{0:T(128)}, u32[]{:S(2)}) copy-start(f32[32]{0:T(128)} %param.11) | copy-start | bytes 388
  6.3 4.8 %copy-start.4 = (f32[32]{0:T(128)S(1)}, f32[32]{0:T(128)}, u32[]{:S(2)}) copy-start(f32[32]{0:T(128)} %param.12) | copy-start | bytes 388
  9.6 3.0 %collective-permute-start.2 = (f32[16,32,256]{2,1,0:T(8,128)S(1)}, f32[16,32,256]{2,1,0:T(8,128)S(1)}, u32[]{:S(2)}, u32[]{:S(2)}) collective-permute-start(f32[16,32,256]{2,1,0:T(8,128)S(1)} %get-tuple-element.72), channel_id=1, source_target_pairs={{0,16},{1,17},{2,18},{3,19},{4,20},{5,21},{6,22},{7,23},{8,24},{9,... | collective-permute-start | bytes 1572872 | tf_op jit(solution)/shard_map/ppermute | solution.py:491
  13.5 7.2 %collective-permute-start.3 = (bf16[40,256]{1,0:T(8,128)(2,1)S(1)}, bf16[40,256]{1,0:T(8,128)(2,1)S(1)}, u32[]{:S(2)}, u32[]{:S(2)}) collective-permute-start(bf16[40,256]{1,0:T(8,128)(2,1)S(1)} %shard_map.77), channel_id=1, source_target_pairs={{0,2},{1,3},{2,0},{3,1},{4,6},{5,7},{6,4},{7,5},{8,10},{9,11},{10,... | collective-permute-start | bytes 61448 | tf_op jit(solution)/shard_map/ppermute | solution.py:554
  20.8 4.0 %collective-permute-start.4 = (bf16[80,256]{1,0:T(8,128)(2,1)S(1)}, bf16[80,256]{1,0:T(8,128)(2,1)S(1)}, u32[]{:S(2)}, u32[]{:S(2)}) collective-permute-start(bf16[80,256]{1,0:T(8,128)(2,1)S(1)} %constant_dynamic-update-slice_fusion), channel_id=1, source_target_pairs={{0,8},{1,9},{2,10},{3,11},{4,12},{5,13},{6,14},{7,15},{8,0},{9,1},... | collective-permute-start | bytes 122888 | tf_op jit(solution)/shard_map/ppermute | solution.py:554
  24.8 4.7 %collective-permute-start.5 = (bf16[160,256]{1,0:T(8,128)(2,1)S(1)}, bf16[160,256]{1,0:T(8,128)(2,1)S(1)}, u32[]{:S(2)}, u32[]{:S(2)}) collective-permute-start(bf16[160,256]{1,0:T(8,128)(2,1)S(1)} %constant_dynamic-update-slice_fusion.2), channel_id=1, source_target_pairs={{0,1},{1,0},{2,3},{3,2},{4,5},{5,4},{6,7},{7,6},{8,9},{9,8},{10,11... | collective-permute-start | bytes 245768 | tf_op jit(solution)/shard_map/ppermute | solution.py:554
  29.5 5.3 %collective-permute-start.6 = (bf16[320,256]{1,0:T(8,128)(2,1)S(1)}, bf16[320,256]{1,0:T(8,128)(2,1)S(1)}, u32[]{:S(2)}, u32[]{:S(2)}) collective-permute-start(bf16[320,256]{1,0:T(8,128)(2,1)S(1)} %constant_dynamic-update-slice_fusion.4), channel_id=1, source_target_pairs={{0,4},{1,5},{2,6},{3,7},{4,0},{5,1},{6,2},{7,3},{8,12},{9,13},{10,... | collective-permute-start | bytes 491528 | tf_op jit(solution)/shard_map/ppermute | solution.py:554
  31.0 3.9 %copy-start.2 = (s32[256]{0:T(256)S(1)}, s32[256]{0:T(256)}, u32[]{:S(2)}) copy-start(s32[256]{0:T(256)} %param.13) | copy-start | bytes 3076
  34.8 1.7 %collective-permute-start.7 = (bf16[640,256]{1,0:T(8,128)(2,1)S(1)}, bf16[640,256]{1,0:T(8,128)(2,1)S(1)}, u32[]{:S(2)}, u32[]{:S(2)}) collective-permute-start(bf16[640,256]{1,0:T(8,128)(2,1)S(1)} %constant_dynamic-update-slice_fusion.6.rows_ref), channel_id=1, source_target_pairs={{0,16},{1,17},{2,18},{3,19},{4,20},{5,21},{6,22},{7,23},{8,24},{9,... | collective-permute-start | bytes 983048 | tf_op jit(solution)/shard_map/ppermute | solution.py:566

commit v6 on v5

--- a/solution.py
+++ b/solution.py
@@ -262,9 +262,10 @@
     )(obs_rows, obs, weight, picks, share, incoming)
 
 
-def forecast_kernel(start, planes, source_ref, inflow_ref, rate_ref, state_ref, term_ref, *refs):
-    out_ref, end_ref = refs[:2]
+def anomaly_kernel(start, planes, source_ref, inflow_ref, rate_ref, state_ref, term_ref, *refs):
+    out_ref, mean_ref, end_ref = refs
     _, span, height, members = source_ref.shape
+    wide = mean_ref.shape[2]
     cells = group_of(span, height)
     group = cells * height
     mix = stencil(group, height)
@@ -273,27 +274,32 @@
         before = state_ref if p == start else end_ref
         for c in range(span // cells):
             term = dot(mix, source_ref[p, c * cells : (c + 1) * cells].reshape(group, members))
+            some = slice(c * cells, (c + 1) * cells)
+            part = slice(c * group, (c + 1) * group)
+            halo = []
             for a in range(c * cells, (c + 1) * cells):
-                part = slice(a * height, (a + 1) * height)
                 low, high = term_ref[0, p, a : a + 1, :], term_ref[1, p, a : a + 1, :]
-                halo = jnp.where(row == 0, low, jnp.where(row == height - 1, high, 0.0))
-                deficit = rate_ref[part, p : p + 1] * before[part] + (
-                    term[a * height - c * group : (a + 1) * height - c * group] + halo
-                )
-                end_ref[part] = deficit
-                out_ref[p - start, a] = (inflow_ref[p, a].astype(jnp.float32) - deficit).astype(jnp.bfloat16)
-
-
-def forecasts(source, inflow, rates, state, term, start, stop):
+                halo.append(jnp.where(row == 0, low, jnp.where(row == height - 1, high, 0.0)))
+            deficit = rate_ref[part, p : p + 1] * before[part] + (term + jnp.concatenate(halo, axis=0))
+            end_ref[part] = deficit
+            forecast = inflow_ref[p, some].astype(jnp.float32).reshape(group, members) - deficit
+            mean = jnp.sum(forecast, axis=1, keepdims=True) * (1.0 / members)
+            anomaly = (forecast - mean).astype(jnp.bfloat16)
+            out_ref[p - start, some] = anomaly.reshape(cells, height, members)
+            mean_ref[p - start, part] = jnp.broadcast_to(mean, (group, wide))
+
+
+def anomalies(source, inflow, rates, state, term, start, stop):
     planes = stop - start
     vmem = pl.BlockSpec(memory_space=pltpu.VMEM)
     size = state.size * planes
     return pl.pallas_call(
-        functools.partial(forecast_kernel, start, planes),
+        functools.partial(anomaly_kernel, start, planes),
         in_specs=[vmem] * 5,
-        out_specs=[vmem, vmem],
+        out_specs=[vmem] * 3,
         out_shape=[
             pltpu.VMEM((planes,) + source.shape[1:], jnp.bfloat16),
+            pltpu.VMEM((planes, state.shape[0], min(128, state.shape[1])), jnp.float32),
             pltpu.VMEM(state.shape, jnp.float32),
         ],
         compiler_params=params(LIMIT),
@@ -355,7 +361,7 @@
 
 
 def update_kernel(picked, rows_ref, gram_ref, pieces_ref, select_ref, select_t_ref, *refs):
-    forecast_refs = refs[:-6]
+    part_refs = refs[:-6]
     out_ref, gram, factor, weights_t, results, out_sem = refs[-6:]
     members = rows_ref.shape[1]
     bf16, f32 = jnp.bfloat16, jnp.float32
@@ -396,9 +402,7 @@
         big, small = halves(turned)
         placed = dot(select, big) + dot(select, small)
         shift = fine_dot(coefficients, turned)[:1]
-        whole = (members - 1.0) ** 0.5 * placed + shift
-        whole = whole + (1.0 - jnp.sum(whole, axis=1, keepdims=True)) * (1.0 / members)
-        weights_t[...] = whole.astype(bf16)
+        weights_t[...] = ((members - 1.0) ** 0.5 * placed + shift).astype(bf16)
 
     inverse = identity - jnp.where(lower, unit, 0.0)
     unit_big = unit.astype(bf16)
@@ -447,11 +451,12 @@
         finish(factor[...])
 
     stores = []
-    for ref in forecast_refs:
+    for ref, mean_ref in zip(part_refs[::2], part_refs[1::2]):
         for p in range(ref.shape[0]):
             at = len(stores)
-            forecast = ref[p].reshape(-1, members)
-            results[at] = dot(forecast, weights_t[...], NT).astype(bf16).reshape(ref.shape[1:])
+            mean = jnp.concatenate([mean_ref[p]] * (members // mean_ref.shape[2]), axis=1)
+            analysis = mean + dot(ref[p].reshape(-1, members), weights_t[...], NT)
+            results[at] = analysis.astype(bf16).reshape(ref.shape[1:])
             store = pltpu.make_async_copy(results.at[at], out_ref.at[at], out_sem.at[at])
             store.start()
             stores.append(store)
@@ -459,13 +464,13 @@
         store.wait()
 
 
-def updated(picked, rows, part, forecasts, shape):
+def updated(picked, rows, part, parts, shape):
     planes, span, height, members = shape
     size = planes * span * height * members
     vmem = pl.BlockSpec(memory_space=pltpu.VMEM)
     return pl.pallas_call(
         functools.partial(update_kernel, picked),
-        in_specs=[vmem] * (1 + len(part) + len(forecasts)),
+        in_specs=[vmem] * (1 + len(part) + len(parts)),
         out_specs=pl.BlockSpec(memory_space=pltpu.HBM),
         out_shape=jax.ShapeDtypeStruct(shape, jnp.bfloat16),
         scratch_shapes=[
@@ -477,7 +482,7 @@
         ],
         compiler_params=params(LIMIT),
         cost_estimate=cost(4 * size, 5 * size),
-    )(rows, *part, *forecasts)
+    )(rows, *part, *parts)
 
 
 def pairs(count, first):
@@ -554,14 +559,14 @@
         other = lax.ppermute(rows, AXES, pairing)
         if len(cuts) > 1:
             state, rows = together((state, rows))
-            forecast, state = forecasts(source, inflow, rates, state, term, cuts[0], cuts[1])
-            other, state, forecast = together((other, state, forecast))
-            parts.append(forecast)
+            anomaly, mean, state = anomalies(source, inflow, rates, state, term, cuts[0], cuts[1])
+            other, state, anomaly, mean = together((other, state, anomaly, mean))
+            parts += [anomaly, mean]
             cuts = cuts[1:]
         rows = jnp.concatenate([rows, other], axis=0)
     while len(cuts) > 1:
-        forecast, state = forecasts(source, inflow, rates, state, term, cuts[0], cuts[1])
-        parts.append(forecast)
+        anomaly, mean, state = anomalies(source, inflow, rates, state, term, cuts[0], cuts[1])
+        parts += [anomaly, mean]
         cuts = cuts[1:]
     other = lax.ppermute(rows, AXES, last_moves)
     part = gram_part(obs_rows.shape[0], rows, member_order)

time: 79.6 us -> 79.3 us (level)
  waiting for transfers between devices: 8.68 us -> 6.24 us
  Pallas kernels: 55 us -> 57.1 us
    ppermute x4, waiting for transfers between devices: 7.26 us -> 4.81 us  [shards(): other = lax.ppermute(rows, AXES, pairing)]
    pallas_call x4, Pallas kernels: 3.67 us -> 6.01 us  [anomalies(): pl.pallas_call(functools.partial(anomaly_kernel, start, planes), in_specs...]
  transfers between devices with their start and end apart: 8 -> 8, of which waited for: 6 -> 6; matrix products, arithmetic and copies ran while one was open for 0% -> 0% of each run, Pallas kernels for 11% -> 14%
where the time goes in v6:
time: 79.3 us; the launch traced here: 79.2 us
  Pallas kernels  57.1 us (72%)
  starting transfers between devices  15.5 us (20%)
  waiting for transfers between devices  6.24 us (8%)
    pallas_call x1, Pallas kernels, updated(): pl.pallas_call(functools.partial(update_kernel, picked), in_specs=[vmem]...  42.8 us
    ppermute x4, starting transfers between devices, shards(): other = lax.ppermute(rows, AXES, pairing)  10.2 us
    pallas_call x4, Pallas kernels, anomalies(): pl.pallas_call(functools.partial(anomaly_kernel, start, planes), in_specs...  6.01 us
    ppermute x4, waiting for transfers between devices, shards(): other = lax.ppermute(rows, AXES, pairing)  4.81 us
    pallas_call x1, Pallas kernels, march(): pl.pallas_call(march_kernel, in_specs=[pl.BlockSpec(memory_space=pltpu.SM...  3.1 us
    ppermute x1, starting transfers between devices, shards(): first = lax.ppermute(first, 'height', pairs(levels, 0))  3.09 us
    pallas_call x1, Pallas kernels, border(): pl.pallas_call(border_kernel, in_specs=[pl.BlockSpec(memory_space=pltpu.S...  2.44 us
  transfers between devices with their start and end apart: 8, of which 6 were waited for; matrix products, arithmetic and copies ran while one was open for 0% of the time, Pallas kernels for 14%

profile of v6, /device:TPU:0, one launch (start us, length us, event | category | flops | bytes accessed | tf_op | source)
XLA Modules:
  0.0 79.2 jit_solution(12686234434599588338)
XLA Ops:
  0.0 0.0 copy-start.5
  0.0 0.0 copy-start.1
  0.0 0.0 copy-start
  0.0 2.4 %shard_map.73 = (bf16[16,16,32,256]{3,2,1,0:T(8,128)(2,1)S(1)}, bf16[16,16,256]{2,1,0:T(8,128)(2,1)S(1)}, bf16[16,16,256]{2,1,0:T(8,128)(2,1)S(1)}) custom-call(s32[1]{0:T(128)} %bitcast.parity_ref, bf16[16,16,32,256]{3,2,1,0:T(8,128)(2,1)} %source_ref.1), custom_call_target="tpu_custom_call" | custom-call | flops 2097152000 | bytes 2097152 | tf_op jit(solution)/shard_map/pallas_call | solution.py:55
  2.5 3.1 %collective-permute-start = (bf16[16,16,256]{2,1,0:T(8,128)(2,1)S(1)}, bf16[16,16,256]{2,1,0:T(8,128)(2,1)S(1)}, u32[]{:S(2)}, u32[]{:S(2)}) collective-permute-start(bf16[16,16,256]{2,1,0:T(8,128)(2,1)S(1)} %get-tuple-element.67), channel_id=1, source_target_pairs={{0,1},{2,3},{1,0},{3,2},{4,5},{6,7},{5,4},{7,6},{8,9},{10,11},{9,8... | collective-permute-start | bytes 393224 | tf_op jit(solution)/shard_map/ppermute | solution.py:545
  5.6 0.7 collective-permute-start.1
  6.2 0.0 copy-done.5
  6.2 0.0 copy-done.1
  6.2 0.0 copy-done
  6.2 0.0 copy-start.3
  6.3 0.0 copy-start.4
  6.3 3.1 %shard_map.74 = (f32[512,256]{1,0:T(8,128)S(1)}, f32[32,256]{1,0:T(8,128)S(1)}, f32[32,256]{1,0:T(8,128)S(1)}, f32[512,16]{1,0:T(8,128)S(1)}, f32[16,16]{1,0:T(8,128)S(1)}, /*index=5*/f32[16,16]{1,0:T(8,128)S(1)}) custom-call(s32[32]{0:T(128)S(1)} %copy-done.5, s32[1,32]{1,0:T(1,128)S(1)} %bitcast.10, ...), custom_call_target="tpu_custom_call" | custom-call | flops 6291456000 | bytes 8388608 | tf_op jit(solution)/shard_map/pallas_call | solution.py:142
  9.4 0.0 collective-permute-done.first_ref
  9.4 0.0 collective-permute-done.1.second_ref
  9.4 0.2 shard_map.75
  9.6 1.5 %collective-permute-start.2 = (f32[16,32,256]{2,1,0:T(8,128)S(1)}, f32[16,32,256]{2,1,0:T(8,128)S(1)}, u32[]{:S(2)}, u32[]{:S(2)}) collective-permute-start(f32[16,32,256]{2,1,0:T(8,128)S(1)} %get-tuple-element.80), channel_id=1, source_target_pairs={{0,16},{1,17},{2,18},{3,19},{4,20},{5,21},{6,22},{7,23},{8,24},{9,... | collective-permute-start | bytes 1572872 | tf_op jit(solution)/shard_map/ppermute | solution.py:496
  11.1 0.0 copy-done.3
  11.1 0.0 copy-done.4
  11.1 1.0 %shard_map.76 = (f32[32,256]{1,0:T(8,128)S(1)}, f32[32,256]{1,0:T(8,128)S(1)}, f32[32,256]{1,0:T(8,128)S(1)}) custom-call(s32[32]{0:T(128)S(1)} %copy-done.5, f32[2,16,16,256]{3,2,1,0:T(8,128)S(1)} %get-tuple-element.74.edge_ref, f32[32,256]{1,0:T(8,128)S(1)} %get-tuple-element.75.picks_ref, f32[1,32]{1,0:T(1,128)S(1)} %bitcast.8, f32[1,32]{1,0:T(1,128)S(1)} %bitcast.9), custom_call_target="tpu_custom_call" | custom-call | flops 819200000 | bytes 524288 | tf_op jit(solution)/shard_map/pallas_call | solution.py:220
  12.1 0.4 collective-permute-done.2.incoming_ref
  12.6 1.0 %shard_map.77 = bf16[40,256]{1,0:T(8,128)(2,1)S(1)} custom-call(s32[32]{0:T(128)S(1)} %copy-done.5, f32[32,256]{1,0:T(8,128)S(1)} %get-tuple-element.76.obs_ref, f32[32,256]{1,0:T(8,128)S(1)} %get-tuple-element.77.weight_ref, f32[32,256]{1,0:T(8,128)S(1)} %get-tuple-element.78.picks_ref, f32[32,256]{1,0:T(8,128)S(1)} %get-tuple-element.79.share_ref, ...), custom_call_target="tpu_custom_call" | custom-call | flops 327680000 | bytes 524288 | tf_op jit(solution)/shard_map/pallas_call | solution.py:254
  13.5 5.5 %collective-permute-start.3 = (bf16[40,256]{1,0:T(8,128)(2,1)S(1)}, bf16[40,256]{1,0:T(8,128)(2,1)S(1)}, u32[]{:S(2)}, u32[]{:S(2)}) collective-permute-start(bf16[40,256]{1,0:T(8,128)(2,1)S(1)} %shard_map.77), channel_id=1, source_target_pairs={{0,2},{1,3},{2,0},{3,1},{4,6},{5,7},{6,4},{7,5},{8,10},{9,11},{10,... | collective-permute-start | bytes 61448 | tf_op jit(solution)/shard_map/ppermute | solution.py:559
  19.0 1.3 %shard_map.78 = (bf16[4,16,32,256]{3,2,1,0:T(8,128)(2,1)S(1)}, f32[4,512,128]{2,1,0:T(8,128)S(1)}, f32[512,256]{1,0:T(8,128)S(1)}) custom-call(bf16[16,16,32,256]{3,2,1,0:T(8,128)(2,1)S(1)} %get-tuple-element.63.source_ref, bf16[16,16,32,256]{3,2,1,0:T(8,128)(2,1)S(1)} %copy-done, f32[512,16]{1,0:T(8,128)S(1)} %get-tuple-element.81.rate_ref, ...), custom_call_target="tpu_custom_call" | custom-call | flops 2097152000 | bytes 3145728 | tf_op jit(solution)/shard_map/pallas_call | solution.py:296
  20.4 0.4 collective-permute-done.3
  20.8 1.5 %collective-permute-start.4 = (bf16[80,256]{1,0:T(8,128)(2,1)S(1)}, bf16[80,256]{1,0:T(8,128)(2,1)S(1)}, u32[]{:S(2)}, u32[]{:S(2)}) collective-permute-start(bf16[80,256]{1,0:T(8,128)(2,1)S(1)} %constant_dynamic-update-slice_fusion), channel_id=1, source_target_pairs={{0,8},{1,9},{2,10},{3,11},{4,12},{5,13},{6,14},{7,15},{8,0},{9,1},... | collective-permute-start | bytes 122888 | tf_op jit(solution)/shard_map/ppermute | solution.py:559
  22.3 1.3 %shard_map.79 = (bf16[4,16,32,256]{3,2,1,0:T(8,128)(2,1)S(1)}, f32[4,512,128]{2,1,0:T(8,128)S(1)}, f32[512,256]{1,0:T(8,128)S(1)}) custom-call(bf16[16,16,32,256]{3,2,1,0:T(8,128)(2,1)S(1)} %get-tuple-element.63.source_ref, bf16[16,16,32,256]{3,2,1,0:T(8,128)(2,1)S(1)} %copy-done, f32[512,16]{1,0:T(8,128)S(1)} %get-tuple-element.81.rate_ref, ...), custom_call_target="tpu_custom_call" | custom-call | flops 2097152000 | bytes 3145728 | tf_op jit(solution)/shard_map/pallas_call | solution.py:296
  23.7 1.1 %collective-permute-done.4 = bf16[80,256]{1,0:T(8,128)(2,1)S(1)} collective-permute-done((bf16[80,256]{1,0:T(8,128)(2,1)S(1)}, bf16[80,256]{1,0:T(8,128)(2,1)S(1)}, u32[]{:S(2)}, u32[]{:S(2)}) %collective-permute-start.4) | collective-permute-done | bytes 40992 | tf_op jit(solution)/shard_map/ppermute | solution.py:559
  24.8 1.7 %collective-permute-start.5 = (bf16[160,256]{1,0:T(8,128)(2,1)S(1)}, bf16[160,256]{1,0:T(8,128)(2,1)S(1)}, u32[]{:S(2)}, u32[]{:S(2)}) collective-permute-start(bf16[160,256]{1,0:T(8,128)(2,1)S(1)} %constant_dynamic-update-slice_fusion.2), channel_id=1, source_target_pairs={{0,1},{1,0},{2,3},{3,2},{4,5},{5,4},{6,7},{7,6},{8,9},{9,8},{10,11... | collective-permute-start | bytes 245768 | tf_op jit(solution)/shard_map/ppermute | solution.py:559
  26.5 1.3 %shard_map.80 = (bf16[4,16,32,256]{3,2,1,0:T(8,128)(2,1)S(1)}, f32[4,512,128]{2,1,0:T(8,128)S(1)}, f32[512,256]{1,0:T(8,128)S(1)}) custom-call(bf16[16,16,32,256]{3,2,1,0:T(8,128)(2,1)S(1)} %get-tuple-element.63.source_ref, bf16[16,16,32,256]{3,2,1,0:T(8,128)(2,1)S(1)} %copy-done, f32[512,16]{1,0:T(8,128)S(1)} %get-tuple-element.81.rate_ref, ...), custom_call_target="tpu_custom_call" | custom-call | flops 2097152000 | bytes 3145728 | tf_op jit(solution)/shard_map/pallas_call | solution.py:296
  27.9 1.5 %collective-permute-done.5 = bf16[160,256]{1,0:T(8,128)(2,1)S(1)} collective-permute-done((bf16[160,256]{1,0:T(8,128)(2,1)S(1)}, bf16[160,256]{1,0:T(8,128)(2,1)S(1)}, u32[]{:S(2)}, u32[]{:S(2)}) %collective-permute-start.5) | collective-permute-done | bytes 81952 | tf_op jit(solution)/shard_map/ppermute | solution.py:559
  29.4 1.5 %collective-permute-start.6 = (bf16[320,256]{1,0:T(8,128)(2,1)S(1)}, bf16[320,256]{1,0:T(8,128)(2,1)S(1)}, u32[]{:S(2)}, u32[]{:S(2)}) collective-permute-start(bf16[320,256]{1,0:T(8,128)(2,1)S(1)} %constant_dynamic-update-slice_fusion.4), channel_id=1, source_target_pairs={{0,4},{1,5},{2,6},{3,7},{4,0},{5,1},{6,2},{7,3},{8,12},{9,13},{10,... | collective-permute-start | bytes 491528 | tf_op jit(solution)/shard_map/ppermute | solution.py:559
  30.9 0.0 copy-start.2
  30.9 2.0 %shard_map.81 = (bf16[4,16,32,256]{3,2,1,0:T(8,128)(2,1)S(1)}, f32[4,512,128]{2,1,0:T(8,128)S(1)}, f32[512,256]{1,0:T(8,128)}) custom-call(bf16[16,16,32,256]{3,2,1,0:T(8,128)(2,1)S(1)} %get-tuple-element.63.source_ref, bf16[16,16,32,256]{3,2,1,0:T(8,128)(2,1)S(1)} %copy-done, f32[512,16]{1,0:T(8,128)S(1)} %get-tuple-element.81.rate_ref, ...), custom_call_target="tpu_custom_call" | custom-call | flops 2097152000 | bytes 3145728 | tf_op jit(solution)/shard_map/pallas_call | solution.py:296
  32.9 1.8 %collective-permute-done.6 = bf16[320,256]{1,0:T(8,128)(2,1)S(1)} collective-permute-done((bf16[320,256]{1,0:T(8,128)(2,1)S(1)}, bf16[320,256]{1,0:T(8,128)(2,1)S(1)}, u32[]{:S(2)}, u32[]{:S(2)}) %collective-permute-start.6) | collective-permute-done | bytes 163872 | tf_op jit(solution)/shard_map/ppermute | solution.py:559
  34.7 0.1 collective-permute-start.7
  34.8 0.0 copy-done.2
  34.8 0.6 shard_map.82
  35.4 1.0 %collective-permute-done.7.rows_ref = bf16[640,256]{1,0:T(8,128)(2,1)S(1)} collective-permute-done((bf16[640,256]{1,0:T(8,128)(2,1)S(1)}, bf16[640,256]{1,0:T(8,128)(2,1)S(1)}, u32[]{:S(2)}, u32[]{:S(2)}) %collective-permute-start.7) | collective-permute-done | bytes 327712 | tf_op jit(solution)/shard_map/ppermute | solution.py:571
  36.4 42.8 %shard_map.83 = bf16[16,16,32,256]{3,2,1,0:T(8,128)(2,1)} custom-call(bf16[640,256]{1,0:T(8,128)(2,1)S(1)} %collective-permute-done.7.rows_ref, f32[256,256]{1,0:T(8,128)S(1)} %get-tuple-element.109.gram_ref, f32[16,256]{1,0:T(8,128)S(1)} %get-tuple-element.110.pieces_ref, bf16[256,256]{1,0:T(8,128)(2,1)S(1)} %get-tuple-element.111.select_ref, ...), custom_call_target="tpu_custom_call" | custom-call | flops 8388608000 | bytes 10485760 | tf_op jit(solution)/shard_map/pallas_call | solution.py:471
  (8 shorter events, 0.1 us)
Async XLA Ops:
  0.0 6.2 %copy-start.5 = (s32[32]{0:T(128)S(1)}, s32[32]{0:T(128)}, u32[]{:S(2)}) copy-start(s32[32]{0:T(128)} %rows_ref.5) | copy-start | bytes 388
  0.0 6.2 %copy-start.1 = (f32[16,16,32]{2,1,0:T(8,128)S(1)}, f32[16,16,32]{2,1,0:T(8,128)}, u32[]{:S(2)}) copy-start(f32[16,16,32]{2,1,0:T(8,128)} %recovery_ref.1) | copy-start | bytes 98308
  0.0 6.2 %copy-start = (bf16[16,16,32,256]{3,2,1,0:T(8,128)(2,1)S(1)}, bf16[16,16,32,256]{3,2,1,0:T(8,128)(2,1)}, u32[]{:S(2)}) copy-start(bf16[16,16,32,256]{3,2,1,0:T(8,128)(2,1)} %inflow_ref.4) | copy-start | bytes 12582916
  2.5 6.9 %collective-permute-start = (bf16[16,16,256]{2,1,0:T(8,128)(2,1)S(1)}, bf16[16,16,256]{2,1,0:T(8,128)(2,1)S(1)}, u32[]{:S(2)}, u32[]{:S(2)}) collective-permute-start(bf16[16,16,256]{2,1,0:T(8,128)(2,1)S(1)} %get-tuple-element.67), channel_id=1, source_target_pairs={{0,1},{2,3},{1,0},{3,2},{4,5},{6,7},{5,4},{7,6},{8,9},{10,11},{9,8... | collective-permute-start | bytes 393224 | tf_op jit(solution)/shard_map/ppermute | solution.py:545
  5.6 3.8 %collective-permute-start.1 = (bf16[16,16,256]{2,1,0:T(8,128)(2,1)S(1)}, bf16[16,16,256]{2,1,0:T(8,128)(2,1)S(1)}, u32[]{:S(2)}, u32[]{:S(2)}) collective-permute-start(bf16[16,16,256]{2,1,0:T(8,128)(2,1)S(1)} %get-tuple-element.68), channel_id=1, source_target_pairs={{1,2},{2,1},{5,6},{6,5},{9,10},{10,9},{13,14},{14,13},{17,18},{18,... | collective-permute-start | bytes 393224 | tf_op jit(solution)/shard_map/ppermute | solution.py:546
  6.2 4.8 %copy-start.3 = (f32[32]{0:T(128)S(1)}, f32[32]{0:T(128)}, u32[]{:S(2)}) copy-start(f32[32]{0:T(128)} %param.11) | copy-start | bytes 388
  6.3 4.8 %copy-start.4 = (f32[32]{0:T(128)S(1)}, f32[32]{0:T(128)}, u32[]{:S(2)}) copy-start(f32[32]{0:T(128)} %param.12) | copy-start | bytes 388
  9.6 3.0 %collective-permute-start.2 = (f32[16,32,256]{2,1,0:T(8,128)S(1)}, f32[16,32,256]{2,1,0:T(8,128)S(1)}, u32[]{:S(2)}, u32[]{:S(2)}) collective-permute-start(f32[16,32,256]{2,1,0:T(8,128)S(1)} %get-tuple-element.80), channel_id=1, source_target_pairs={{0,16},{1,17},{2,18},{3,19},{4,20},{5,21},{6,22},{7,23},{8,24},{9,... | collective-permute-start | bytes 1572872 | tf_op jit(solution)/shard_map/ppermute | solution.py:496
  13.5 7.2 %collective-permute-start.3 = (bf16[40,256]{1,0:T(8,128)(2,1)S(1)}, bf16[40,256]{1,0:T(8,128)(2,1)S(1)}, u32[]{:S(2)}, u32[]{:S(2)}) collective-permute-start(bf16[40,256]{1,0:T(8,128)(2,1)S(1)} %shard_map.77), channel_id=1, source_target_pairs={{0,2},{1,3},{2,0},{3,1},{4,6},{5,7},{6,4},{7,5},{8,10},{9,11},{10,... | collective-permute-start | bytes 61448 | tf_op jit(solution)/shard_map/ppermute | solution.py:559
  20.8 4.0 %collective-permute-start.4 = (bf16[80,256]{1,0:T(8,128)(2,1)S(1)}, bf16[80,256]{1,0:T(8,128)(2,1)S(1)}, u32[]{:S(2)}, u32[]{:S(2)}) collective-permute-start(bf16[80,256]{1,0:T(8,128)(2,1)S(1)} %constant_dynamic-update-slice_fusion), channel_id=1, source_target_pairs={{0,8},{1,9},{2,10},{3,11},{4,12},{5,13},{6,14},{7,15},{8,0},{9,1},... | collective-permute-start | bytes 122888 | tf_op jit(solution)/shard_map/ppermute | solution.py:559
  24.8 4.6 %collective-permute-start.5 = (bf16[160,256]{1,0:T(8,128)(2,1)S(1)}, bf16[160,256]{1,0:T(8,128)(2,1)S(1)}, u32[]{:S(2)}, u32[]{:S(2)}) collective-permute-start(bf16[160,256]{1,0:T(8,128)(2,1)S(1)} %constant_dynamic-update-slice_fusion.2), channel_id=1, source_target_pairs={{0,1},{1,0},{2,3},{3,2},{4,5},{5,4},{6,7},{7,6},{8,9},{9,8},{10,11... | collective-permute-start | bytes 245768 | tf_op jit(solution)/shard_map/ppermute | solution.py:559
  29.4 5.3 %collective-permute-start.6 = (bf16[320,256]{1,0:T(8,128)(2,1)S(1)}, bf16[320,256]{1,0:T(8,128)(2,1)S(1)}, u32[]{:S(2)}, u32[]{:S(2)}) collective-permute-start(bf16[320,256]{1,0:T(8,128)(2,1)S(1)} %constant_dynamic-update-slice_fusion.4), channel_id=1, source_target_pairs={{0,4},{1,5},{2,6},{3,7},{4,0},{5,1},{6,2},{7,3},{8,12},{9,13},{10,... | collective-permute-start | bytes 491528 | tf_op jit(solution)/shard_map/ppermute | solution.py:559
  30.9 3.9 %copy-start.2 = (s32[256]{0:T(256)S(1)}, s32[256]{0:T(256)}, u32[]{:S(2)}) copy-start(s32[256]{0:T(256)} %param.13) | copy-start | bytes 3076
  34.7 1.7 %collective-permute-start.7 = (bf16[640,256]{1,0:T(8,128)(2,1)S(1)}, bf16[640,256]{1,0:T(8,128)(2,1)S(1)}, u32[]{:S(2)}, u32[]{:S(2)}) collective-permute-start(bf16[640,256]{1,0:T(8,128)(2,1)S(1)} %constant_dynamic-update-slice_fusion.6.rows_ref), channel_id=1, source_target_pairs={{0,16},{1,17},{2,18},{3,19},{4,20},{5,21},{6,22},{7,23},{8,24},{9,... | collective-permute-start | bytes 983048 | tf_op jit(solution)/shard_map/ppermute | solution.py:571

commit v7 on v6

--- a/solution.py
+++ b/solution.py
@@ -29,9 +29,9 @@
     return pl.CostEstimate(flops=1000 * elements, bytes_accessed=nbytes, transcendentals=0)
 
 
-def border_kernel(parity_ref, source_ref, held_ref, first_ref, second_ref, sems):
+def border_kernel(place_ref, source_ref, held_ref, first_ref, second_ref, sems):
     planes, span, height, _ = source_ref.shape
-    even = parity_ref[0] == 0
+    even = lax.bitwise_and(place_ref[0], 1) == 0
 
     def fetch(p):
         return pltpu.make_async_copy(source_ref.at[p], held_ref.at[p], sems.at[p])
@@ -48,7 +48,7 @@
         second_ref[p] = jnp.where(even, low, top).astype(jnp.bfloat16)
 
 
-def border(source, parity):
+def border(source, place):
     planes, span, height, members = source.shape
     vmem = pl.BlockSpec(memory_space=pltpu.VMEM)
     row = jax.ShapeDtypeStruct((planes, span, members), jnp.bfloat16)
@@ -60,12 +60,20 @@
         scratch_shapes=[pltpu.SemaphoreType.DMA((planes,))],
         compiler_params=params(LIMIT),
         cost_estimate=cost(source.size, source.size),
-    )(parity, pltpu.with_memory_space_constraint(source, pltpu.HBM))
+    )(place, pltpu.with_memory_space_constraint(source, pltpu.HBM))
+
+
+def parted(value, size):
+    if size & (size - 1):
+        return lax.div(value, size), lax.rem(value, size)
+    return lax.shift_right_logical(value, size.bit_length() - 1), lax.bitwise_and(value, size - 1)
 
 
 def place_of(r, shape):
     _, span, height = shape
-    return r // (span * height), r // height % span, r % height
+    rest, b = parted(r, height)
+    p, a = parted(rest, span)
+    return p, a, b
 
 
 def group_of(span, height):
@@ -119,13 +127,13 @@
     end_ref[...] = deficits[planes - 1]
     for k in range(count):
         p, a, b = place_of(rows_ref[k], shape)
-        first = pl.multiple_of(b // 16 * 16, 16)
+        first = pl.multiple_of(b - lax.bitwise_and(b, 15), 16)
         tiles[k] = inflow_ref[p, a, pl.ds(first, 16), :].astype(jnp.float32)
         through_rows[pl.ds(k, 1), :] = through[p, pl.ds(a, 1), :]
     for k in range(count):
         p, a, b = place_of(rows_ref[k], shape)
         picks_ref[pl.ds(k, 1), :] = (
-            tiles[k, pl.ds(b % 16, 1), :] - deficits[p, pl.ds(a * height + b, 1), :]
+            tiles[k, pl.ds(lax.bitwise_and(b, 15), 1), :] - deficits[p, pl.ds(a * height + b, 1), :]
         )
     cell = upright(rows_row_ref[...].astype(jnp.float32)).astype(jnp.int32) % height
     lane = lax.broadcasted_iota(jnp.int32, (count, height), 1)
@@ -163,11 +171,11 @@
 
 
 def edge_kernel(
-    parity_ref, first_ref, second_ref, low_rate_ref, high_rate_ref, end_ref, term_ref, edge_ref, leaving_ref
+    place_ref, first_ref, second_ref, low_rate_ref, high_rate_ref, end_ref, term_ref, edge_ref, leaving_ref
 ):
     planes, span, members = first_ref.shape
     height = leaving_ref.shape[1]
-    even = parity_ref[0] == 0
+    even = lax.bitwise_and(place_ref[0], 1) == 0
     low, high = None, None
     for p in range(planes):
         one = vertical_mix * first_ref[p].astype(jnp.float32)
@@ -186,7 +194,7 @@
         leaving_ref[a] = end_ref[a * height : (a + 1) * height] + share
 
 
-def edge_march(parity, first, second, low_rate, high_rate, end):
+def edge_march(place, first, second, low_rate, high_rate, end):
     planes, span, members = first.shape
     vmem = pl.BlockSpec(memory_space=pltpu.VMEM)
     return pl.pallas_call(
@@ -200,66 +208,81 @@
         ],
         compiler_params=params(LIMIT),
         cost_estimate=cost(first.size, 8 * first.size),
-    )(parity, first, second, low_rate, high_rate, end)
-
-
-def prepare_kernel(height, rows_ref, edge_ref, picks_ref, obs_ref, weight_ref, out_ref, obs_out_ref, weight_out_ref):
+    )(place, first, second, low_rate, high_rate, end)
+
+
+def payload(forecast, obs, weight):
+    members = forecast.shape[1]
+    mean = jnp.sum(forecast, axis=1, keepdims=True) * (1.0 / members)
+    anomaly = (forecast - mean).astype(jnp.bfloat16).astype(jnp.float32)
+    observed = weight * anomaly
+    misfit = weight * (obs - mean)
+    projection = jnp.sum(observed * misfit, axis=0, keepdims=True)
+    one = projection.astype(jnp.bfloat16).astype(jnp.float32)
+    two = (projection - one).astype(jnp.bfloat16).astype(jnp.float32)
+    three = projection - one - two
+    row = lax.broadcasted_iota(jnp.int32, (EXTRA, members), 0)
+    pieces = jnp.where(row == 0, one, jnp.where(row == 1, two, jnp.where(row == 2, three, 0.0)))
+    return jnp.concatenate([observed, pieces], axis=0).astype(jnp.bfloat16)
+
+
+def prepare_kernel(
+    height, rows_ref, edge_ref, picks_ref, obs_ref, weight_ref, out_ref, obs_out_ref, weight_out_ref, first_ref
+):
     _, planes, span, _ = edge_ref.shape
     for k in range(picks_ref.shape[0]):
         p, a, b = place_of(rows_ref[k], (planes, span, height))
         side = jnp.where(b == height - 1, 1, 0)
         at_edge = jnp.where((b == 0) | (b == height - 1), 1.0, 0.0)
         out_ref[pl.ds(k, 1), :] = picks_ref[pl.ds(k, 1), :] - at_edge * edge_ref[side, p, pl.ds(a, 1), :]
-    obs_out_ref[...] = jnp.broadcast_to(upright(obs_ref[...]), obs_out_ref.shape)
-    weight_out_ref[...] = jnp.broadcast_to(upright(weight_ref[...]), weight_out_ref.shape)
+    obs, weight = upright(obs_ref[...]), upright(weight_ref[...])
+    obs_out_ref[...] = jnp.broadcast_to(obs, obs_out_ref.shape)
+    weight_out_ref[...] = jnp.broadcast_to(weight, weight_out_ref.shape)
+    first_ref[...] = payload(out_ref[...], obs, weight)
 
 
 def prepare(obs_rows, obs, weight, picks, edge, height):
+    count, members = picks.shape
     vmem = pl.BlockSpec(memory_space=pltpu.VMEM)
     out = jax.ShapeDtypeStruct(picks.shape, jnp.float32)
     return pl.pallas_call(
         functools.partial(prepare_kernel, height),
         in_specs=[pl.BlockSpec(memory_space=pltpu.SMEM)] + [vmem] * 4,
-        out_specs=[vmem] * 3,
-        out_shape=[out] * 3,
+        out_specs=[vmem] * 4,
+        out_shape=[out] * 3 + [jax.ShapeDtypeStruct((count + EXTRA, members), jnp.bfloat16)],
         compiler_params=params(LIMIT),
         cost_estimate=cost(100 * picks.size, 64 * picks.size),
     )(obs_rows, edge, picks, obs[None, :], weight[None, :])
 
 
-def observe_kernel(rows_ref, obs_ref, weight_ref, picks_ref, share_ref, incoming_ref, out_ref, arriving):
-    span, height, members = incoming_ref.shape
-    count = picks_ref.shape[0]
-    for k in range(count):
-        _, a, b = place_of(rows_ref[k], (0, span, height))
-        arriving[pl.ds(k, 1), :] = incoming_ref[a, pl.ds(b, 1), :]
-    forecast = picks_ref[...] - share_ref[...] * arriving[...]
-    mean = jnp.sum(forecast, axis=1, keepdims=True) * (1.0 / members)
-    anomaly = (forecast - mean).astype(jnp.bfloat16).astype(jnp.float32)
-    weight = weight_ref[...]
-    observed = weight * anomaly
-    misfit = weight * (obs_ref[...] - mean)
-    projection = jnp.sum(observed * misfit, axis=0, keepdims=True)
-    one = projection.astype(jnp.bfloat16).astype(jnp.float32)
-    two = (projection - one).astype(jnp.bfloat16).astype(jnp.float32)
-    three = projection - one - two
-    row = lax.broadcasted_iota(jnp.int32, (EXTRA, members), 0)
-    pieces = jnp.where(row == 0, one, jnp.where(row == 1, two, jnp.where(row == 2, three, 0.0)))
-    out_ref[...] = jnp.concatenate([observed, pieces], axis=0).astype(jnp.bfloat16)
-
-
-def observe(obs_rows, obs, weight, picks, share, incoming):
+def observe_kernel(
+    place_ref, rows_ref, obs_ref, weight_ref, picks_ref, share_ref, first_ref, incoming_ref, out_ref, arriving
+):
+    @pl.when(place_ref[0] < 2)
+    def _():
+        out_ref[...] = first_ref[...]
+
+    @pl.when(place_ref[0] >= 2)
+    def _():
+        for k in range(picks_ref.shape[0]):
+            _, a, b = place_of(rows_ref[k], (0,) + incoming_ref.shape[:2])
+            arriving[pl.ds(k, 1), :] = incoming_ref[a, pl.ds(b, 1), :]
+        forecast = picks_ref[...] - share_ref[...] * arriving[...]
+        out_ref[...] = payload(forecast, obs_ref[...], weight_ref[...])
+
+
+def observe(place, obs_rows, obs, weight, picks, share, first, incoming):
     count, members = picks.shape
-    vmem = pl.BlockSpec(memory_space=pltpu.VMEM)
+    vmem, smem = pl.BlockSpec(memory_space=pltpu.VMEM), pl.BlockSpec(memory_space=pltpu.SMEM)
     return pl.pallas_call(
         observe_kernel,
-        in_specs=[pl.BlockSpec(memory_space=pltpu.SMEM)] + [vmem] * 5,
+        in_specs=[smem, smem] + [vmem] * 6,
         out_specs=vmem,
         out_shape=jax.ShapeDtypeStruct((count + EXTRA, members), jnp.bfloat16),
         scratch_shapes=[pltpu.VMEM((count, members), jnp.float32)],
         compiler_params=params(LIMIT),
         cost_estimate=cost(40 * count * members, 64 * count * members),
-    )(obs_rows, obs, weight, picks, share, incoming)
+    )(place, obs_rows, obs, weight, picks, share, first, incoming)
 
 
 def anomaly_kernel(start, planes, source_ref, inflow_ref, rate_ref, state_ref, term_ref, *refs):
@@ -503,7 +526,7 @@
     steps = []
     for axis in ("height", "span"):
         bits = (lax.axis_size(axis) - 1).bit_length()
-        steps.append([(axis, 1 << bit) for bit in reversed(range(bits))])
+        steps.append([(axis, (2 << bit) - 1 if axis == "height" else 1 << bit) for bit in reversed(range(bits))])
     mixed = []
     while steps[0] or steps[1]:
         pair = [axis.pop(0) for axis in steps if axis]
@@ -536,21 +559,21 @@
 def shards(source, inflow, recovery, obs_rows, obs, observation_weight, member_order):
     planes, span, height, members = source.shape
     levels = lax.axis_size("height")
-    parity = (lax.axis_index("height") % 2)[None]
+    place = (lax.axis_index("height") % 2 + 2 * lax.axis_index("stream"))[None]
     together = lax.optimization_barrier
 
-    source, first, second = border(source, parity)
+    source, first, second = border(source, place)
     inflow, first = together((inflow, first))
     inflow = pltpu.with_memory_space_constraint(inflow, pltpu.VMEM)
     first = lax.ppermute(first, "height", pairs(levels, 0))
     second = lax.ppermute(second, "height", pairs(levels, 1))
     end, picks, share, rates, low_rate, high_rate = march(source, inflow, recovery, obs_rows)
     end, first, second = together((end, first, second))
-    term, edge, leaving = edge_march(parity, first, second, low_rate, high_rate, end)
+    term, edge, leaving = edge_march(place, first, second, low_rate, high_rate, end)
     total = jnp.prod(recovery, axis=0)[..., None] if lax.axis_size("stream") > 2 else None
     incoming = downstream(leaving, total)
-    picks, obs, weight = prepare(obs_rows, obs, observation_weight, picks, edge, height)
-    rows = observe(obs_rows, obs, weight, picks, share, incoming)
+    picks, obs, weight, first = prepare(obs_rows, obs, observation_weight, picks, edge, height)
+    rows = observe(place, obs_rows, obs, weight, picks, share, first, incoming)
     state = incoming.reshape(span * height, members)
     cuts = [planes * part // 16 for part in CUTS]
     parts = []

time: 79.3 us -> 78.5 us (0.990)
  Pallas kernels: 57.1 us -> 55.8 us
  transfers between devices with their start and end apart: 8 -> 8, of which waited for: 6 -> 7; matrix products, arithmetic and copies ran while one was open for 0% -> 0% of each run, Pallas kernels for 14% -> 12%
where the time goes in v7:
time: 78.5 us; the launch traced here: 78.3 us
  Pallas kernels  55.8 us (71%)
  starting transfers between devices  15.6 us (20%)
  waiting for transfers between devices  6.74 us (9%)
    pallas_call x1, Pallas kernels, updated(): pl.pallas_call(functools.partial(update_kernel, picked), in_specs=[vmem]...  42.8 us
    ppermute x4, starting transfers between devices, shards(): other = lax.ppermute(rows, AXES, pairing)  10.4 us
    pallas_call x4, Pallas kernels, anomalies(): pl.pallas_call(functools.partial(anomaly_kernel, start, planes), in_specs...  6.01 us
    ppermute x4, waiting for transfers between devices, shards(): other = lax.ppermute(rows, AXES, pairing)  4.68 us
    ppermute x1, starting transfers between devices, shards(): first = lax.ppermute(first, 'height', pairs(levels, 0))  3.1 us
    pallas_call x1, Pallas kernels, border(): pl.pallas_call(border_kernel, in_specs=[pl.BlockSpec(memory_space=pltpu.S...  2.44 us
    pallas_call x1, Pallas kernels, march(): pl.pallas_call(march_kernel, in_specs=[pl.BlockSpec(memory_space=pltpu.SM...  2.33 us
  transfers between devices with their start and end apart: 8, of which 7 were waited for; matrix products, arithmetic and copies ran while one was open for 0% of the time, Pallas kernels for 12%

profile of v7, /device:TPU:0, one launch (start us, length us, event | category | flops | bytes accessed | tf_op | source)
XLA Modules:
  0.0 78.3 jit_solution(5638163841901118718)
XLA Ops:
  0.0 0.0 copy-start.5
  0.0 0.0 copy-start.1
  0.0 0.0 copy-start
  0.0 2.4 %shard_map.73 = (bf16[16,16,32,256]{3,2,1,0:T(8,128)(2,1)S(1)}, bf16[16,16,256]{2,1,0:T(8,128)(2,1)S(1)}, bf16[16,16,256]{2,1,0:T(8,128)(2,1)S(1)}) custom-call(s32[1]{0:T(128)} %bitcast.place_ref, bf16[16,16,32,256]{3,2,1,0:T(8,128)(2,1)} %source_ref.1), custom_call_target="tpu_custom_call" | custom-call | flops 2097152000 | bytes 2097152 | tf_op jit(solution)/shard_map/pallas_call | solution.py:55
  2.5 3.1 %collective-permute-start = (bf16[16,16,256]{2,1,0:T(8,128)(2,1)S(1)}, bf16[16,16,256]{2,1,0:T(8,128)(2,1)S(1)}, u32[]{:S(2)}, u32[]{:S(2)}) collective-permute-start(bf16[16,16,256]{2,1,0:T(8,128)(2,1)S(1)} %get-tuple-element.68), channel_id=1, source_target_pairs={{0,1},{2,3},{1,0},{3,2},{4,5},{6,7},{5,4},{7,6},{8,9},{10,11},{9,8... | collective-permute-start | bytes 393224 | tf_op jit(solution)/shard_map/ppermute | solution.py:568
  5.6 0.7 collective-permute-start.1
  6.2 0.0 copy-done.5
  6.2 0.0 copy-done.1
  6.2 0.0 copy-done
  6.3 0.0 copy-start.3
  6.3 0.0 copy-start.4
  6.3 2.3 %shard_map.74 = (f32[512,256]{1,0:T(8,128)S(1)}, f32[32,256]{1,0:T(8,128)S(1)}, f32[32,256]{1,0:T(8,128)S(1)}, f32[512,16]{1,0:T(8,128)S(1)}, f32[16,16]{1,0:T(8,128)S(1)}, /*index=5*/f32[16,16]{1,0:T(8,128)S(1)}) custom-call(s32[32]{0:T(128)S(1)} %copy-done.5, s32[1,32]{1,0:T(1,128)S(1)} %bitcast.10, ...), custom_call_target="tpu_custom_call" | custom-call | flops 6291456000 | bytes 8388608 | tf_op jit(solution)/shard_map/pallas_call | solution.py:150
  8.6 0.4 collective-permute-done.first_ref
  9.1 0.0 collective-permute-done.1.second_ref
  9.1 0.2 shard_map.75
  9.2 1.3 %collective-permute-start.2 = (f32[16,32,256]{2,1,0:T(8,128)S(1)}, f32[16,32,256]{2,1,0:T(8,128)S(1)}, u32[]{:S(2)}, u32[]{:S(2)}) collective-permute-start(f32[16,32,256]{2,1,0:T(8,128)S(1)} %get-tuple-element.82), channel_id=1, source_target_pairs={{0,16},{1,17},{2,18},{3,19},{4,20},{5,21},{6,22},{7,23},{8,24},{9,... | collective-permute-start | bytes 1572872 | tf_op jit(solution)/shard_map/ppermute | solution.py:519
  10.6 0.0 copy-done.3
  10.6 0.0 copy-done.4
  10.6 0.8 %shard_map.76 = (f32[32,256]{1,0:T(8,128)S(1)}, f32[32,256]{1,0:T(8,128)S(1)}, f32[32,256]{1,0:T(8,128)S(1)}, bf16[40,256]{1,0:T(8,128)(2,1)S(1)}) custom-call(s32[32]{0:T(128)S(1)} %copy-done.5, f32[2,16,16,256]{3,2,1,0:T(8,128)S(1)} %get-tuple-element.75.edge_ref, f32[32,256]{1,0:T(8,128)S(1)} %get-tuple-element.76.picks_ref, f32[1,32]{1,0:T(1,128)S(1)} %bitcast.8, ...), custom_call_target="tpu_custom_call" | custom-call | flops 819200000 | bytes 524288 | tf_op jit(solution)/shard_map/pallas_call | solution.py:248
  11.4 0.6 collective-permute-done.2.incoming_ref
  12.1 0.6 shard_map.77
  12.6 3.8 %collective-permute-start.3 = (bf16[40,256]{1,0:T(8,128)(2,1)S(1)}, bf16[40,256]{1,0:T(8,128)(2,1)S(1)}, u32[]{:S(2)}, u32[]{:S(2)}) collective-permute-start(bf16[40,256]{1,0:T(8,128)(2,1)S(1)} %shard_map.77), channel_id=1, source_target_pairs={{0,3},{1,2},{2,1},{3,0},{4,7},{5,6},{6,5},{7,4},{8,11},{9,10},{10,... | collective-permute-start | bytes 61448 | tf_op jit(solution)/shard_map/ppermute | solution.py:582
  16.5 1.3 %shard_map.78 = (bf16[4,16,32,256]{3,2,1,0:T(8,128)(2,1)S(1)}, f32[4,512,128]{2,1,0:T(8,128)S(1)}, f32[512,256]{1,0:T(8,128)S(1)}) custom-call(bf16[16,16,32,256]{3,2,1,0:T(8,128)(2,1)S(1)} %get-tuple-element.64.source_ref, bf16[16,16,32,256]{3,2,1,0:T(8,128)(2,1)S(1)} %copy-done, f32[512,16]{1,0:T(8,128)S(1)} %get-tuple-element.83.rate_ref, ...), custom_call_target="tpu_custom_call" | custom-call | flops 2097152000 | bytes 3145728 | tf_op jit(solution)/shard_map/pallas_call | solution.py:319
  17.8 0.5 collective-permute-done.3
  18.3 1.7 %collective-permute-start.4 = (bf16[80,256]{1,0:T(8,128)(2,1)S(1)}, bf16[80,256]{1,0:T(8,128)(2,1)S(1)}, u32[]{:S(2)}, u32[]{:S(2)}) collective-permute-start(bf16[80,256]{1,0:T(8,128)(2,1)S(1)} %constant_dynamic-update-slice_fusion), channel_id=1, source_target_pairs={{0,8},{1,9},{2,10},{3,11},{4,12},{5,13},{6,14},{7,15},{8,0},{9,1},... | collective-permute-start | bytes 122888 | tf_op jit(solution)/shard_map/ppermute | solution.py:582
  20.0 1.3 %shard_map.79 = (bf16[4,16,32,256]{3,2,1,0:T(8,128)(2,1)S(1)}, f32[4,512,128]{2,1,0:T(8,128)S(1)}, f32[512,256]{1,0:T(8,128)S(1)}) custom-call(bf16[16,16,32,256]{3,2,1,0:T(8,128)(2,1)S(1)} %get-tuple-element.64.source_ref, bf16[16,16,32,256]{3,2,1,0:T(8,128)(2,1)S(1)} %copy-done, f32[512,16]{1,0:T(8,128)S(1)} %get-tuple-element.83.rate_ref, ...), custom_call_target="tpu_custom_call" | custom-call | flops 2097152000 | bytes 3145728 | tf_op jit(solution)/shard_map/pallas_call | solution.py:319
  21.3 1.0 %collective-permute-done.4 = bf16[80,256]{1,0:T(8,128)(2,1)S(1)} collective-permute-done((bf16[80,256]{1,0:T(8,128)(2,1)S(1)}, bf16[80,256]{1,0:T(8,128)(2,1)S(1)}, u32[]{:S(2)}, u32[]{:S(2)}) %collective-permute-start.4) | collective-permute-done | bytes 40992 | tf_op jit(solution)/shard_map/ppermute | solution.py:582
  22.3 3.4 %collective-permute-start.5 = (bf16[160,256]{1,0:T(8,128)(2,1)S(1)}, bf16[160,256]{1,0:T(8,128)(2,1)S(1)}, u32[]{:S(2)}, u32[]{:S(2)}) collective-permute-start(bf16[160,256]{1,0:T(8,128)(2,1)S(1)} %constant_dynamic-update-slice_fusion.2), channel_id=1, source_target_pairs={{0,1},{1,0},{2,3},{3,2},{4,5},{5,4},{6,7},{7,6},{8,9},{9,8},{10,11... | collective-permute-start | bytes 245768 | tf_op jit(solution)/shard_map/ppermute | solution.py:582
  25.7 1.3 %shard_map.80 = (bf16[4,16,32,256]{3,2,1,0:T(8,128)(2,1)S(1)}, f32[4,512,128]{2,1,0:T(8,128)S(1)}, f32[512,256]{1,0:T(8,128)S(1)}) custom-call(bf16[16,16,32,256]{3,2,1,0:T(8,128)(2,1)S(1)} %get-tuple-element.64.source_ref, bf16[16,16,32,256]{3,2,1,0:T(8,128)(2,1)S(1)} %copy-done, f32[512,16]{1,0:T(8,128)S(1)} %get-tuple-element.83.rate_ref, ...), custom_call_target="tpu_custom_call" | custom-call | flops 2097152000 | bytes 3145728 | tf_op jit(solution)/shard_map/pallas_call | solution.py:319
  27.0 1.5 %collective-permute-done.5 = bf16[160,256]{1,0:T(8,128)(2,1)S(1)} collective-permute-done((bf16[160,256]{1,0:T(8,128)(2,1)S(1)}, bf16[160,256]{1,0:T(8,128)(2,1)S(1)}, u32[]{:S(2)}, u32[]{:S(2)}) %collective-permute-start.5) | collective-permute-done | bytes 81952 | tf_op jit(solution)/shard_map/ppermute | solution.py:582
  28.5 1.5 %collective-permute-start.6 = (bf16[320,256]{1,0:T(8,128)(2,1)S(1)}, bf16[320,256]{1,0:T(8,128)(2,1)S(1)}, u32[]{:S(2)}, u32[]{:S(2)}) collective-permute-start(bf16[320,256]{1,0:T(8,128)(2,1)S(1)} %constant_dynamic-update-slice_fusion.4), channel_id=1, source_target_pairs={{0,4},{1,5},{2,6},{3,7},{4,0},{5,1},{6,2},{7,3},{8,12},{9,13},{10,... | collective-permute-start | bytes 491528 | tf_op jit(solution)/shard_map/ppermute | solution.py:582
  30.0 0.0 copy-start.2
  30.0 2.0 %shard_map.81 = (bf16[4,16,32,256]{3,2,1,0:T(8,128)(2,1)S(1)}, f32[4,512,128]{2,1,0:T(8,128)S(1)}, f32[512,256]{1,0:T(8,128)}) custom-call(bf16[16,16,32,256]{3,2,1,0:T(8,128)(2,1)S(1)} %get-tuple-element.64.source_ref, bf16[16,16,32,256]{3,2,1,0:T(8,128)(2,1)S(1)} %copy-done, f32[512,16]{1,0:T(8,128)S(1)} %get-tuple-element.83.rate_ref, ...), custom_call_target="tpu_custom_call" | custom-call | flops 2097152000 | bytes 3145728 | tf_op jit(solution)/shard_map/pallas_call | solution.py:319
  32.0 1.8 %collective-permute-done.6 = bf16[320,256]{1,0:T(8,128)(2,1)S(1)} collective-permute-done((bf16[320,256]{1,0:T(8,128)(2,1)S(1)}, bf16[320,256]{1,0:T(8,128)(2,1)S(1)}, u32[]{:S(2)}, u32[]{:S(2)}) %collective-permute-start.6) | collective-permute-done | bytes 163872 | tf_op jit(solution)/shard_map/ppermute | solution.py:582
  33.8 0.1 collective-permute-start.7
  33.9 0.0 copy-done.2
  33.9 0.6 shard_map.82
  34.5 1.0 %collective-permute-done.7.rows_ref = bf16[640,256]{1,0:T(8,128)(2,1)S(1)} collective-permute-done((bf16[640,256]{1,0:T(8,128)(2,1)S(1)}, bf16[640,256]{1,0:T(8,128)(2,1)S(1)}, u32[]{:S(2)}, u32[]{:S(2)}) %collective-permute-start.7) | collective-permute-done | bytes 327712 | tf_op jit(solution)/shard_map/ppermute | solution.py:594
  35.5 42.8 %shard_map.83 = bf16[16,16,32,256]{3,2,1,0:T(8,128)(2,1)} custom-call(bf16[640,256]{1,0:T(8,128)(2,1)S(1)} %collective-permute-done.7.rows_ref, f32[256,256]{1,0:T(8,128)S(1)} %get-tuple-element.111.gram_ref, f32[16,256]{1,0:T(8,128)S(1)} %get-tuple-element.112.pieces_ref, bf16[256,256]{1,0:T(8,128)(2,1)S(1)} %get-tuple-element.113.select_ref, ...), custom_call_target="tpu_custom_call" | custom-call | flops 8388608000 | bytes 10485760 | tf_op jit(solution)/shard_map/pallas_call | solution.py:494
  (8 shorter events, 0.1 us)
Async XLA Ops:
  0.0 6.2 %copy-start.5 = (s32[32]{0:T(128)S(1)}, s32[32]{0:T(128)}, u32[]{:S(2)}) copy-start(s32[32]{0:T(128)} %rows_ref.5) | copy-start | bytes 388
  0.0 6.2 %copy-start.1 = (f32[16,16,32]{2,1,0:T(8,128)S(1)}, f32[16,16,32]{2,1,0:T(8,128)}, u32[]{:S(2)}) copy-start(f32[16,16,32]{2,1,0:T(8,128)} %recovery_ref.1) | copy-start | bytes 98308
  0.0 6.2 %copy-start = (bf16[16,16,32,256]{3,2,1,0:T(8,128)(2,1)S(1)}, bf16[16,16,32,256]{3,2,1,0:T(8,128)(2,1)}, u32[]{:S(2)}) copy-start(bf16[16,16,32,256]{3,2,1,0:T(8,128)(2,1)} %inflow_ref.4) | copy-start | bytes 12582916
  2.5 6.6 %collective-permute-start = (bf16[16,16,256]{2,1,0:T(8,128)(2,1)S(1)}, bf16[16,16,256]{2,1,0:T(8,128)(2,1)S(1)}, u32[]{:S(2)}, u32[]{:S(2)}) collective-permute-start(bf16[16,16,256]{2,1,0:T(8,128)(2,1)S(1)} %get-tuple-element.68), channel_id=1, source_target_pairs={{0,1},{2,3},{1,0},{3,2},{4,5},{6,7},{5,4},{7,6},{8,9},{10,11},{9,8... | collective-permute-start | bytes 393224 | tf_op jit(solution)/shard_map/ppermute | solution.py:568
  5.6 3.5 %collective-permute-start.1 = (bf16[16,16,256]{2,1,0:T(8,128)(2,1)S(1)}, bf16[16,16,256]{2,1,0:T(8,128)(2,1)S(1)}, u32[]{:S(2)}, u32[]{:S(2)}) collective-permute-start(bf16[16,16,256]{2,1,0:T(8,128)(2,1)S(1)} %get-tuple-element.69), channel_id=1, source_target_pairs={{1,2},{2,1},{5,6},{6,5},{9,10},{10,9},{13,14},{14,13},{17,18},{18,... | collective-permute-start | bytes 393224 | tf_op jit(solution)/shard_map/ppermute | solution.py:569
  6.3 4.3 %copy-start.3 = (f32[32]{0:T(128)S(1)}, f32[32]{0:T(128)}, u32[]{:S(2)}) copy-start(f32[32]{0:T(128)} %param.11) | copy-start | bytes 388
  6.3 4.3 %copy-start.4 = (f32[32]{0:T(128)S(1)}, f32[32]{0:T(128)}, u32[]{:S(2)}) copy-start(f32[32]{0:T(128)} %param.12) | copy-start | bytes 388
  9.2 2.8 %collective-permute-start.2 = (f32[16,32,256]{2,1,0:T(8,128)S(1)}, f32[16,32,256]{2,1,0:T(8,128)S(1)}, u32[]{:S(2)}, u32[]{:S(2)}) collective-permute-start(f32[16,32,256]{2,1,0:T(8,128)S(1)} %get-tuple-element.82), channel_id=1, source_target_pairs={{0,16},{1,17},{2,18},{3,19},{4,20},{5,21},{6,22},{7,23},{8,24},{9,... | collective-permute-start | bytes 1572872 | tf_op jit(solution)/shard_map/ppermute | solution.py:519
  12.6 5.6 %collective-permute-start.3 = (bf16[40,256]{1,0:T(8,128)(2,1)S(1)}, bf16[40,256]{1,0:T(8,128)(2,1)S(1)}, u32[]{:S(2)}, u32[]{:S(2)}) collective-permute-start(bf16[40,256]{1,0:T(8,128)(2,1)S(1)} %shard_map.77), channel_id=1, source_target_pairs={{0,3},{1,2},{2,1},{3,0},{4,7},{5,6},{6,5},{7,4},{8,11},{9,10},{10,... | collective-permute-start | bytes 61448 | tf_op jit(solution)/shard_map/ppermute | solution.py:582
  18.3 4.0 %collective-permute-start.4 = (bf16[80,256]{1,0:T(8,128)(2,1)S(1)}, bf16[80,256]{1,0:T(8,128)(2,1)S(1)}, u32[]{:S(2)}, u32[]{:S(2)}) collective-permute-start(bf16[80,256]{1,0:T(8,128)(2,1)S(1)} %constant_dynamic-update-slice_fusion), channel_id=1, source_target_pairs={{0,8},{1,9},{2,10},{3,11},{4,12},{5,13},{6,14},{7,15},{8,0},{9,1},... | collective-permute-start | bytes 122888 | tf_op jit(solution)/shard_map/ppermute | solution.py:582
  22.3 6.2 %collective-permute-start.5 = (bf16[160,256]{1,0:T(8,128)(2,1)S(1)}, bf16[160,256]{1,0:T(8,128)(2,1)S(1)}, u32[]{:S(2)}, u32[]{:S(2)}) collective-permute-start(bf16[160,256]{1,0:T(8,128)(2,1)S(1)} %constant_dynamic-update-slice_fusion.2), channel_id=1, source_target_pairs={{0,1},{1,0},{2,3},{3,2},{4,5},{5,4},{6,7},{7,6},{8,9},{9,8},{10,11... | collective-permute-start | bytes 245768 | tf_op jit(solution)/shard_map/ppermute | solution.py:582
  28.5 5.3 %collective-permute-start.6 = (bf16[320,256]{1,0:T(8,128)(2,1)S(1)}, bf16[320,256]{1,0:T(8,128)(2,1)S(1)}, u32[]{:S(2)}, u32[]{:S(2)}) collective-permute-start(bf16[320,256]{1,0:T(8,128)(2,1)S(1)} %constant_dynamic-update-slice_fusion.4), channel_id=1, source_target_pairs={{0,4},{1,5},{2,6},{3,7},{4,0},{5,1},{6,2},{7,3},{8,12},{9,13},{10,... | collective-permute-start | bytes 491528 | tf_op jit(solution)/shard_map/ppermute | solution.py:582
  30.0 3.9 %copy-start.2 = (s32[256]{0:T(256)S(1)}, s32[256]{0:T(256)}, u32[]{:S(2)}) copy-start(s32[256]{0:T(256)} %param.13) | copy-start | bytes 3076
  33.8 1.7 %collective-permute-start.7 = (bf16[640,256]{1,0:T(8,128)(2,1)S(1)}, bf16[640,256]{1,0:T(8,128)(2,1)S(1)}, u32[]{:S(2)}, u32[]{:S(2)}) collective-permute-start(bf16[640,256]{1,0:T(8,128)(2,1)S(1)} %constant_dynamic-update-slice_fusion.6.rows_ref), channel_id=1, source_target_pairs={{0,16},{1,17},{2,18},{3,19},{4,20},{5,21},{6,22},{7,23},{8,24},{9,... | collective-permute-start | bytes 983048 | tf_op jit(solution)/shard_map/ppermute | solution.py:594

commit v8 on v7

--- a/solution.py
+++ b/solution.py
@@ -29,38 +29,57 @@
     return pl.CostEstimate(flops=1000 * elements, bytes_accessed=nbytes, transcendentals=0)
 
 
-def border_kernel(place_ref, source_ref, held_ref, first_ref, second_ref, sems):
-    planes, span, height, _ = source_ref.shape
-    even = lax.bitwise_and(place_ref[0], 1) == 0
-
-    def fetch(p):
-        return pltpu.make_async_copy(source_ref.at[p], held_ref.at[p], sems.at[p])
-
-    for p in range(planes):
-        fetch(p).start()
-    for p in range(planes):
-        fetch(p).wait()
-        low = held_ref[p, :, :16].astype(jnp.float32)
-        top = held_ref[p, :, height - 16 :].astype(jnp.float32)
-        low = jnp.concatenate([low[a, :1] for a in range(span)], axis=0)
-        top = jnp.concatenate([top[a, 15:] for a in range(span)], axis=0)
-        first_ref[p] = jnp.where(even, top, low).astype(jnp.bfloat16)
-        second_ref[p] = jnp.where(even, low, top).astype(jnp.bfloat16)
-
-
-def border(source, place):
-    planes, span, height, members = source.shape
-    vmem = pl.BlockSpec(memory_space=pltpu.VMEM)
-    row = jax.ShapeDtypeStruct((planes, span, members), jnp.bfloat16)
-    return pl.pallas_call(
-        border_kernel,
-        in_specs=[pl.BlockSpec(memory_space=pltpu.SMEM), pl.BlockSpec(memory_space=pltpu.HBM)],
-        out_specs=[vmem] * 3,
-        out_shape=[pltpu.VMEM(source.shape, jnp.bfloat16), row, row],
-        scratch_shapes=[pltpu.SemaphoreType.DMA((planes,))],
-        compiler_params=params(LIMIT),
-        cost_estimate=cost(source.size, source.size),
-    )(place, pltpu.with_memory_space_constraint(source, pltpu.HBM))
+def take_border(out_ref, p, block, top):
+    span = block.shape[0]
+    block = block.astype(jnp.float32)
+    low = jnp.concatenate([block[a, :1] for a in range(span)], axis=0)
+    high = jnp.concatenate([block[a, 15:] for a in range(span)], axis=0)
+    out_ref[p] = jnp.where(top, high, low).astype(jnp.bfloat16)
+
+
+def first_border_kernel(place_ref, source_ref, out_ref, held, sems):
+    planes, _, height, _ = source_ref.shape
+    top = lax.bitwise_and(place_ref[0], 1) == 0
+    start = pl.multiple_of(jnp.where(top, height - 16, 0), 16)
+    step = planes // sems.shape[0]
+
+    def fetch(c):
+        part = pl.ds(c * step, step)
+        return pltpu.make_async_copy(source_ref.at[part, :, pl.ds(start, 16), :], held.at[part], sems.at[c])
+
+    for c in range(sems.shape[0]):
+        fetch(c).start()
+    for c in range(sems.shape[0]):
+        fetch(c).wait()
+        for p in range(c * step, (c + 1) * step):
+            take_border(out_ref, p, held[p], top)
+
+
+def second_border_kernel(place_ref, source_ref, out_ref):
+    height = source_ref.shape[2]
+    top = lax.bitwise_and(place_ref[0], 1) == 1
+    start = pl.multiple_of(jnp.where(top, height - 16, 0), 16)
+    for p in range(source_ref.shape[0]):
+        take_border(out_ref, p, source_ref[p, :, pl.ds(start, 16), :], top)
+
+
+def border(source, place, far):
+    planes, span, _, members = source.shape
+    count = 4 if planes % 4 == 0 else 1
+    vmem, hbm = pl.BlockSpec(memory_space=pltpu.VMEM), pl.BlockSpec(memory_space=pltpu.HBM)
+    scratch = [
+        pltpu.VMEM((planes, span, 16, members), jnp.bfloat16),
+        pltpu.SemaphoreType.DMA((count,)),
+    ]
+    return pl.pallas_call(
+        first_border_kernel if far else second_border_kernel,
+        in_specs=[pl.BlockSpec(memory_space=pltpu.SMEM), hbm if far else vmem],
+        out_specs=vmem,
+        out_shape=jax.ShapeDtypeStruct((planes, span, members), jnp.bfloat16),
+        scratch_shapes=scratch if far else [],
+        compiler_params=params(LIMIT),
+        cost_estimate=cost(source.size // 2, source.size),
+    )(place, source)
 
 
 def parted(value, size):
@@ -562,9 +581,11 @@
     place = (lax.axis_index("height") % 2 + 2 * lax.axis_index("stream"))[None]
     together = lax.optimization_barrier
 
-    source, first, second = border(source, place)
+    first = border(pltpu.with_memory_space_constraint(source, pltpu.HBM), place, True)
+    source = pltpu.with_memory_space_constraint(source, pltpu.VMEM)
     inflow, first = together((inflow, first))
     inflow = pltpu.with_memory_space_constraint(inflow, pltpu.VMEM)
+    second = border(source, place, False)
     first = lax.ppermute(first, "height", pairs(levels, 0))
     second = lax.ppermute(second, "height", pairs(levels, 1))
     end, picks, share, rates, low_rate, high_rate = march(source, inflow, recovery, obs_rows)

time: 78.5 us -> 77.6 us (0.989)
    pallas_call x1 -> x2, Pallas kernels: 2.44 us -> 2.19 us  [border(): pl.pallas_call(first_border_kernel if far else second_border_kernel, in_s...]
  transfers between devices with their start and end apart: 8 -> 8, of which waited for: 7 -> 6; matrix products, arithmetic and copies ran while one was open for 0% -> 0% of each run, Pallas kernels for 12% -> 13%
where the time goes in v8:
time: 77.6 us; the launch traced here: 77.5 us
  Pallas kernels  55.5 us (72%)
  starting transfers between devices  15.4 us (20%)
  waiting for transfers between devices  6.32 us (8%)
    pallas_call x1, Pallas kernels, updated(): pl.pallas_call(functools.partial(update_kernel, picked), in_specs=[vmem]...  42.8 us
    ppermute x4, starting transfers between devices, shards(): other = lax.ppermute(rows, AXES, pairing)  10 us
    pallas_call x4, Pallas kernels, anomalies(): pl.pallas_call(functools.partial(anomaly_kernel, start, planes), in_specs...  6.01 us
    ppermute x4, waiting for transfers between devices, shards(): other = lax.ppermute(rows, AXES, pairing)  4.67 us
    ppermute x1, starting transfers between devices, shards(): first = lax.ppermute(first, 'height', pairs(levels, 0))  3.1 us
    pallas_call x1, Pallas kernels, march(): pl.pallas_call(march_kernel, in_specs=[pl.BlockSpec(memory_space=pltpu.SM...  2.33 us
    pallas_call x2, Pallas kernels, border(): pl.pallas_call(first_border_kernel if far else second_border_kernel, in_s...  2.19 us
  transfers between devices with their start and end apart: 8, of which 6 were waited for; matrix products, arithmetic and copies ran while one was open for 0% of the time, Pallas kernels for 13%

profile of v8, /device:TPU:0, one launch (start us, length us, event | category | flops | bytes accessed | tf_op | source)
XLA Modules:
  0.0 77.5 jit_solution(13535452669033995737)
XLA Ops:
  0.0 0.0 copy-start
  0.0 0.0 copy-start.1
  0.0 0.0 copy-start.2
  0.0 0.0 copy-start.6
  0.0 1.8 %shard_map.73 = bf16[16,16,256]{2,1,0:T(8,128)(2,1)S(1)} custom-call(s32[1]{0:T(128)} %bitcast.place_ref, bf16[16,16,32,256]{3,2,1,0:T(8,128)(2,1)} %source_ref.13), custom_call_target="tpu_custom_call" | custom-call | flops 1048576000 | bytes 2097152 | tf_op jit(solution)/shard_map/pallas_call | solution.py:74
  1.8 3.1 %collective-permute-start = (bf16[16,16,256]{2,1,0:T(8,128)(2,1)S(1)}, bf16[16,16,256]{2,1,0:T(8,128)(2,1)S(1)}, u32[]{:S(2)}, u32[]{:S(2)}) collective-permute-start(bf16[16,16,256]{2,1,0:T(8,128)(2,1)S(1)} %shard_map.73), channel_id=1, source_target_pairs={{0,1},{2,3},{1,0},{3,2},{4,5},{6,7},{5,4},{7,6},{8,9},{10,11},{9,8... | collective-permute-start | bytes 393224 | tf_op jit(solution)/shard_map/ppermute | solution.py:589
  4.9 0.0 copy-done
  4.9 0.4 shard_map.75
  5.3 0.7 collective-permute-start.1
  6.0 0.0 copy-done.1
  6.0 0.0 copy-done.2
  6.0 0.0 copy-done.6
  6.0 0.0 copy-start.4
  6.0 0.0 copy-start.5
  6.0 2.3 %shard_map.74 = (f32[512,256]{1,0:T(8,128)S(1)}, f32[32,256]{1,0:T(8,128)S(1)}, f32[32,256]{1,0:T(8,128)S(1)}, f32[512,16]{1,0:T(8,128)S(1)}, f32[16,16]{1,0:T(8,128)S(1)}, /*index=5*/f32[16,16]{1,0:T(8,128)S(1)}) custom-call(s32[32]{0:T(128)S(1)} %copy-done.6, s32[1,32]{1,0:T(1,128)S(1)} %bitcast.10, bf16[16,16,32,256]{3,2,1,0:T(8,128)(2,1)S(1)} %copy-done, ...), custom_call_target="tpu_custom_call" | custom-call | flops 6291456000 | bytes 8388608 | tf_op jit(solution)/shard_map/pallas_call | solution.py:169
  8.4 0.0 collective-permute-done.first_ref
  8.4 0.0 collective-permute-done.1.second_ref
  8.4 0.2 shard_map.76
  8.6 1.5 %collective-permute-start.2 = (f32[16,32,256]{2,1,0:T(8,128)S(1)}, f32[16,32,256]{2,1,0:T(8,128)S(1)}, u32[]{:S(2)}, u32[]{:S(2)}) collective-permute-start(f32[16,32,256]{2,1,0:T(8,128)S(1)} %get-tuple-element.76), channel_id=1, source_target_pairs={{0,16},{1,17},{2,18},{3,19},{4,20},{5,21},{6,22},{7,23},{8,24},{9,... | collective-permute-start | bytes 1572872 | tf_op jit(solution)/shard_map/ppermute | solution.py:538
  10.1 0.0 copy-done.4
  10.1 0.0 copy-done.5
  10.1 0.8 %shard_map.77 = (f32[32,256]{1,0:T(8,128)S(1)}, f32[32,256]{1,0:T(8,128)S(1)}, f32[32,256]{1,0:T(8,128)S(1)}, bf16[40,256]{1,0:T(8,128)(2,1)S(1)}) custom-call(s32[32]{0:T(128)S(1)} %copy-done.6, f32[2,16,16,256]{3,2,1,0:T(8,128)S(1)} %get-tuple-element.69.edge_ref, f32[32,256]{1,0:T(8,128)S(1)} %get-tuple-element.70.picks_ref, f32[1,32]{1,0:T(1,128)S(1)} %bitcast.8, ...), custom_call_target="tpu_custom_call" | custom-call | flops 819200000 | bytes 524288 | tf_op jit(solution)/shard_map/pallas_call | solution.py:267
  11.0 0.6 collective-permute-done.2.incoming_ref
  11.6 0.6 shard_map.78
  12.2 3.7 %collective-permute-start.3 = (bf16[40,256]{1,0:T(8,128)(2,1)S(1)}, bf16[40,256]{1,0:T(8,128)(2,1)S(1)}, u32[]{:S(2)}, u32[]{:S(2)}) collective-permute-start(bf16[40,256]{1,0:T(8,128)(2,1)S(1)} %shard_map.78), channel_id=1, source_target_pairs={{0,3},{1,2},{2,1},{3,0},{4,7},{5,6},{6,5},{7,4},{8,11},{9,10},{10,... | collective-permute-start | bytes 61448 | tf_op jit(solution)/shard_map/ppermute | solution.py:603
  15.8 1.3 %shard_map.79 = (bf16[4,16,32,256]{3,2,1,0:T(8,128)(2,1)S(1)}, f32[4,512,128]{2,1,0:T(8,128)S(1)}, f32[512,256]{1,0:T(8,128)S(1)}) custom-call(bf16[16,16,32,256]{3,2,1,0:T(8,128)(2,1)S(1)} %copy-done, bf16[16,16,32,256]{3,2,1,0:T(8,128)(2,1)S(1)} %copy-done.1, f32[512,16]{1,0:T(8,128)S(1)} %get-tuple-element.77.rate_ref, f32[512,256]{1,0:T(8,128)S(1)} %bitcast.6, ...), custom_call_target="tpu_custom_call" | custom-call | flops 2097152000 | bytes 3145728 | tf_op jit(solution)/shard_map/pallas_call | solution.py:338
  17.2 0.6 collective-permute-done.3
  17.8 1.5 %collective-permute-start.4 = (bf16[80,256]{1,0:T(8,128)(2,1)S(1)}, bf16[80,256]{1,0:T(8,128)(2,1)S(1)}, u32[]{:S(2)}, u32[]{:S(2)}) collective-permute-start(bf16[80,256]{1,0:T(8,128)(2,1)S(1)} %constant_dynamic-update-slice_fusion), channel_id=1, source_target_pairs={{0,8},{1,9},{2,10},{3,11},{4,12},{5,13},{6,14},{7,15},{8,0},{9,1},... | collective-permute-start | bytes 122888 | tf_op jit(solution)/shard_map/ppermute | solution.py:603
  19.3 1.3 %shard_map.80 = (bf16[4,16,32,256]{3,2,1,0:T(8,128)(2,1)S(1)}, f32[4,512,128]{2,1,0:T(8,128)S(1)}, f32[512,256]{1,0:T(8,128)S(1)}) custom-call(bf16[16,16,32,256]{3,2,1,0:T(8,128)(2,1)S(1)} %copy-done, bf16[16,16,32,256]{3,2,1,0:T(8,128)(2,1)S(1)} %copy-done.1, f32[512,16]{1,0:T(8,128)S(1)} %get-tuple-element.77.rate_ref, ...), custom_call_target="tpu_custom_call" | custom-call | flops 2097152000 | bytes 3145728 | tf_op jit(solution)/shard_map/pallas_call | solution.py:338
  20.7 1.1 %collective-permute-done.4 = bf16[80,256]{1,0:T(8,128)(2,1)S(1)} collective-permute-done((bf16[80,256]{1,0:T(8,128)(2,1)S(1)}, bf16[80,256]{1,0:T(8,128)(2,1)S(1)}, u32[]{:S(2)}, u32[]{:S(2)}) %collective-permute-start.4) | collective-permute-done | bytes 40992 | tf_op jit(solution)/shard_map/ppermute | solution.py:603
  21.8 3.3 %collective-permute-start.5 = (bf16[160,256]{1,0:T(8,128)(2,1)S(1)}, bf16[160,256]{1,0:T(8,128)(2,1)S(1)}, u32[]{:S(2)}, u32[]{:S(2)}) collective-permute-start(bf16[160,256]{1,0:T(8,128)(2,1)S(1)} %constant_dynamic-update-slice_fusion.2), channel_id=1, source_target_pairs={{0,1},{1,0},{2,3},{3,2},{4,5},{5,4},{6,7},{7,6},{8,9},{9,8},{10,11... | collective-permute-start | bytes 245768 | tf_op jit(solution)/shard_map/ppermute | solution.py:603
  25.2 1.3 %shard_map.81 = (bf16[4,16,32,256]{3,2,1,0:T(8,128)(2,1)S(1)}, f32[4,512,128]{2,1,0:T(8,128)S(1)}, f32[512,256]{1,0:T(8,128)S(1)}) custom-call(bf16[16,16,32,256]{3,2,1,0:T(8,128)(2,1)S(1)} %copy-done, bf16[16,16,32,256]{3,2,1,0:T(8,128)(2,1)S(1)} %copy-done.1, f32[512,16]{1,0:T(8,128)S(1)} %get-tuple-element.77.rate_ref, ...), custom_call_target="tpu_custom_call" | custom-call | flops 2097152000 | bytes 3145728 | tf_op jit(solution)/shard_map/pallas_call | solution.py:338
  26.5 1.1 %collective-permute-done.5 = bf16[160,256]{1,0:T(8,128)(2,1)S(1)} collective-permute-done((bf16[160,256]{1,0:T(8,128)(2,1)S(1)}, bf16[160,256]{1,0:T(8,128)(2,1)S(1)}, u32[]{:S(2)}, u32[]{:S(2)}) %collective-permute-start.5) | collective-permute-done | bytes 81952 | tf_op jit(solution)/shard_map/ppermute | solution.py:603
  27.6 1.5 %collective-permute-start.6 = (bf16[320,256]{1,0:T(8,128)(2,1)S(1)}, bf16[320,256]{1,0:T(8,128)(2,1)S(1)}, u32[]{:S(2)}, u32[]{:S(2)}) collective-permute-start(bf16[320,256]{1,0:T(8,128)(2,1)S(1)} %constant_dynamic-update-slice_fusion.4), channel_id=1, source_target_pairs={{0,4},{1,5},{2,6},{3,7},{4,0},{5,1},{6,2},{7,3},{8,12},{9,13},{10,... | collective-permute-start | bytes 491528 | tf_op jit(solution)/shard_map/ppermute | solution.py:603
  29.2 0.0 copy-start.3
  29.2 2.0 %shard_map.82 = (bf16[4,16,32,256]{3,2,1,0:T(8,128)(2,1)S(1)}, f32[4,512,128]{2,1,0:T(8,128)S(1)}, f32[512,256]{1,0:T(8,128)}) custom-call(bf16[16,16,32,256]{3,2,1,0:T(8,128)(2,1)S(1)} %copy-done, bf16[16,16,32,256]{3,2,1,0:T(8,128)(2,1)S(1)} %copy-done.1, f32[512,16]{1,0:T(8,128)S(1)} %get-tuple-element.77.rate_ref, ...), custom_call_target="tpu_custom_call" | custom-call | flops 2097152000 | bytes 3145728 | tf_op jit(solution)/shard_map/pallas_call | solution.py:338
  31.2 1.8 %collective-permute-done.6 = bf16[320,256]{1,0:T(8,128)(2,1)S(1)} collective-permute-done((bf16[320,256]{1,0:T(8,128)(2,1)S(1)}, bf16[320,256]{1,0:T(8,128)(2,1)S(1)}, u32[]{:S(2)}, u32[]{:S(2)}) %collective-permute-start.6) | collective-permute-done | bytes 163872 | tf_op jit(solution)/shard_map/ppermute | solution.py:603
  33.0 0.1 collective-permute-start.7
  33.1 0.0 copy-done.3
  33.1 0.6 shard_map.83
  33.7 1.0 %collective-permute-done.7.rows_ref = bf16[640,256]{1,0:T(8,128)(2,1)S(1)} collective-permute-done((bf16[640,256]{1,0:T(8,128)(2,1)S(1)}, bf16[640,256]{1,0:T(8,128)(2,1)S(1)}, u32[]{:S(2)}, u32[]{:S(2)}) %collective-permute-start.7) | collective-permute-done | bytes 327712 | tf_op jit(solution)/shard_map/ppermute | solution.py:615
  34.7 42.8 %shard_map.84 = bf16[16,16,32,256]{3,2,1,0:T(8,128)(2,1)} custom-call(bf16[640,256]{1,0:T(8,128)(2,1)S(1)} %collective-permute-done.7.rows_ref, f32[256,256]{1,0:T(8,128)S(1)} %get-tuple-element.105.gram_ref, f32[16,256]{1,0:T(8,128)S(1)} %get-tuple-element.106.pieces_ref, bf16[256,256]{1,0:T(8,128)(2,1)S(1)} %get-tuple-element.107.select_ref, ...), custom_call_target="tpu_custom_call" | custom-call | flops 8388608000 | bytes 10485760 | tf_op jit(solution)/shard_map/pallas_call | solution.py:513
  (8 shorter events, 0.1 us)
Async XLA Ops:
  0.0 4.9 %copy-start = (bf16[16,16,32,256]{3,2,1,0:T(8,128)(2,1)S(1)}, bf16[16,16,32,256]{3,2,1,0:T(8,128)(2,1)}, u32[]{:S(2)}) copy-start(bf16[16,16,32,256]{3,2,1,0:T(8,128)(2,1)} %source_ref.13) | copy-start | bytes 12582916
  0.0 6.0 %copy-start.1 = (bf16[16,16,32,256]{3,2,1,0:T(8,128)(2,1)S(1)}, bf16[16,16,32,256]{3,2,1,0:T(8,128)(2,1)}, u32[]{:S(2)}) copy-start(bf16[16,16,32,256]{3,2,1,0:T(8,128)(2,1)} %inflow_ref.4) | copy-start | bytes 12582916
  0.0 6.0 %copy-start.2 = (f32[16,16,32]{2,1,0:T(8,128)S(1)}, f32[16,16,32]{2,1,0:T(8,128)}, u32[]{:S(2)}) copy-start(f32[16,16,32]{2,1,0:T(8,128)} %recovery_ref.1) | copy-start | bytes 98308
  0.0 6.0 %copy-start.6 = (s32[32]{0:T(128)S(1)}, s32[32]{0:T(128)}, u32[]{:S(2)}) copy-start(s32[32]{0:T(128)} %rows_ref.5) | copy-start | bytes 388
  1.8 6.6 %collective-permute-start = (bf16[16,16,256]{2,1,0:T(8,128)(2,1)S(1)}, bf16[16,16,256]{2,1,0:T(8,128)(2,1)S(1)}, u32[]{:S(2)}, u32[]{:S(2)}) collective-permute-start(bf16[16,16,256]{2,1,0:T(8,128)(2,1)S(1)} %shard_map.73), channel_id=1, source_target_pairs={{0,1},{2,3},{1,0},{3,2},{4,5},{6,7},{5,4},{7,6},{8,9},{10,11},{9,8... | collective-permute-start | bytes 393224 | tf_op jit(solution)/shard_map/ppermute | solution.py:589
  5.3 3.1 %collective-permute-start.1 = (bf16[16,16,256]{2,1,0:T(8,128)(2,1)S(1)}, bf16[16,16,256]{2,1,0:T(8,128)(2,1)S(1)}, u32[]{:S(2)}, u32[]{:S(2)}) collective-permute-start(bf16[16,16,256]{2,1,0:T(8,128)(2,1)S(1)} %shard_map.75), channel_id=1, source_target_pairs={{1,2},{2,1},{5,6},{6,5},{9,10},{10,9},{13,14},{14,13},{17,18},{18,... | collective-permute-start | bytes 393224 | tf_op jit(solution)/shard_map/ppermute | solution.py:590
  6.0 4.1 %copy-start.4 = (f32[32]{0:T(128)S(1)}, f32[32]{0:T(128)}, u32[]{:S(2)}) copy-start(f32[32]{0:T(128)} %param.11) | copy-start | bytes 388
  6.0 4.1 %copy-start.5 = (f32[32]{0:T(128)S(1)}, f32[32]{0:T(128)}, u32[]{:S(2)}) copy-start(f32[32]{0:T(128)} %param.12) | copy-start | bytes 388
  8.6 3.0 %collective-permute-start.2 = (f32[16,32,256]{2,1,0:T(8,128)S(1)}, f32[16,32,256]{2,1,0:T(8,128)S(1)}, u32[]{:S(2)}, u32[]{:S(2)}) collective-permute-start(f32[16,32,256]{2,1,0:T(8,128)S(1)} %get-tuple-element.76), channel_id=1, source_target_pairs={{0,16},{1,17},{2,18},{3,19},{4,20},{5,21},{6,22},{7,23},{8,24},{9,... | collective-permute-start | bytes 1572872 | tf_op jit(solution)/shard_map/ppermute | solution.py:538
  12.2 5.6 %collective-permute-start.3 = (bf16[40,256]{1,0:T(8,128)(2,1)S(1)}, bf16[40,256]{1,0:T(8,128)(2,1)S(1)}, u32[]{:S(2)}, u32[]{:S(2)}) collective-permute-start(bf16[40,256]{1,0:T(8,128)(2,1)S(1)} %shard_map.78), channel_id=1, source_target_pairs={{0,3},{1,2},{2,1},{3,0},{4,7},{5,6},{6,5},{7,4},{8,11},{9,10},{10,... | collective-permute-start | bytes 61448 | tf_op jit(solution)/shard_map/ppermute | solution.py:603
  17.8 4.0 %collective-permute-start.4 = (bf16[80,256]{1,0:T(8,128)(2,1)S(1)}, bf16[80,256]{1,0:T(8,128)(2,1)S(1)}, u32[]{:S(2)}, u32[]{:S(2)}) collective-permute-start(bf16[80,256]{1,0:T(8,128)(2,1)S(1)} %constant_dynamic-update-slice_fusion), channel_id=1, source_target_pairs={{0,8},{1,9},{2,10},{3,11},{4,12},{5,13},{6,14},{7,15},{8,0},{9,1},... | collective-permute-start | bytes 122888 | tf_op jit(solution)/shard_map/ppermute | solution.py:603
  21.8 5.8 %collective-permute-start.5 = (bf16[160,256]{1,0:T(8,128)(2,1)S(1)}, bf16[160,256]{1,0:T(8,128)(2,1)S(1)}, u32[]{:S(2)}, u32[]{:S(2)}) collective-permute-start(bf16[160,256]{1,0:T(8,128)(2,1)S(1)} %constant_dynamic-update-slice_fusion.2), channel_id=1, source_target_pairs={{0,1},{1,0},{2,3},{3,2},{4,5},{5,4},{6,7},{7,6},{8,9},{9,8},{10,11... | collective-permute-start | bytes 245768 | tf_op jit(solution)/shard_map/ppermute | solution.py:603
  27.6 5.3 %collective-permute-start.6 = (bf16[320,256]{1,0:T(8,128)(2,1)S(1)}, bf16[320,256]{1,0:T(8,128)(2,1)S(1)}, u32[]{:S(2)}, u32[]{:S(2)}) collective-permute-start(bf16[320,256]{1,0:T(8,128)(2,1)S(1)} %constant_dynamic-update-slice_fusion.4), channel_id=1, source_target_pairs={{0,4},{1,5},{2,6},{3,7},{4,0},{5,1},{6,2},{7,3},{8,12},{9,13},{10,... | collective-permute-start | bytes 491528 | tf_op jit(solution)/shard_map/ppermute | solution.py:603
  29.2 3.9 %copy-start.3 = (s32[256]{0:T(256)S(1)}, s32[256]{0:T(256)}, u32[]{:S(2)}) copy-start(s32[256]{0:T(256)} %param.13) | copy-start | bytes 3076
  33.0 1.7 %collective-permute-start.7 = (bf16[640,256]{1,0:T(8,128)(2,1)S(1)}, bf16[640,256]{1,0:T(8,128)(2,1)S(1)}, u32[]{:S(2)}, u32[]{:S(2)}) collective-permute-start(bf16[640,256]{1,0:T(8,128)(2,1)S(1)} %constant_dynamic-update-slice_fusion.6.rows_ref), channel_id=1, source_target_pairs={{0,16},{1,17},{2,18},{3,19},{4,20},{5,21},{6,22},{7,23},{8,24},{9,... | collective-permute-start | bytes 983048 | tf_op jit(solution)/shard_map/ppermute | solution.py:615

commit v9 on v8

--- a/solution.py
+++ b/solution.py
@@ -274,8 +274,14 @@
     )(obs_rows, edge, picks, obs[None, :], weight[None, :])
 
 
+def exact_pick(chosen, table):
+    big = table.astype(jnp.bfloat16)
+    middle, small = halves(table - big.astype(jnp.float32))
+    return dot(chosen, big) + (dot(chosen, middle) + dot(chosen, small))
+
+
 def observe_kernel(
-    place_ref, rows_ref, obs_ref, weight_ref, picks_ref, share_ref, first_ref, incoming_ref, out_ref, arriving
+    place_ref, rows_ref, obs_ref, weight_ref, picks_ref, share_ref, first_ref, incoming_ref, out_ref
 ):
     @pl.when(place_ref[0] < 2)
     def _():
@@ -283,10 +289,14 @@
 
     @pl.when(place_ref[0] >= 2)
     def _():
-        for k in range(picks_ref.shape[0]):
-            _, a, b = place_of(rows_ref[k], (0,) + incoming_ref.shape[:2])
-            arriving[pl.ds(k, 1), :] = incoming_ref[a, pl.ds(b, 1), :]
-        forecast = picks_ref[...] - share_ref[...] * arriving[...]
+        span, height, members = incoming_ref.shape
+        cells = span * height
+        row = upright(rows_ref[...].astype(jnp.float32)).astype(jnp.int32)
+        _, cell = parted(row, cells)
+        lane = lax.broadcasted_iota(jnp.int32, (row.shape[0], cells), 1)
+        chosen = jnp.where(lane == cell, 1.0, 0.0).astype(jnp.bfloat16)
+        arriving = exact_pick(chosen, incoming_ref[...].reshape(cells, members))
+        forecast = picks_ref[...] - share_ref[...] * arriving
         out_ref[...] = payload(forecast, obs_ref[...], weight_ref[...])
 
 
@@ -295,13 +305,12 @@
     vmem, smem = pl.BlockSpec(memory_space=pltpu.VMEM), pl.BlockSpec(memory_space=pltpu.SMEM)
     return pl.pallas_call(
         observe_kernel,
-        in_specs=[smem, smem] + [vmem] * 6,
+        in_specs=[smem] + [vmem] * 7,
         out_specs=vmem,
         out_shape=jax.ShapeDtypeStruct((count + EXTRA, members), jnp.bfloat16),
-        scratch_shapes=[pltpu.VMEM((count, members), jnp.float32)],
         compiler_params=params(LIMIT),
         cost_estimate=cost(40 * count * members, 64 * count * members),
-    )(place, obs_rows, obs, weight, picks, share, first, incoming)
+    )(place, obs_rows[None, :], obs, weight, picks, share, first, incoming)
 
 
 def anomaly_kernel(start, planes, source_ref, inflow_ref, rate_ref, state_ref, term_ref, *refs):

time: 77.6 us -> 77.2 us (level)
  no operation moved by 1% of the time
where the time goes in v9:
time: 77.2 us; the launch traced here: 77.1 us
  Pallas kernels  55 us (71%)
  starting transfers between devices  15.6 us (20%)
  waiting for transfers between devices  6.25 us (8%)
    pallas_call x1, Pallas kernels, updated(): pl.pallas_call(functools.partial(update_kernel, picked), in_specs=[vmem]...  42.8 us
    ppermute x4, starting transfers between devices, shards(): other = lax.ppermute(rows, AXES, pairing)  10.2 us
    pallas_call x4, Pallas kernels, anomalies(): pl.pallas_call(functools.partial(anomaly_kernel, start, planes), in_specs...  6.01 us
    ppermute x4, waiting for transfers between devices, shards(): other = lax.ppermute(rows, AXES, pairing)  4.61 us
    ppermute x1, starting transfers between devices, shards(): first = lax.ppermute(first, 'height', pairs(levels, 0))  3.1 us
    pallas_call x1, Pallas kernels, march(): pl.pallas_call(march_kernel, in_specs=[pl.BlockSpec(memory_space=pltpu.SM...  2.34 us
    pallas_call x2, Pallas kernels, border(): pl.pallas_call(first_border_kernel if far else second_border_kernel, in_s...  2.19 us
  transfers between devices with their start and end apart: 8, of which 6 were waited for; matrix products, arithmetic and copies ran while one was open for 0% of the time, Pallas kernels for 13%

profile of v9, /device:TPU:0, one launch (start us, length us, event | category | flops | bytes accessed | tf_op | source)
XLA Modules:
  0.0 77.1 jit_solution(8077251109215138194)
XLA Ops:
  0.0 0.0 copy-start
  0.0 0.0 copy-start.1
  0.0 0.0 copy-start.2
  0.0 0.0 copy-start.6
  0.0 1.8 %shard_map.73 = bf16[16,16,256]{2,1,0:T(8,128)(2,1)S(1)} custom-call(s32[1]{0:T(128)} %bitcast.place_ref, bf16[16,16,32,256]{3,2,1,0:T(8,128)(2,1)} %source_ref.13), custom_call_target="tpu_custom_call" | custom-call | flops 1048576000 | bytes 2097152 | tf_op jit(solution)/shard_map/pallas_call | solution.py:74
  1.8 3.1 %collective-permute-start = (bf16[16,16,256]{2,1,0:T(8,128)(2,1)S(1)}, bf16[16,16,256]{2,1,0:T(8,128)(2,1)S(1)}, u32[]{:S(2)}, u32[]{:S(2)}) collective-permute-start(bf16[16,16,256]{2,1,0:T(8,128)(2,1)S(1)} %shard_map.73), channel_id=1, source_target_pairs={{0,1},{2,3},{1,0},{3,2},{4,5},{6,7},{5,4},{7,6},{8,9},{10,11},{9,8... | collective-permute-start | bytes 393224 | tf_op jit(solution)/shard_map/ppermute | solution.py:598
  4.9 0.0 copy-done
  4.9 0.4 shard_map.75
  5.3 0.7 collective-permute-start.1
  6.0 0.0 copy-done.1
  6.0 0.0 copy-done.2
  6.0 0.0 copy-done.6
  6.0 0.0 copy-start.4
  6.0 0.0 copy-start.5
  6.0 2.3 %shard_map.74 = (f32[512,256]{1,0:T(8,128)S(1)}, f32[32,256]{1,0:T(8,128)S(1)}, f32[32,256]{1,0:T(8,128)S(1)}, f32[512,16]{1,0:T(8,128)S(1)}, f32[16,16]{1,0:T(8,128)S(1)}, /*index=5*/f32[16,16]{1,0:T(8,128)S(1)}) custom-call(s32[32]{0:T(128)S(1)} %copy-done.6, s32[1,32]{1,0:T(1,128)S(1)} %bitcast.10, bf16[16,16,32,256]{3,2,1,0:T(8,128)(2,1)S(1)} %copy-done, ...), custom_call_target="tpu_custom_call" | custom-call | flops 6291456000 | bytes 8388608 | tf_op jit(solution)/shard_map/pallas_call | solution.py:169
  8.4 0.0 collective-permute-done.first_ref
  8.4 0.0 collective-permute-done.1.second_ref
  8.4 0.2 shard_map.76
  8.6 1.5 %collective-permute-start.2 = (f32[16,32,256]{2,1,0:T(8,128)S(1)}, f32[16,32,256]{2,1,0:T(8,128)S(1)}, u32[]{:S(2)}, u32[]{:S(2)}) collective-permute-start(f32[16,32,256]{2,1,0:T(8,128)S(1)} %get-tuple-element.76), channel_id=1, source_target_pairs={{0,16},{1,17},{2,18},{3,19},{4,20},{5,21},{6,22},{7,23},{8,24},{9,... | collective-permute-start | bytes 1572872 | tf_op jit(solution)/shard_map/ppermute | solution.py:547
  10.1 0.0 copy-done.4
  10.1 0.0 copy-done.5
  10.1 0.8 %shard_map.77 = (f32[32,256]{1,0:T(8,128)S(1)}, f32[32,256]{1,0:T(8,128)S(1)}, f32[32,256]{1,0:T(8,128)S(1)}, bf16[40,256]{1,0:T(8,128)(2,1)S(1)}) custom-call(s32[32]{0:T(128)S(1)} %copy-done.6, f32[2,16,16,256]{3,2,1,0:T(8,128)S(1)} %get-tuple-element.69.edge_ref, f32[32,256]{1,0:T(8,128)S(1)} %get-tuple-element.70.picks_ref, f32[1,32]{1,0:T(1,128)S(1)} %bitcast.8, ...), custom_call_target="tpu_custom_call" | custom-call | flops 819200000 | bytes 524288 | tf_op jit(solution)/shard_map/pallas_call | solution.py:267
  11.0 0.6 collective-permute-done.2.incoming_ref
  11.6 3.6 %collective-permute-start.3 = (bf16[40,256]{1,0:T(8,128)(2,1)S(1)}, bf16[40,256]{1,0:T(8,128)(2,1)S(1)}, u32[]{:S(2)}, u32[]{:S(2)}) collective-permute-start(bf16[40,256]{1,0:T(8,128)(2,1)S(1)} %shard_map.78), channel_id=1, source_target_pairs={{0,3},{1,2},{2,1},{3,0},{4,7},{5,6},{6,5},{7,4},{8,11},{9,10},{10,... | collective-permute-start | bytes 61448 | tf_op jit(solution)/shard_map/ppermute | solution.py:612
  15.2 1.3 %shard_map.79 = (bf16[4,16,32,256]{3,2,1,0:T(8,128)(2,1)S(1)}, f32[4,512,128]{2,1,0:T(8,128)S(1)}, f32[512,256]{1,0:T(8,128)S(1)}) custom-call(bf16[16,16,32,256]{3,2,1,0:T(8,128)(2,1)S(1)} %copy-done, bf16[16,16,32,256]{3,2,1,0:T(8,128)(2,1)S(1)} %copy-done.1, f32[512,16]{1,0:T(8,128)S(1)} %get-tuple-element.77.rate_ref, f32[512,256]{1,0:T(8,128)S(1)} %bitcast.6, ...), custom_call_target="tpu_custom_call" | custom-call | flops 2097152000 | bytes 3145728 | tf_op jit(solution)/shard_map/pallas_call | solution.py:347
  16.6 0.6 collective-permute-done.3
  17.2 1.5 %collective-permute-start.4 = (bf16[80,256]{1,0:T(8,128)(2,1)S(1)}, bf16[80,256]{1,0:T(8,128)(2,1)S(1)}, u32[]{:S(2)}, u32[]{:S(2)}) collective-permute-start(bf16[80,256]{1,0:T(8,128)(2,1)S(1)} %constant_dynamic-update-slice_fusion), channel_id=1, source_target_pairs={{0,8},{1,9},{2,10},{3,11},{4,12},{5,13},{6,14},{7,15},{8,0},{9,1},... | collective-permute-start | bytes 122888 | tf_op jit(solution)/shard_map/ppermute | solution.py:612
  18.7 1.3 %shard_map.80 = (bf16[4,16,32,256]{3,2,1,0:T(8,128)(2,1)S(1)}, f32[4,512,128]{2,1,0:T(8,128)S(1)}, f32[512,256]{1,0:T(8,128)S(1)}) custom-call(bf16[16,16,32,256]{3,2,1,0:T(8,128)(2,1)S(1)} %copy-done, bf16[16,16,32,256]{3,2,1,0:T(8,128)(2,1)S(1)} %copy-done.1, f32[512,16]{1,0:T(8,128)S(1)} %get-tuple-element.77.rate_ref, ...), custom_call_target="tpu_custom_call" | custom-call | flops 2097152000 | bytes 3145728 | tf_op jit(solution)/shard_map/pallas_call | solution.py:347
  20.1 1.1 %collective-permute-done.4 = bf16[80,256]{1,0:T(8,128)(2,1)S(1)} collective-permute-done((bf16[80,256]{1,0:T(8,128)(2,1)S(1)}, bf16[80,256]{1,0:T(8,128)(2,1)S(1)}, u32[]{:S(2)}, u32[]{:S(2)}) %collective-permute-start.4) | collective-permute-done | bytes 40992 | tf_op jit(solution)/shard_map/ppermute | solution.py:612
  21.2 3.6 %collective-permute-start.5 = (bf16[160,256]{1,0:T(8,128)(2,1)S(1)}, bf16[160,256]{1,0:T(8,128)(2,1)S(1)}, u32[]{:S(2)}, u32[]{:S(2)}) collective-permute-start(bf16[160,256]{1,0:T(8,128)(2,1)S(1)} %constant_dynamic-update-slice_fusion.2), channel_id=1, source_target_pairs={{0,1},{1,0},{2,3},{3,2},{4,5},{5,4},{6,7},{7,6},{8,9},{9,8},{10,11... | collective-permute-start | bytes 245768 | tf_op jit(solution)/shard_map/ppermute | solution.py:612
  24.8 1.3 %shard_map.81 = (bf16[4,16,32,256]{3,2,1,0:T(8,128)(2,1)S(1)}, f32[4,512,128]{2,1,0:T(8,128)S(1)}, f32[512,256]{1,0:T(8,128)S(1)}) custom-call(bf16[16,16,32,256]{3,2,1,0:T(8,128)(2,1)S(1)} %copy-done, bf16[16,16,32,256]{3,2,1,0:T(8,128)(2,1)S(1)} %copy-done.1, f32[512,16]{1,0:T(8,128)S(1)} %get-tuple-element.77.rate_ref, ...), custom_call_target="tpu_custom_call" | custom-call | flops 2097152000 | bytes 3145728 | tf_op jit(solution)/shard_map/pallas_call | solution.py:347
  26.1 1.1 %collective-permute-done.5 = bf16[160,256]{1,0:T(8,128)(2,1)S(1)} collective-permute-done((bf16[160,256]{1,0:T(8,128)(2,1)S(1)}, bf16[160,256]{1,0:T(8,128)(2,1)S(1)}, u32[]{:S(2)}, u32[]{:S(2)}) %collective-permute-start.5) | collective-permute-done | bytes 81952 | tf_op jit(solution)/shard_map/ppermute | solution.py:612
  27.2 1.5 %collective-permute-start.6 = (bf16[320,256]{1,0:T(8,128)(2,1)S(1)}, bf16[320,256]{1,0:T(8,128)(2,1)S(1)}, u32[]{:S(2)}, u32[]{:S(2)}) collective-permute-start(bf16[320,256]{1,0:T(8,128)(2,1)S(1)} %constant_dynamic-update-slice_fusion.4), channel_id=1, source_target_pairs={{0,4},{1,5},{2,6},{3,7},{4,0},{5,1},{6,2},{7,3},{8,12},{9,13},{10,... | collective-permute-start | bytes 491528 | tf_op jit(solution)/shard_map/ppermute | solution.py:612
  28.7 0.0 copy-start.3
  28.7 2.0 %shard_map.82 = (bf16[4,16,32,256]{3,2,1,0:T(8,128)(2,1)S(1)}, f32[4,512,128]{2,1,0:T(8,128)S(1)}, f32[512,256]{1,0:T(8,128)}) custom-call(bf16[16,16,32,256]{3,2,1,0:T(8,128)(2,1)S(1)} %copy-done, bf16[16,16,32,256]{3,2,1,0:T(8,128)(2,1)S(1)} %copy-done.1, f32[512,16]{1,0:T(8,128)S(1)} %get-tuple-element.77.rate_ref, ...), custom_call_target="tpu_custom_call" | custom-call | flops 2097152000 | bytes 3145728 | tf_op jit(solution)/shard_map/pallas_call | solution.py:347
  30.8 1.8 %collective-permute-done.6 = bf16[320,256]{1,0:T(8,128)(2,1)S(1)} collective-permute-done((bf16[320,256]{1,0:T(8,128)(2,1)S(1)}, bf16[320,256]{1,0:T(8,128)(2,1)S(1)}, u32[]{:S(2)}, u32[]{:S(2)}) %collective-permute-start.6) | collective-permute-done | bytes 163872 | tf_op jit(solution)/shard_map/ppermute | solution.py:612
  32.6 0.1 collective-permute-start.7
  32.6 0.0 copy-done.3
  32.7 0.6 shard_map.83
  33.3 1.0 %collective-permute-done.7.rows_ref = bf16[640,256]{1,0:T(8,128)(2,1)S(1)} collective-permute-done((bf16[640,256]{1,0:T(8,128)(2,1)S(1)}, bf16[640,256]{1,0:T(8,128)(2,1)S(1)}, u32[]{:S(2)}, u32[]{:S(2)}) %collective-permute-start.7) | collective-permute-done | bytes 327712 | tf_op jit(solution)/shard_map/ppermute | solution.py:624
  34.3 42.8 %shard_map.84 = bf16[16,16,32,256]{3,2,1,0:T(8,128)(2,1)} custom-call(bf16[640,256]{1,0:T(8,128)(2,1)S(1)} %collective-permute-done.7.rows_ref, f32[256,256]{1,0:T(8,128)S(1)} %get-tuple-element.105.gram_ref, f32[16,256]{1,0:T(8,128)S(1)} %get-tuple-element.106.pieces_ref, bf16[256,256]{1,0:T(8,128)(2,1)S(1)} %get-tuple-element.107.select_ref, ...), custom_call_target="tpu_custom_call" | custom-call | flops 8388608000 | bytes 10485760 | tf_op jit(solution)/shard_map/pallas_call | solution.py:522
  (9 shorter events, 0.1 us)
Async XLA Ops:
  0.0 4.9 %copy-start = (bf16[16,16,32,256]{3,2,1,0:T(8,128)(2,1)S(1)}, bf16[16,16,32,256]{3,2,1,0:T(8,128)(2,1)}, u32[]{:S(2)}) copy-start(bf16[16,16,32,256]{3,2,1,0:T(8,128)(2,1)} %source_ref.13) | copy-start | bytes 12582916
  0.0 6.0 %copy-start.1 = (bf16[16,16,32,256]{3,2,1,0:T(8,128)(2,1)S(1)}, bf16[16,16,32,256]{3,2,1,0:T(8,128)(2,1)}, u32[]{:S(2)}) copy-start(bf16[16,16,32,256]{3,2,1,0:T(8,128)(2,1)} %inflow_ref.4) | copy-start | bytes 12582916
  0.0 6.0 %copy-start.2 = (f32[16,16,32]{2,1,0:T(8,128)S(1)}, f32[16,16,32]{2,1,0:T(8,128)}, u32[]{:S(2)}) copy-start(f32[16,16,32]{2,1,0:T(8,128)} %recovery_ref.1) | copy-start | bytes 98308
  0.0 6.0 %copy-start.6 = (s32[32]{0:T(128)S(1)}, s32[32]{0:T(128)}, u32[]{:S(2)}) copy-start(s32[32]{0:T(128)} %rows_ref.3) | copy-start | bytes 388
  1.8 6.6 %collective-permute-start = (bf16[16,16,256]{2,1,0:T(8,128)(2,1)S(1)}, bf16[16,16,256]{2,1,0:T(8,128)(2,1)S(1)}, u32[]{:S(2)}, u32[]{:S(2)}) collective-permute-start(bf16[16,16,256]{2,1,0:T(8,128)(2,1)S(1)} %shard_map.73), channel_id=1, source_target_pairs={{0,1},{2,3},{1,0},{3,2},{4,5},{6,7},{5,4},{7,6},{8,9},{10,11},{9,8... | collective-permute-start | bytes 393224 | tf_op jit(solution)/shard_map/ppermute | solution.py:598
  5.3 3.1 %collective-permute-start.1 = (bf16[16,16,256]{2,1,0:T(8,128)(2,1)S(1)}, bf16[16,16,256]{2,1,0:T(8,128)(2,1)S(1)}, u32[]{:S(2)}, u32[]{:S(2)}) collective-permute-start(bf16[16,16,256]{2,1,0:T(8,128)(2,1)S(1)} %shard_map.75), channel_id=1, source_target_pairs={{1,2},{2,1},{5,6},{6,5},{9,10},{10,9},{13,14},{14,13},{17,18},{18,... | collective-permute-start | bytes 393224 | tf_op jit(solution)/shard_map/ppermute | solution.py:599
  6.0 4.1 %copy-start.4 = (f32[32]{0:T(128)S(1)}, f32[32]{0:T(128)}, u32[]{:S(2)}) copy-start(f32[32]{0:T(128)} %param.11) | copy-start | bytes 388
  6.0 4.1 %copy-start.5 = (f32[32]{0:T(128)S(1)}, f32[32]{0:T(128)}, u32[]{:S(2)}) copy-start(f32[32]{0:T(128)} %param.12) | copy-start | bytes 388
  8.6 3.0 %collective-permute-start.2 = (f32[16,32,256]{2,1,0:T(8,128)S(1)}, f32[16,32,256]{2,1,0:T(8,128)S(1)}, u32[]{:S(2)}, u32[]{:S(2)}) collective-permute-start(f32[16,32,256]{2,1,0:T(8,128)S(1)} %get-tuple-element.76), channel_id=1, source_target_pairs={{0,16},{1,17},{2,18},{3,19},{4,20},{5,21},{6,22},{7,23},{8,24},{9,... | collective-permute-start | bytes 1572872 | tf_op jit(solution)/shard_map/ppermute | solution.py:547
  11.6 5.6 %collective-permute-start.3 = (bf16[40,256]{1,0:T(8,128)(2,1)S(1)}, bf16[40,256]{1,0:T(8,128)(2,1)S(1)}, u32[]{:S(2)}, u32[]{:S(2)}) collective-permute-start(bf16[40,256]{1,0:T(8,128)(2,1)S(1)} %shard_map.78), channel_id=1, source_target_pairs={{0,3},{1,2},{2,1},{3,0},{4,7},{5,6},{6,5},{7,4},{8,11},{9,10},{10,... | collective-permute-start | bytes 61448 | tf_op jit(solution)/shard_map/ppermute | solution.py:612
  17.2 4.0 %collective-permute-start.4 = (bf16[80,256]{1,0:T(8,128)(2,1)S(1)}, bf16[80,256]{1,0:T(8,128)(2,1)S(1)}, u32[]{:S(2)}, u32[]{:S(2)}) collective-permute-start(bf16[80,256]{1,0:T(8,128)(2,1)S(1)} %constant_dynamic-update-slice_fusion), channel_id=1, source_target_pairs={{0,8},{1,9},{2,10},{3,11},{4,12},{5,13},{6,14},{7,15},{8,0},{9,1},... | collective-permute-start | bytes 122888 | tf_op jit(solution)/shard_map/ppermute | solution.py:612
  21.2 6.0 %collective-permute-start.5 = (bf16[160,256]{1,0:T(8,128)(2,1)S(1)}, bf16[160,256]{1,0:T(8,128)(2,1)S(1)}, u32[]{:S(2)}, u32[]{:S(2)}) collective-permute-start(bf16[160,256]{1,0:T(8,128)(2,1)S(1)} %constant_dynamic-update-slice_fusion.2), channel_id=1, source_target_pairs={{0,1},{1,0},{2,3},{3,2},{4,5},{5,4},{6,7},{7,6},{8,9},{9,8},{10,11... | collective-permute-start | bytes 245768 | tf_op jit(solution)/shard_map/ppermute | solution.py:612
  27.2 5.3 %collective-permute-start.6 = (bf16[320,256]{1,0:T(8,128)(2,1)S(1)}, bf16[320,256]{1,0:T(8,128)(2,1)S(1)}, u32[]{:S(2)}, u32[]{:S(2)}) collective-permute-start(bf16[320,256]{1,0:T(8,128)(2,1)S(1)} %constant_dynamic-update-slice_fusion.4), channel_id=1, source_target_pairs={{0,4},{1,5},{2,6},{3,7},{4,0},{5,1},{6,2},{7,3},{8,12},{9,13},{10,... | collective-permute-start | bytes 491528 | tf_op jit(solution)/shard_map/ppermute | solution.py:612
  28.7 3.9 %copy-start.3 = (s32[256]{0:T(256)S(1)}, s32[256]{0:T(256)}, u32[]{:S(2)}) copy-start(s32[256]{0:T(256)} %param.13) | copy-start | bytes 3076
  32.6 1.7 %collective-permute-start.7 = (bf16[640,256]{1,0:T(8,128)(2,1)S(1)}, bf16[640,256]{1,0:T(8,128)(2,1)S(1)}, u32[]{:S(2)}, u32[]{:S(2)}) collective-permute-start(bf16[640,256]{1,0:T(8,128)(2,1)S(1)} %constant_dynamic-update-slice_fusion.6.rows_ref), channel_id=1, source_target_pairs={{0,16},{1,17},{2,18},{3,19},{4,20},{5,21},{6,22},{7,23},{8,24},{9,... | collective-permute-start | bytes 983048 | tf_op jit(solution)/shard_map/ppermute | solution.py:624
